TPU v7x, 32 devices: a whole 2x2x4 slice. The times are simulated.
32 devices in a mesh: pix: 8 (over z, x), ch: 4 (over y, core).
Axes of the slice: x: 2, y: 2, z: 4, core: 2. Of those that a mesh axis runs over, the one named last changes fastest.
Arguments:
- pixels: bfloat16 [384, 32768], P('pix', 'ch'), may hold values from -6 to 6
- cotangent: bfloat16 [384, 32768], P('pix', 'ch'), may hold values from -6 to 6
- crop_rows: int32 [16], replicated, may hold values from 1 to 32, 384 in all
- condition: bfloat16 [16, 1024], replicated, may hold values from -6 to 6
- context: bfloat16 [16, 4, 1024], replicated, may hold values from -6 to 6
- kernels: bfloat16 [1024, 18432], P('pix', 'ch'), may hold values from -0.0625 to 0.0625
- attention: bfloat16 [1024, 6144], P('pix', 'ch'), as said below
- embedding: bfloat16 [1024, 2048], P('pix', 'ch'), may hold values from -0.1875 to 0.1875
- gains: float32 [3, 1024], P(None, 'ch'), may hold values from 0.1 to 1.9
- shifts: float32 [3, 1024], P(None, 'ch'), may hold values from -2 to 2
- offsets: float32 [4, 1024], P(None, 'ch'), may hold values from -2 to 2
Outputs:
- result: float32 [384, 32768], P('pix', 'ch')
- grad_pixels: float32 [384, 32768], P('pix', 'ch')
- grad_kernels: float32 [1024, 18432], P('pix', 'ch')
- grad_attention: float32 [1024, 6144], P('pix', 'ch')
- grad_embedding: float32 [1024, 2048], P('pix', 'ch')
- grad_gains: float32 [3, 1024], P(None, 'ch')
- grad_shifts: float32 [3, 1024], P(None, 'ch')
- grad_offsets: float32 [4, 1024], P(None, 'ch')
Inputs may be any that keep to these rules, and one draw needn't show every extreme that they name: crop_rows sums to 384; the largest entry is 32. `attention`: drawn as weights scaled by the fan-in of each matrix.
All inputs are finite; a program needn't handle non-finite values.
Results may differ from a plain program's by a relative error of at most 0.025.
Values may be sent and summed in bfloat16 or wider, within the bound.
No kernel may reach another device: no remote copies, remote signals or barrier semaphores. Data moves between devices by JAX's collectives and lax.ppermute only.
A program may use at most 448 MiB of HBM per device.

v0:
```python
import jax
import jax.numpy as jnp
from jax import lax
from jax.sharding import PartitionSpec as P

HEAD_DIM = 64
W = 32
CROP_ROWS = 32
CTX = 4
GSIZE = 32


HIGHEST = lax.Precision.HIGHEST
EPSILON = 1e-05
NEGATIVE = -1e30


def padded_2(cells, sides, width):
    for axis, dim in sides:
        count = lax.axis_size(axis)
        ends = count - 1
        head = lax.slice_in_dim(cells, 0, width, axis=dim)
        tail = lax.slice_in_dim(cells, cells.shape[dim] - width, cells.shape[dim], axis=dim)
        cells = jnp.concatenate(
            [
                lax.ppermute(tail, axis, [(i, (i + 1) % count) for i in range(ends)]),
                cells,
                lax.ppermute(head, axis, [((i + 1) % count, i) for i in range(ends)]),
            ],
            axis=dim,
        )
    return cells


def passed_along(value, axis, by):
    size = lax.axis_size(axis)
    pairs = [(i, i + by) for i in range(size) if 0 <= i + by < size]
    return lax.ppermute(value, axis, pairs)


def crop_lookup(crop_rows, places):
    bounds = jnp.cumsum(crop_rows) * W
    crop_found = jnp.sum((places[:, None] >= bounds[None, :]).astype(jnp.int32), axis=1)
    inside = (places >= 0) & (places < bounds[-1])
    return jnp.where(inside, crop_found, -1)


def tap_offset(tap_index):
    return (tap_index // 3 - 1) * W + tap_index % 3 - 1


def tap_valid(crop_rows, targets, tap_index):
    step_x = tap_index % 3 - 1
    crop_dest = crop_lookup(crop_rows, targets)
    crop_src = crop_lookup(crop_rows, targets + tap_offset(tap_index))
    column = targets % W
    valid_tap = (
        (crop_dest >= 0) & (crop_src == crop_dest) & (column + step_x >= 0) & (column + step_x < W)
    )
    return valid_tap.astype(jnp.bfloat16)


def unpack_rows(packed):
    line_count = packed.shape[0]
    width_here = packed.shape[1] // W
    return (
        packed.reshape(line_count, width_here, W)
        .transpose(0, 2, 1)
        .reshape(line_count * W, width_here)
    )


def pack_rows(flat):
    width_here = flat.shape[1]
    line_count = flat.shape[0] // W
    return (
        flat.reshape(line_count, W, width_here)
        .transpose(0, 2, 1)
        .reshape(line_count, width_here * W)
    )


def unpack_local(packed, count):
    return packed.reshape(packed.shape[0], -1, count).transpose(2, 0, 1)


def pack_local(stacked):
    count = stacked.shape[0]
    return stacked.transpose(1, 2, 0).reshape(stacked.shape[1], stacked.shape[2] * count)


def rims(values):
    return padded_2(values, (("pix", 0),), W)


def all_channels(values):
    return lax.all_gather(values, "ch", axis=1, tiled=True)


def channel_sums(values):
    return lax.psum_scatter(
        values.astype(jnp.bfloat16), "ch", scatter_dimension=1, tiled=True
    ).astype(jnp.float32)


def crop_group_sums(first_term, second_term, selector):
    tokens_here = first_term.shape[0]
    reach = (CROP_ROWS * W - 1) // tokens_here + 1
    first_sum = jnp.dot(
        selector.T, jnp.sum(first_term.reshape(tokens_here, -1, GSIZE), axis=2), precision=HIGHEST
    )
    second_sum = jnp.dot(
        selector.T, jnp.sum(second_term.reshape(tokens_here, -1, GSIZE), axis=2), precision=HIGHEST
    )
    first_total = first_sum
    second_total = second_sum
    for shift_by in range(-reach, reach + 1):
        if shift_by != 0:
            arrived = passed_along((first_sum, second_sum), "pix", shift_by)
            first_total = first_total + arrived[0]
            second_total = second_total + arrived[1]
    return (first_total, second_total)


def norm_forward(values, gain_row, shift_row, selector, counts):
    tokens_here = values.shape[0]
    first_sum, second_sum = crop_group_sums(values, values * values, selector)
    mean_crop = first_sum / counts[:, None]
    inverse = lax.rsqrt(second_sum / counts[:, None] - mean_crop * mean_crop + EPSILON)
    mean_here = jnp.dot(selector, mean_crop, precision=HIGHEST)
    inverse_here = jnp.dot(selector, inverse, precision=HIGHEST)
    grouped = values.reshape(tokens_here, -1, GSIZE)
    normal = ((grouped - mean_here[:, :, None]) * inverse_here[:, :, None]).reshape(tokens_here, -1)
    return (normal * gain_row + shift_row, normal, inverse_here)


def norm_backward(upstream, normal, inverse_here, gain_row, selector, counts):
    tokens_here = upstream.shape[0]
    grad_gain = jnp.sum(upstream * normal, axis=0)
    grad_shift = jnp.sum(upstream, axis=0)
    scaled = upstream * gain_row
    first_sum, second_sum = crop_group_sums(scaled, scaled * normal, selector)
    mean_first = jnp.dot(selector, first_sum / counts[:, None], precision=HIGHEST)
    mean_second = jnp.dot(selector, second_sum / counts[:, None], precision=HIGHEST)
    grouped = scaled.reshape(tokens_here, -1, GSIZE)
    grouped_normal = normal.reshape(tokens_here, -1, GSIZE)
    outcome = inverse_here[:, :, None] * (
        grouped - mean_first[:, :, None] - grouped_normal * mean_second[:, :, None]
    )
    return (outcome.reshape(tokens_here, -1), grad_gain, grad_shift)


def conv_columns(wide, fore_masks):
    tokens_here = fore_masks.shape[1]
    padded = jnp.pad(wide, ((1, 1), (0, 0)))
    pieces = []
    for tap_index in range(9):
        start_row = 1 + W + tap_offset(tap_index)
        pieces.append(padded[start_row : start_row + tokens_here] * fore_masks[tap_index][:, None])
    return jnp.concatenate(pieces, axis=1)


def shifted_taps(rimmed, back_masks):
    tokens_here = back_masks.shape[1]
    padded = jnp.pad(rimmed, ((1, 1), (0, 0)))
    pieces = []
    for tap_index in range(9):
        start_row = 1 + W - tap_offset(tap_index)
        pieces.append(padded[start_row : start_row + tokens_here] * back_masks[tap_index][:, None])
    return jnp.stack(pieces, axis=1)


def conv_backward(grad_out, columns, layer_kernels, back_masks):
    grad_kernel = jnp.einsum("tk,tc->kc", columns, grad_out, preferred_element_type=jnp.float32)
    stacked = shifted_taps(rims(grad_out), back_masks)
    grad_in = channel_sums(
        jnp.einsum("tkc,kdc->td", stacked, layer_kernels, preferred_element_type=jnp.float32)
    )
    return (grad_in, grad_kernel.reshape(layer_kernels.shape))


def silu_slope(values):
    sigmoid = jax.nn.sigmoid(values)
    return sigmoid * (1.0 + values * (1.0 - sigmoid))


def local(
    pixels,
    cotangent,
    crop_rows,
    condition,
    context,
    kernels,
    attention,
    embedding,
    gains,
    shifts,
    offsets,
):
    inputs_flat = unpack_rows(pixels)
    tokens_here = inputs_flat.shape[0]
    width_here = inputs_flat.shape[1]
    heads_here = width_here // HEAD_DIM
    crop_count = crop_rows.shape[0]
    reach = (CROP_ROWS * W - 1) // tokens_here + 1
    block_rows = min(512, tokens_here)
    block_count = tokens_here // block_rows
    places = lax.axis_index("pix") * tokens_here + jnp.arange(tokens_here, dtype=jnp.int32)
    crop_here = crop_lookup(crop_rows, places)
    selector = (crop_here[:, None] == jnp.arange(crop_count, dtype=jnp.int32)[None, :]).astype(
        jnp.float32
    )
    counts = (crop_rows * (W * GSIZE)).astype(jnp.float32)
    fore_masks = jnp.stack([tap_valid(crop_rows, places, tap_index) for tap_index in range(9)])
    back_masks = jnp.stack(
        [tap_valid(crop_rows, places - tap_offset(tap_index), tap_index) for tap_index in range(9)]
    )
    kernels_packed, attention_packed, embedding_packed = (
        lax.all_gather(kernels, "pix", axis=0, tiled=True),
        lax.all_gather(attention, "pix", axis=0, tiled=True),
        lax.all_gather(embedding, "pix", axis=0, tiled=True),
    )
    kernels_all = unpack_local(kernels_packed, 18)
    maps_all = unpack_local(attention_packed, 6)
    projections_all = maps_all[:3]
    encoder_all = maps_all[3:5]
    readout_all = maps_all[5].T
    embedding_all = unpack_local(embedding_packed, 2)
    score_scale = HEAD_DIM ** (-0.5)
    inputs = inputs_flat.astype(jnp.float32)
    norm_one, normal_one, inverse_one = norm_forward(inputs, gains[0], shifts[0], selector, counts)
    active_one = jax.nn.silu(norm_one).astype(jnp.bfloat16)
    columns_one = conv_columns(all_channels(rims(active_one)), fore_masks)
    conv_one = jnp.dot(
        columns_one, kernels_all[:9].reshape(-1, width_here), preferred_element_type=jnp.float32
    )
    embed_terms = (
        jnp.einsum("nc,jcd->njd", condition, embedding_all, preferred_element_type=jnp.float32)
        + offsets[2:4][None]
    )
    growth = 1.0 + jnp.dot(selector, embed_terms[:, 0], precision=HIGHEST)
    shift_add = jnp.dot(selector, embed_terms[:, 1], precision=HIGHEST)
    norm_two, normal_two, inverse_two = norm_forward(
        conv_one, gains[1], shifts[1], selector, counts
    )
    inner_two = norm_two * growth + shift_add
    active_two = jax.nn.silu(inner_two).astype(jnp.bfloat16)
    columns_two = conv_columns(all_channels(rims(active_two)), fore_masks)
    conv_two = jnp.dot(
        columns_two, kernels_all[9:].reshape(-1, width_here), preferred_element_type=jnp.float32
    )
    residual = inputs + conv_two + offsets[0]
    norm_three, normal_three, inverse_three = norm_forward(
        residual, gains[2], shifts[2], selector, counts
    )
    normed_all = all_channels(norm_three.astype(jnp.bfloat16))
    qkv_rows = jnp.einsum(
        "tc,jcd->jtd", normed_all, projections_all, preferred_element_type=jnp.float32
    ).astype(jnp.bfloat16)
    context_flat = context.reshape(-1, context.shape[2])
    context_pairs = jnp.einsum(
        "nc,jcd->jnd", context_flat, encoder_all, preferred_element_type=jnp.float32
    ).astype(jnp.bfloat16)
    key_list = []
    value_list = []
    crop_list = []
    for shift_by in range(-reach, reach + 1):
        if shift_by == 0:
            arrived = (qkv_rows[1], qkv_rows[2])
        else:
            arrived = passed_along((qkv_rows[1], qkv_rows[2]), "pix", shift_by)
        key_list.append(arrived[0])
        value_list.append(arrived[1])
        crop_list.append(crop_lookup(crop_rows, places - shift_by * tokens_here))
    key_list.append(context_pairs[0])
    value_list.append(context_pairs[1])
    crop_list.append(jnp.repeat(jnp.arange(crop_count, dtype=jnp.int32), CTX))
    keys_all = jnp.concatenate(key_list).reshape(-1, heads_here, HEAD_DIM)
    values_all = jnp.concatenate(value_list).reshape(-1, heads_here, HEAD_DIM)
    key_crops = jnp.concatenate(crop_list)
    key_total = keys_all.shape[0]
    query_blocks = qkv_rows[0].reshape(block_count, block_rows, heads_here, HEAD_DIM)
    crop_blocks = crop_here.reshape(block_count, block_rows)

    def scores_block(query_block, crop_block):
        raw_scores = (
            jnp.einsum("qhd,khd->hqk", query_block, keys_all, preferred_element_type=jnp.float32)
            * score_scale
        )
        return jnp.where((crop_block[:, None] == key_crops[None, :])[None], raw_scores, NEGATIVE)

    def forward_block(inputs_block):
        query_block, crop_block = inputs_block
        scores = scores_block(query_block, crop_block)
        largest = jnp.max(scores, axis=2, keepdims=True)
        log_total = largest + jnp.log(jnp.sum(jnp.exp(scores - largest), axis=2, keepdims=True))
        prob_rows = jnp.exp(scores - log_total).astype(jnp.bfloat16)
        mixed = jnp.einsum(
            "hqk,khd->qhd", prob_rows, values_all, preferred_element_type=jnp.float32
        )
        return (mixed.reshape(block_rows, width_here).astype(jnp.bfloat16), log_total)

    attended_blocks, log_blocks = lax.map(forward_block, (query_blocks, crop_blocks))
    attended = attended_blocks.reshape(tokens_here, width_here)
    projected = channel_sums(jnp.dot(attended, readout_all, preferred_element_type=jnp.float32))
    result = residual + projected + offsets[1]
    cotangent_flat = unpack_rows(cotangent)
    grad_result = cotangent_flat.astype(jnp.float32)
    grad_all = all_channels(cotangent_flat)
    grad_readout = jnp.einsum("tc,td->cd", attended, grad_all, preferred_element_type=jnp.float32)
    grad_attended = jnp.einsum(
        "td,cd->tc", grad_all, readout_all, preferred_element_type=jnp.float32
    ).astype(jnp.bfloat16)
    grad_blocks = grad_attended.reshape(block_count, block_rows, heads_here, HEAD_DIM)

    def backward_block(carry, inputs_block):
        keys_sum, values_sum = carry
        query_block, crop_block, grad_block, log_block = inputs_block
        scores = scores_block(query_block, crop_block)
        prob_full = jnp.exp(scores - log_block)
        prob_rows = prob_full.astype(jnp.bfloat16)
        grad_probs = jnp.einsum(
            "qhd,khd->hqk", grad_block, values_all, preferred_element_type=jnp.float32
        )
        row_dot = jnp.sum(prob_full * grad_probs, axis=2, keepdims=True)
        grad_scores = (prob_full * (grad_probs - row_dot)).astype(jnp.bfloat16)
        grad_query = (
            jnp.einsum("hqk,khd->qhd", grad_scores, keys_all, preferred_element_type=jnp.float32)
            * score_scale
        ).reshape(block_rows, width_here)
        keys_sum = keys_sum + (
            jnp.einsum("hqk,qhd->khd", grad_scores, query_block, preferred_element_type=jnp.float32)
            * score_scale
        ).reshape(key_total, width_here)
        values_sum = values_sum + jnp.einsum(
            "hqk,qhd->khd", prob_rows, grad_block, preferred_element_type=jnp.float32
        ).reshape(key_total, width_here)
        return ((keys_sum, values_sum), grad_query)

    empty_keys = jnp.zeros((key_total, width_here), jnp.float32)
    (grad_keys, grad_values), grad_query_blocks = lax.scan(
        backward_block,
        (empty_keys, empty_keys),
        (query_blocks, crop_blocks, grad_blocks, log_blocks),
    )
    grad_queries = grad_query_blocks.reshape(tokens_here, width_here)
    own_start = reach * tokens_here
    grad_keys_local = grad_keys[own_start : own_start + tokens_here]
    grad_values_local = grad_values[own_start : own_start + tokens_here]
    for shift_by in range(-reach, reach + 1):
        if shift_by != 0:
            block_start = (shift_by + reach) * tokens_here
            returned = (
                passed_along(
                    grad_keys[block_start : block_start + tokens_here].astype(jnp.bfloat16),
                    "pix",
                    -shift_by,
                ).astype(jnp.float32),
                passed_along(
                    grad_values[block_start : block_start + tokens_here].astype(jnp.bfloat16),
                    "pix",
                    -shift_by,
                ).astype(jnp.float32),
            )
            grad_keys_local = grad_keys_local + returned[0]
            grad_values_local = grad_values_local + returned[1]
    context_start = (2 * reach + 1) * tokens_here
    grad_context = jnp.stack([grad_keys[context_start:], grad_values[context_start:]])
    grad_encoder = jnp.einsum(
        "nc,jnd->jcd", context_flat.astype(jnp.float32), grad_context, precision=HIGHEST
    )
    grad_triple = jnp.stack([grad_queries, grad_keys_local, grad_values_local]).astype(jnp.bfloat16)
    grad_projections = jnp.einsum(
        "tc,jtd->jcd", normed_all, grad_triple, preferred_element_type=jnp.float32
    )
    grad_attention = pack_local(
        jnp.concatenate([grad_projections, grad_encoder, grad_readout.T[None]], axis=0)
    )
    grad_normed = lax.psum_scatter(
        jnp.einsum(
            "jtd,jcd->tc", grad_triple, projections_all, preferred_element_type=jnp.float32
        ).astype(jnp.bfloat16),
        "ch",
        scatter_dimension=1,
        tiled=True,
    ).astype(jnp.float32)
    grad_from_norm, grad_gain_three, grad_shift_three = norm_backward(
        grad_normed, normal_three, inverse_three, gains[2], selector, counts
    )
    grad_residual = grad_result + grad_from_norm
    grad_offset_conv = jnp.sum(grad_residual, axis=0)
    grad_offset_out = jnp.sum(grad_result, axis=0)
    grad_active_two, grad_kernel_two = conv_backward(
        grad_residual.astype(jnp.bfloat16), columns_two, kernels_all[9:], back_masks
    )
    grad_inner = grad_active_two * silu_slope(inner_two)
    grad_embed = jnp.stack(
        [
            jnp.dot(selector.T, grad_inner * norm_two, precision=HIGHEST),
            jnp.dot(selector.T, grad_inner, precision=HIGHEST),
        ],
        axis=1,
    )
    grad_embedding = pack_local(
        jnp.einsum("nc,njd->jcd", condition.astype(jnp.float32), grad_embed, precision=HIGHEST)
    )
    grad_offset_embed = jnp.sum(grad_embed, axis=0)
    grad_conv_one, grad_gain_two, grad_shift_two = norm_backward(
        grad_inner * growth, normal_two, inverse_two, gains[1], selector, counts
    )
    grad_active_one, grad_kernel_one = conv_backward(
        grad_conv_one.astype(jnp.bfloat16), columns_one, kernels_all[:9], back_masks
    )
    grad_pre_one = grad_active_one * silu_slope(norm_one)
    grad_input_norm, grad_gain_one, grad_shift_one = norm_backward(
        grad_pre_one, normal_one, inverse_one, gains[0], selector, counts
    )
    grad_pixels = grad_residual + grad_input_norm
    grad_gains, grad_shifts, grad_offsets = lax.psum(
        (
            jnp.stack([grad_gain_one, grad_gain_two, grad_gain_three]),
            jnp.stack([grad_shift_one, grad_shift_two, grad_shift_three]),
            jnp.stack(
                [grad_offset_conv, grad_offset_out, grad_offset_embed[0], grad_offset_embed[1]]
            ),
        ),
        "pix",
    )
    grad_kernels = pack_local(jnp.concatenate([grad_kernel_one, grad_kernel_two], axis=0))
    reduced = (
        lax.psum_scatter(
            grad_kernels.astype(jnp.bfloat16), "pix", scatter_dimension=0, tiled=True
        ).astype(jnp.float32),
        lax.psum_scatter(
            grad_attention.astype(jnp.bfloat16), "pix", scatter_dimension=0, tiled=True
        ).astype(jnp.float32),
        lax.psum_scatter(
            grad_embedding.astype(jnp.bfloat16), "pix", scatter_dimension=0, tiled=True
        ).astype(jnp.float32),
    )
    return (
        pack_rows(result),
        pack_rows(grad_pixels),
        reduced[0],
        reduced[1],
        reduced[2],
        grad_gains,
        grad_shifts,
        grad_offsets,
    )


def solution(mesh):
    placed = (
        P("pix", "ch"),
        P("pix", "ch"),
        P(),
        P(),
        P(),
        P("pix", "ch"),
        P("pix", "ch"),
        P("pix", "ch"),
        P(None, "ch"),
        P(None, "ch"),
        P(None, "ch"),
    )
    return jax.shard_map(
        local,
        mesh=mesh,
        in_specs=placed,
        out_specs=(
            P("pix", "ch"),
            P("pix", "ch"),
            P("pix", "ch"),
            P("pix", "ch"),
            P("pix", "ch"),
            P(None, "ch"),
            P(None, "ch"),
            P(None, "ch"),
        ),
        check_vma=False,
    )
```

profile of v0, /device:TPU:0, one launch (start us, length us, event | category | flops | bytes accessed | tf_op | source)
XLA Modules:
  0.0 1767.3 jit_solution(15438860938599261069)
XLA Ops:
  21.8 8.0 fusion.327
  73.5 15.4 all-gather.12.cloned.1.call-done
  93.0 26.5 %all-gather.8.cloned.1.call-done = bf16[1600,1024]{1,0:T(8,128)(2,1)} async-done(((bf16[1600,256]{1,0:T(8,128)(2,1)}), bf16[1600,1024]{1,0:T(8,128)(2,1)}) %all-gather.8.cloned.1.call-update) | async-done | bytes 3276816 | tf_op jit(solution)/shard_map/all_gather | solution.py:97
  144.0 115.7 %all-gather.10.cloned.1.call-done = bf16[1024,4608]{1,0:T(8,128)(2,1)} async-done(((bf16[128,4608]{1,0:T(8,128)(2,1)}), bf16[1024,4608]{1,0:T(8,128)(2,1)}) %all-gather.10.cloned.1.call-update) | async-done | bytes 9437200 | tf_op jit(solution)/shard_map/all_gather | solution.py:219
  259.8 12.6 copy.188
  272.4 13.9 reshape.771
  286.3 15.4 copy.189
  301.8 6.7 fusion.334
  308.5 14.7 fusion.346
  363.5 28.9 %all-gather.14.cloned.1.call-done = bf16[1600,1024]{1,0:T(8,128)(2,1)} async-done(((bf16[1600,256]{1,0:T(8,128)(2,1)}), bf16[1600,1024]{1,0:T(8,128)(2,1)}) %all-gather.14.cloned.1.call-update) | async-done | bytes 3276816 | tf_op jit(solution)/shard_map/all_gather | solution.py:97
  402.9 9.5 copy-done.8
  412.3 15.2 fusion.347
  477.6 6.5 all-gather.16.cloned.1.call-done
  496.9 17.8 %all-gather.20.cloned.1.call-done = bf16[1536,1024]{1,0:T(8,128)(2,1)} async-done(((bf16[1536,256]{1,0:T(8,128)(2,1)}), bf16[1536,1024]{1,0:T(8,128)(2,1)}) %all-gather.20.cloned.1.call-update) | async-done | bytes 3145744 | tf_op jit(solution)/shard_map/all_gather | solution.py:97
  530.4 15.8 collective-permute-done.17
  548.0 14.4 collective-permute-done.19
  565.3 173.1 %while.27 = (s32[]{:T(128)}, bf16[3,512,256]{2,1,0:T(8,128)(2,1)}, f32[3,4,512,1]{2,1,3,0:T(4,128)}, s32[3,512]{1,0:T(4,128)S(1)}, s32[4672]{0:T(1024)S(1)}, /*i...) while((s32[]{:T(128)}, bf16[3,512,256]{2,1,0:T(8,128)(2,1)}, ...), condition=%wide.region_21.22_spmd, body=%wide.region_18.21_spmd.sunk | while | flops 2557245440 | bytes 130867568 | solution.py:303
  568.6 17.0 fusion.400
  585.6 16.3 exponential_reduce_fusion.2
  602.6 18.7 %fusion.401 = bf16[4,512,64]{1,2,0:T(8,128)(2,1)} fusion(bf16[4672,4,64]{0,2,1:T(8,128)(2,1)} %get-tuple-element.567, f32[4,512,4672]{1,2,0:T(8,128)} %get-tuple-element.523, f32[4,512]{1,0:T(4,128)S(1)} %get-tuple-element.525, pred[512,4672]{0,1:T(8,128)(4,1)} %broadcast_compare_fusion.7), kind=kOutput, calls=%fused_computation.7.clone.1 | convolution fusion | flops 1263140864 | bytes 43327488 | tf_op jit(solution)/shard_map/while/body/eval_jaxpr/hqk,khd->qhd/dot_general | solution.py:298
  626.3 17.0 fusion.400
  643.4 16.3 exponential_reduce_fusion.2
  660.3 18.7 %fusion.401 = bf16[4,512,64]{1,2,0:T(8,128)(2,1)} fusion(bf16[4672,4,64]{0,2,1:T(8,128)(2,1)} %get-tuple-element.567, f32[4,512,4672]{1,2,0:T(8,128)} %get-tuple-element.523, f32[4,512]{1,0:T(4,128)S(1)} %get-tuple-element.525, pred[512,4672]{0,1:T(8,128)(4,1)} %broadcast_compare_fusion.7), kind=kOutput, calls=%fused_computation.7.clone.1 | convolution fusion | flops 1263140864 | bytes 43327488 | tf_op jit(solution)/shard_map/while/body/eval_jaxpr/hqk,khd->qhd/dot_general | solution.py:298
  684.0 17.0 fusion.400
  701.1 16.3 exponential_reduce_fusion.2
  718.0 18.6 %fusion.401 = bf16[4,512,64]{1,2,0:T(8,128)(2,1)} fusion(bf16[4672,4,64]{0,2,1:T(8,128)(2,1)} %get-tuple-element.567, f32[4,512,4672]{1,2,0:T(8,128)} %get-tuple-element.523, f32[4,512]{1,0:T(4,128)S(1)} %get-tuple-element.525, pred[512,4672]{0,1:T(8,128)(4,1)} %broadcast_compare_fusion.7), kind=kOutput, calls=%fused_computation.7.clone.1 | convolution fusion | flops 1263140864 | bytes 43327488 | tf_op jit(solution)/shard_map/while/body/eval_jaxpr/hqk,khd->qhd/dot_general | solution.py:298
  738.5 404.5 %while.28 = (s32[]{:T(128)}, f32[4672,256]{0,1:T(8,128)}, f32[4672,256]{0,1:T(8,128)}, bf16[3,512,256]{1,2,0:T(8,128)(2,1)}, bf16[3,512,4,64]{1,3,2,0:T(8,128)(2...) while((s32[]{:T(128)}, f32[4672,256]{0,1:T(8,128)}, ...), condition=%wide.region_25.26_spmd.clone, body=%wide.region_23.25_spmd.clone.sunk | while | flops 6275840000 | bytes 372687328 | solution.py:341
  742.9 16.8 fusion.411
  759.7 18.3 %fusion.412 = f32[4,64,4672]{2,1,0:T(8,128)} fusion(f32[4,512,4672]{1,2,0:T(8,128)} %fusion.411, f32[4,512]{1,0:T(4,128)S(1)} %dynamic-slice_bitcast_fusion.2, pred[512,4672]{0,1:T(8,128)(4,1)S(1)} %broadcast_compare_fusion.8, bf16[3,512,4,64]{1,3,2,0:T(8,128)(2,1)} %get-tuple-element.604, s32[]{:T(128)S(6)} %copy.306), kind=kOutput, calls=%fused_computation.22.clone.1 | convolution fusion | flops 1263009792 | bytes 45719556 | tf_op jit(solution)/shard_map/while/body/eval_jaxpr/hqk,qhd->khd/dot_general | solution.py:335
  778.0 29.9 %multiply_reduce_fusion.6 = (f32[4,512]{1,0:T(4,128)S(1)}, f32[4,512,4672]{1,2,0:T(8,128)}) fusion(f32[4,512,4672]{1,2,0:T(8,128)} %fusion.411, f32[4,512]{1,0:T(4,128)S(1)} %dynamic-slice_bitcast_fusion.2, pred[512,4672]{0,1:T(8,128)(4,1)S(1)} %broadcast_compare_fusion.8, bf16[4672,4,64]{0,2,1:T(8,128)(2,1)S(1)} %copy-done.5, ...), kind=kOutput, calls=%fused_computation.19.clone.1 | convolution fusion | flops 1272576000 | bytes 81608704 | tf_op jit(solution)/shard_map/while/body/eval_jaxpr/qhd,khd->hqk/dot_general | solution.py:322
  807.9 31.8 %multiply_convert_fusion.6 = bf16[4,512,4672]{1,2,0:T(8,128)(2,1)} fusion(f32[4,512,4672]{1,2,0:T(8,128)} %get-tuple-element.538, f32[4,512,4672]{1,2,0:T(8,128)} %fusion.411, f32[4,512]{1,0:T(4,128)S(1)} %get-tuple-element.539, f32[4,512]{1,0:T(4,128)S(1)} %dynamic-slice_bitcast_fusion.2, pred[512,4672]{0,1:T(8,128)(4,1)S(1)} %broadcast_compare_fusion.8), kind=kLoop, calls=%fused_computation.18.clone.1 | loop fusion | flops 57409536 | bytes 98091008 | tf_op jit(solution)/shard_map/while/body/eval_jaxpr/convert_element_type | solution.py:326
  839.6 10.6 convolution_multiply_fusion.5
  850.2 11.9 convolution_multiply_fusion.4
  862.2 8.6 bitcast_add_fusion.3
  875.7 16.8 fusion.411
  892.5 18.3 %fusion.412 = f32[4,64,4672]{2,1,0:T(8,128)} fusion(f32[4,512,4672]{1,2,0:T(8,128)} %fusion.411, f32[4,512]{1,0:T(4,128)S(1)} %dynamic-slice_bitcast_fusion.2, pred[512,4672]{0,1:T(8,128)(4,1)S(1)} %broadcast_compare_fusion.8, bf16[3,512,4,64]{1,3,2,0:T(8,128)(2,1)} %get-tuple-element.604, s32[]{:T(128)S(6)} %copy.306), kind=kOutput, calls=%fused_computation.22.clone.1 | convolution fusion | flops 1263009792 | bytes 45719556 | tf_op jit(solution)/shard_map/while/body/eval_jaxpr/hqk,qhd->khd/dot_general | solution.py:335
  910.8 29.9 %multiply_reduce_fusion.6 = (f32[4,512]{1,0:T(4,128)S(1)}, f32[4,512,4672]{1,2,0:T(8,128)}) fusion(f32[4,512,4672]{1,2,0:T(8,128)} %fusion.411, f32[4,512]{1,0:T(4,128)S(1)} %dynamic-slice_bitcast_fusion.2, pred[512,4672]{0,1:T(8,128)(4,1)S(1)} %broadcast_compare_fusion.8, bf16[4672,4,64]{0,2,1:T(8,128)(2,1)S(1)} %copy-done.5, ...), kind=kOutput, calls=%fused_computation.19.clone.1 | convolution fusion | flops 1272576000 | bytes 81608704 | tf_op jit(solution)/shard_map/while/body/eval_jaxpr/qhd,khd->hqk/dot_general | solution.py:322
  940.7 31.8 %multiply_convert_fusion.6 = bf16[4,512,4672]{1,2,0:T(8,128)(2,1)} fusion(f32[4,512,4672]{1,2,0:T(8,128)} %get-tuple-element.538, f32[4,512,4672]{1,2,0:T(8,128)} %fusion.411, f32[4,512]{1,0:T(4,128)S(1)} %get-tuple-element.539, f32[4,512]{1,0:T(4,128)S(1)} %dynamic-slice_bitcast_fusion.2, pred[512,4672]{0,1:T(8,128)(4,1)S(1)} %broadcast_compare_fusion.8), kind=kLoop, calls=%fused_computation.18.clone.1 | loop fusion | flops 57409536 | bytes 98091008 | tf_op jit(solution)/shard_map/while/body/eval_jaxpr/convert_element_type | solution.py:326
  972.5 10.6 convolution_multiply_fusion.5
  983.1 11.9 convolution_multiply_fusion.4
  995.0 11.3 bitcast_add_fusion.3
  1011.3 16.8 fusion.411
  1028.1 18.3 %fusion.412 = f32[4,64,4672]{2,1,0:T(8,128)} fusion(f32[4,512,4672]{1,2,0:T(8,128)} %fusion.411, f32[4,512]{1,0:T(4,128)S(1)} %dynamic-slice_bitcast_fusion.2, pred[512,4672]{0,1:T(8,128)(4,1)S(1)} %broadcast_compare_fusion.8, bf16[3,512,4,64]{1,3,2,0:T(8,128)(2,1)} %get-tuple-element.604, s32[]{:T(128)S(6)} %copy.306), kind=kOutput, calls=%fused_computation.22.clone.1 | convolution fusion | flops 1263009792 | bytes 45719556 | tf_op jit(solution)/shard_map/while/body/eval_jaxpr/hqk,qhd->khd/dot_general | solution.py:335
  1046.4 29.9 %multiply_reduce_fusion.6 = (f32[4,512]{1,0:T(4,128)S(1)}, f32[4,512,4672]{1,2,0:T(8,128)}) fusion(f32[4,512,4672]{1,2,0:T(8,128)} %fusion.411, f32[4,512]{1,0:T(4,128)S(1)} %dynamic-slice_bitcast_fusion.2, pred[512,4672]{0,1:T(8,128)(4,1)S(1)} %broadcast_compare_fusion.8, bf16[4672,4,64]{0,2,1:T(8,128)(2,1)S(1)} %copy-done.5, ...), kind=kOutput, calls=%fused_computation.19.clone.1 | convolution fusion | flops 1272576000 | bytes 81608704 | tf_op jit(solution)/shard_map/while/body/eval_jaxpr/qhd,khd->hqk/dot_general | solution.py:322
  1076.3 31.8 %multiply_convert_fusion.6 = bf16[4,512,4672]{1,2,0:T(8,128)(2,1)} fusion(f32[4,512,4672]{1,2,0:T(8,128)} %get-tuple-element.538, f32[4,512,4672]{1,2,0:T(8,128)} %fusion.411, f32[4,512]{1,0:T(4,128)S(1)} %get-tuple-element.539, f32[4,512]{1,0:T(4,128)S(1)} %dynamic-slice_bitcast_fusion.2, pred[512,4672]{0,1:T(8,128)(4,1)S(1)} %broadcast_compare_fusion.8), kind=kLoop, calls=%fused_computation.18.clone.1 | loop fusion | flops 57409536 | bytes 98091008 | tf_op jit(solution)/shard_map/while/body/eval_jaxpr/convert_element_type | solution.py:326
  1108.0 10.6 convolution_multiply_fusion.5
  1118.6 11.9 convolution_multiply_fusion.4
  1130.6 11.3 bitcast_add_fusion.3
  1174.7 32.8 %collective-permute-done.20 = bf16[1536,256]{1,0:T(8,128)(2,1)} collective-permute-done((bf16[1536,256]{1,0:T(8,128)(2,1)S(1)}, bf16[1536,256]{1,0:T(8,128)(2,1)}, u32[]{:S(2)}, u32[]{:S(2)}) %collective-permute-start.20) | collective-permute-done | bytes 786464 | tf_op jit(solution)/shard_map/ppermute | solution.py:38
  1209.7 13.2 collective-permute-done.22
  1229.9 40.5 %reduce-scatter.16.cloned.1.call-done = bf16[1536,256]{1,0:T(8,128)(2,1)} async-done(((bf16[1536,1024]{1,0:T(8,128)(2,1)}), bf16[1536,256]{1,0:T(8,128)(2,1)}) %reduce-scatter.16.cloned.1.call-update) | async-done | bytes 786448 | tf_op jit(solution)/shard_map/reduce_scatter | solution.py:379
  1316.9 9.5 bitcast_convert_fusion.1
  1356.5 7.4 reduce-scatter.18.cloned.1.call-done
  1422.1 11.0 bitcast_convert_fusion
  1433.3 36.7 %copy.234 = bf16[9216,1536]{1,0:T(8,128)(2,1)} copy(bf16[9216,1536]{0,1:T(8,128)(2,1)} %bitcast.92) | data formatting | bytes 56623104 | tf_op jit(solution)/shard_map/tk,tc->kc/dot_general | solution.py:174
  1470.1 36.7 %copy.236 = bf16[9216,1536]{1,0:T(8,128)(2,1)} copy(bf16[9216,1536]{0,1:T(8,128)(2,1)} %bitcast.364) | data formatting | bytes 56623104 | tf_op jit(solution)/shard_map/tk,tc->kc/dot_general | solution.py:174
  1506.8 13.4 convolution_convert_fusion.2
  1520.2 15.5 convolution_convert_fusion.3
  1539.2 23.7 %copy.238 = bf16[1024,256,18]{0,2,1:T(8,128)(2,1)} copy(bf16[1024,256,18]{0,1,2:T(8,128)(2,1)S(1)} %maximum_bitcast_fusion) | data formatting | bytes 18874368 | tf_op jit(solution)/shard_map/convert_element_type | solution.py:432
  1562.9 14.2 convert_element_type.410
  1577.1 12.4 copy.258
  1617.5 6.3 collective-permute-start.39
  1635.1 40.3 %all-reduce.4 = (f32[3,256]{1,0:T(4,128)}, f32[3,256]{1,0:T(4,128)}, f32[4,256]{1,0:T(4,128)}) all-reduce(f32[3,256]{1,0:T(4,128)S(1)} %pad_maximum_fusion.13, f32[3,256]{1,0:T(4,128)S(1)} %pad_maximum_fusion.14, f32[4,256]{1,0:T(4,128)S(1)} %pad_maximum_fusion.15), channel_id=1, replica_groups=mesh['pix'=8,'ch'=4] {'pix'}, use_global_device_ids=true, to_apply=%region_41.42 | all-reduce | flops 2560 | bytes 20480 | tf_op jit(solution)/shard_map/psum | solution.py:419
  1698.6 58.5 %reduce-scatter.22.cloned.1.call-done = bf16[128,4608]{1,0:T(8,128)(2,1)} async-done(((bf16[1024,4608]{1,0:T(8,128)(2,1)}), bf16[128,4608]{1,0:T(8,128)(2,1)}) %reduce-scatter.22.cloned.1.call-update) | async-done | bytes 1179664
  (528 shorter events, 496.1 us)
Async XLA Ops:
  7.2 84.7 %copy-start = (bf16[16,1024]{1,0:T(8,128)(2,1)S(1)}, bf16[16,1024]{1,0:T(8,128)(2,1)}, u32[]{:S(2)}) copy-start(bf16[16,1024]{1,0:T(8,128)(2,1)} %param.18) | copy-start | bytes 98308
  7.2 81.7 %all-gather.12.cloned.1.call-start = ((), (), s32[]{:S(2)}) async-start(), calls=%async_computation.9 | async-start | bytes 1179648 | tf_op jit(solution)/shard_map/all_gather | solution.py:221
  31.3 430.5 %copy-start.41 = (s32[1536]{0:T(1024)}, s32[1536]{0:T(1024)S(1)}, u32[]{:S(2)}) copy-start(s32[1536]{0:T(1024)S(1)} %get-tuple-element.322) | copy-start | bytes 18436
  32.3 20.0 %collective-permute-start.3 = (f32[16,8]{0,1:T(8,128)S(1)}, f32[16,8]{0,1:T(8,128)S(1)}, u32[]{:S(2)}, u32[]{:S(2)}) collective-permute-start(f32[16,8]{0,1:T(8,128)S(1)} %fusion.160), channel_id=1, source_target_pairs={{0,4},{4,8},{8,12},{12,16},{16,20},{20,24},{24,28},{1,5},{5,9},{9,... | collective-permute-start | bytes 1544 | tf_op jit(solution)/shard_map/ppermute | solution.py:38
  37.2 15.2 collective-permute-start.2
  39.4 6.1 collective-permute-start.1
  44.0 5.9 collective-permute-start
  45.3 74.2 %all-gather.8.cloned.1.call-start = ((), (), s32[]{:S(2)}) async-start(), calls=%async_computation.7 | async-start | bytes 4096000 | tf_op jit(solution)/shard_map/all_gather | solution.py:97
  45.4 303.3 %copy-start.60 = (f32[1,256]{1,0:T(1,128)}, f32[1,256]{1,0:T(1,128)S(1)}, u32[]{:S(2)}) copy-start(f32[1,256]{1,0:T(1,128)S(1)} %get-tuple-element.390) | copy-start | bytes 3076
  45.4 405.0 %copy-start.56 = (f32[1,256]{1,0:T(1,128)}, f32[1,256]{1,0:T(1,128)S(1)}, u32[]{:S(2)}) copy-start(f32[1,256]{1,0:T(1,128)S(1)} %get-tuple-element.388) | copy-start | bytes 3076
  45.5 303.3 %copy-start.62 = (f32[1,256]{1,0:T(1,128)}, f32[1,256]{1,0:T(1,128)S(1)}, u32[]{:S(2)}) copy-start(f32[1,256]{1,0:T(1,128)S(1)} %get-tuple-element.393) | copy-start | bytes 3076
  45.5 401.1 %copy-start.73 = (f32[16]{0:T(128)}, f32[16]{0:T(128)S(1)}, u32[]{:S(2)}) copy-start(f32[16]{0:T(128)S(1)} %multiply_convert_fusion.4) | copy-start | bytes 196
  59.8 6.3 collective-permute-start.4
  64.6 5.6 collective-permute-start.5
  71.2 188.6 %all-gather.10.cloned.1.call-start = ((), (), s32[]{:S(2)}) async-start(), calls=%async_computation.8 | async-start | bytes 10616832 | tf_op jit(solution)/shard_map/all_gather | solution.py:219
  72.0 320.4 %all-gather.14.cloned.1.call-start = ((), (), s32[]{:S(2)}) async-start(), calls=%async_computation.10 | async-start | bytes 4096000 | tf_op jit(solution)/shard_map/all_gather | solution.py:97
  73.5 324.8 %copy-start.44 = (bf16[1536]{0:T(1024)(128)(2,1)}, bf16[1536]{0:T(1024)(128)(2,1)S(1)}, u32[]{:S(2)}) copy-start(bf16[1536]{0:T(1024)(128)(2,1)S(1)} %get-tuple-element.383) | copy-start | bytes 9220
  93.0 255.8 %copy-start.20 = (f32[1536,256]{1,0:T(8,128)}, f32[1536,256]{1,0:T(8,128)S(1)}, u32[]{:S(2)}) copy-start(f32[1536,256]{1,0:T(8,128)S(1)} %convolution_add_fusion.1) | copy-start | bytes 4718596
  325.7 12.2 collective-permute-start.7
  328.2 9.7 collective-permute-start.6
  332.1 8.3 collective-permute-start.9
  336.7 5.5 collective-permute-start.8
  351.3 5.7 collective-permute-start.10
  355.6 5.6 collective-permute-start.11
  362.2 100.3 %all-gather.18.cloned.1.call-start = ((), (), s32[]{:S(2)}) async-start(), calls=%async_computation.12 | async-start | bytes 3538944 | tf_op jit(solution)/shard_map/all_gather | solution.py:220
  362.8 121.3 %all-gather.16.cloned.1.call-start = ((), (), s32[]{:S(2)}) async-start(), calls=%async_computation.11 | async-start | bytes 3932160 | tf_op jit(solution)/shard_map/all_gather | solution.py:97
  428.7 13.4 collective-permute-start.13
  432.1 9.9 collective-permute-start.12
  436.1 8.4 collective-permute-start.15
  440.7 5.9 collective-permute-start.14
  454.2 60.5 %all-gather.20.cloned.1.call-start = ((), (), s32[]{:S(2)}) async-start(), calls=%async_computation.14 | async-start | bytes 3932160 | tf_op jit(solution)/shard_map/all_gather | solution.py:97
  460.2 810.2 %reduce-scatter.16.cloned.1.call-start = ((), (), s32[]{:S(2)}) async-start(), calls=%async_computation.15 | async-start | bytes 3932160 | tf_op jit(solution)/shard_map/reduce_scatter | solution.py:379
  490.9 55.3 %collective-permute-start.17 = (bf16[1536,256]{0,1:T(8,128)(2,1)}, bf16[1536,256]{0,1:T(8,128)(2,1)}, u32[]{:S(2)}, u32[]{:S(2)}) collective-permute-start(bf16[1536,256]{0,1:T(8,128)(2,1)} %get-tuple-element.341), channel_id=1, source_target_pairs={{0,4},{4,8},{8,12},{12,16},{16,20},{20,24},{24,28},{1,5},{5,9},{9,... | collective-permute-start | bytes 2359304 | tf_op jit(solution)/shard_map/ppermute | solution.py:38
  495.2 51.0 %collective-permute-start.16 = (bf16[1536,256]{0,1:T(8,128)(2,1)}, bf16[1536,256]{0,1:T(8,128)(2,1)}, u32[]{:S(2)}, u32[]{:S(2)}) collective-permute-start(bf16[1536,256]{0,1:T(8,128)(2,1)} %get-tuple-element.341), channel_id=1, source_target_pairs={{4,0},{8,4},{12,8},{16,12},{20,16},{24,20},{28,24},{5,1},{9,5},{13... | collective-permute-start | bytes 2359304 | tf_op jit(solution)/shard_map/ppermute | solution.py:38
  518.5 43.9 %collective-permute-start.19 = (bf16[1536,256]{0,1:T(8,128)(2,1)}, bf16[1536,256]{0,1:T(8,128)(2,1)}, u32[]{:S(2)}, u32[]{:S(2)}) collective-permute-start(bf16[1536,256]{0,1:T(8,128)(2,1)} %get-tuple-element.342), channel_id=1, source_target_pairs={{0,4},{4,8},{8,12},{12,16},{16,20},{20,24},{24,28},{1,5},{5,9},{9,... | collective-permute-start | bytes 2359304 | tf_op jit(solution)/shard_map/ppermute | solution.py:38
  522.9 39.5 %collective-permute-start.18 = (bf16[1536,256]{0,1:T(8,128)(2,1)}, bf16[1536,256]{0,1:T(8,128)(2,1)}, u32[]{:S(2)}, u32[]{:S(2)}) collective-permute-start(bf16[1536,256]{0,1:T(8,128)(2,1)} %get-tuple-element.342), channel_id=1, source_target_pairs={{4,0},{8,4},{12,8},{16,12},{20,16},{24,20},{28,24},{5,1},{9,5},{13... | collective-permute-start | bytes 2359304 | tf_op jit(solution)/shard_map/ppermute | solution.py:38
  1151.4 56.1 %collective-permute-start.20 = (bf16[1536,256]{1,0:T(8,128)(2,1)S(1)}, bf16[1536,256]{1,0:T(8,128)(2,1)}, u32[]{:S(2)}, u32[]{:S(2)}) collective-permute-start(bf16[1536,256]{1,0:T(8,128)(2,1)S(1)} %get-tuple-element.335), channel_id=1, source_target_pairs={{0,4},{4,8},{8,12},{12,16},{16,20},{20,24},{24,28},{1,5},{5,9},{9,... | collective-permute-start | bytes 2359304 | tf_op jit(solution)/shard_map/ppermute | solution.py:38
  1156.7 50.8 %collective-permute-start.21 = (bf16[1536,256]{1,0:T(8,128)(2,1)S(1)}, bf16[1536,256]{1,0:T(8,128)(2,1)}, u32[]{:S(2)}, u32[]{:S(2)}) collective-permute-start(bf16[1536,256]{1,0:T(8,128)(2,1)S(1)} %get-tuple-element.336), channel_id=1, source_target_pairs={{4,0},{8,4},{12,8},{16,12},{20,16},{24,20},{28,24},{5,1},{9,5},{13... | collective-permute-start | bytes 2359304 | tf_op jit(solution)/shard_map/ppermute | solution.py:38
  1167.6 55.3 %collective-permute-start.22 = (bf16[1536,256]{1,0:T(8,128)(2,1)}, bf16[1536,256]{1,0:T(8,128)(2,1)}, u32[]{:S(2)}, u32[]{:S(2)}) collective-permute-start(bf16[1536,256]{1,0:T(8,128)(2,1)} %get-tuple-element.337), channel_id=1, source_target_pairs={{0,4},{4,8},{8,12},{12,16},{16,20},{20,24},{24,28},{1,5},{5,9},{9,... | collective-permute-start | bytes 2359304 | tf_op jit(solution)/shard_map/ppermute | solution.py:38
  1173.1 49.8 %collective-permute-start.23 = (bf16[1536,256]{1,0:T(8,128)(2,1)}, bf16[1536,256]{1,0:T(8,128)(2,1)}, u32[]{:S(2)}, u32[]{:S(2)}) collective-permute-start(bf16[1536,256]{1,0:T(8,128)(2,1)} %get-tuple-element.338), channel_id=1, source_target_pairs={{4,0},{8,4},{12,8},{16,12},{20,16},{24,20},{28,24},{5,1},{9,5},{13... | collective-permute-start | bytes 2359304 | tf_op jit(solution)/shard_map/ppermute | solution.py:38
  1174.7 50.4 %copy-start.34 = (bf16[3,512,256]{2,1,0:T(8,128)(2,1)}, bf16[3,512,256]{2,1,0:T(8,128)(2,1)S(1)}, u32[]{:S(2)}) copy-start(bf16[3,512,256]{2,1,0:T(8,128)(2,1)S(1)} %copy.212) | copy-start | bytes 2359300
  1174.7 51.3 %copy-start.28 = (bf16[1024,256,6]{0,1,2:T(8,128)(2,1)S(1)}, bf16[1024,256,6]{0,1,2:T(8,128)(2,1)}, u32[]{:S(2)}) copy-start(bf16[1024,256,6]{0,1,2:T(8,128)(2,1)} %copy-done.27) | copy-start | bytes 9437188
  1229.9 134.0 %reduce-scatter.18.cloned.1.call-start = ((), (), s32[]{:S(2)}) async-start(), calls=%async_computation.16 | async-start | bytes 3932160 | tf_op jit(solution)/shard_map/reduce_scatter | solution.py:101
  1276.8 13.1 collective-permute-start.27
  1280.2 9.7 collective-permute-start.26
  1284.0 8.3 collective-permute-start.25
  1288.6 5.9 collective-permute-start.24
  1303.1 6.5 collective-permute-start.28
  1308.2 5.6 collective-permute-start.29
  1326.4 265.7 %reduce-scatter.14.cloned.1.call-start = ((), (), s32[]{:S(2)}) async-start(), calls=%async_computation.13 | async-start | bytes 3932160 | tf_op jit(solution)/shard_map/reduce_scatter | solution.py:101
  1331.2 272.8 %reduce-scatter.24.cloned.1.call-start = ((), (), s32[]{:S(2)}) async-start(), calls=%async_computation.19 | async-start | bytes 3538944
  1356.1 250.4 %reduce-scatter.26.cloned.1.call-start = ((), (), s32[]{:S(2)}) async-start(), calls=%async_computation.20 | async-start | bytes 1179648
  1374.2 19.7 %collective-permute-start.33 = (f32[16,8]{0,1:T(8,128)S(1)}, f32[16,8]{0,1:T(8,128)S(1)}, u32[]{:S(2)}, u32[]{:S(2)}) collective-permute-start(f32[16,8]{0,1:T(8,128)S(1)} %fusion.144), channel_id=1, source_target_pairs={{0,4},{4,8},{8,12},{12,16},{16,20},{20,24},{24,28},{1,5},{5,9},{9,... | collective-permute-start | bytes 1544 | tf_op jit(solution)/shard_map/ppermute | solution.py:38
  1377.6 16.3 collective-permute-start.32
  1388.0 10.9 collective-permute-start.31
  1392.6 6.3 collective-permute-start.30
  1407.2 12.0 collective-permute-start.34
  1412.2 7.0 collective-permute-start.35
  1419.1 189.2 %reduce-scatter.20.cloned.1.call-start = ((), (), s32[]{:S(2)}) async-start(), calls=%async_computation.17 | async-start | bytes 3932160 | tf_op jit(solution)/shard_map/reduce_scatter | solution.py:101
  1433.1 324.0 %reduce-scatter.22.cloned.1.call-start = ((), (), s32[]{:S(2)}) async-start(), calls=%async_computation.18 | async-start | bytes 10616832
  1617.5 57.9 %collective-permute-start.39 = (f32[16,8]{0,1:T(8,128)S(1)}, f32[16,8]{0,1:T(8,128)S(1)}, u32[]{:S(2)}, u32[]{:S(2)}) collective-permute-start(f32[16,8]{0,1:T(8,128)S(1)} %fusion.140), channel_id=1, source_target_pairs={{0,4},{4,8},{8,12},{12,16},{16,20},{20,24},{24,28},{1,5},{5,9},{9,... | collective-permute-start | bytes 1544 | tf_op jit(solution)/shard_map/ppermute | solution.py:38
  1623.9 51.6 %collective-permute-start.38 = (f32[16,8]{0,1:T(8,128)S(1)}, f32[16,8]{0,1:T(8,128)S(1)}, u32[]{:S(2)}, u32[]{:S(2)}) collective-permute-start(f32[16,8]{0,1:T(8,128)S(1)} %fusion.140), channel_id=1, source_target_pairs={{4,0},{8,4},{12,8},{16,12},{20,16},{24,20},{28,24},{5,1},{9,5},{13... | collective-permute-start | bytes 1544 | tf_op jit(solution)/shard_map/ppermute | solution.py:38
  1628.9 48.9 %collective-permute-start.37 = (f32[16,8]{0,1:T(8,128)S(1)}, f32[16,8]{0,1:T(8,128)S(1)}, u32[]{:S(2)}, u32[]{:S(2)}) collective-permute-start(f32[16,8]{0,1:T(8,128)S(1)} %fusion.142), channel_id=1, source_target_pairs={{0,4},{4,8},{8,12},{12,16},{16,20},{20,24},{24,28},{1,5},{5,9},{9,... | collective-permute-start | bytes 1544 | tf_op jit(solution)/shard_map/ppermute | solution.py:38
  1633.8 44.1 %collective-permute-start.36 = (f32[16,8]{0,1:T(8,128)S(1)}, f32[16,8]{0,1:T(8,128)S(1)}, u32[]{:S(2)}, u32[]{:S(2)}) collective-permute-start(f32[16,8]{0,1:T(8,128)S(1)} %fusion.142), channel_id=1, source_target_pairs={{4,0},{8,4},{12,8},{16,12},{20,16},{24,20},{28,24},{5,1},{9,5},{13... | collective-permute-start | bytes 1544 | tf_op jit(solution)/shard_map/ppermute | solution.py:38
  (74 other events, 800.7 us)
Sparse Core Ops, SparseCore 0:
  45.4 43.4 all-gather.11
  91.0 28.4 all-gather.7
  121.7 138.0 all-gather.9
  362.3 30.0 all-gather.13
  394.4 60.7 all-gather.17
  456.6 27.4 all-gather.15
  485.7 28.9 all-gather.19
  1230.0 40.4 reduce-scatter.15
  1326.5 37.3 reduce-scatter.17
  1366.3 37.9 reduce-scatter.13
  1408.3 74.3 reduce-scatter.23
  1486.3 62.6 reduce-scatter.25
  1551.5 36.9 reduce-scatter.19
  1592.4 164.6 reduce-scatter.21
where the time goes:
time: 1780 us; the launch traced here: 1770 us
  matrix products  495 us (28%)
  waiting for transfers between devices  418 us (23%)
  local copies, waits for them, and re-layouts  368 us (21%)
  other arithmetic  311 us (17%)
  starting transfers between devices  118 us (7%)
  blocking collectives  40.3 us (2%)
    all_gather x1, waiting for transfers between devices, local(): lax.all_gather(kernels, 'pix', axis=0, tiled=True)  116 us
    dot_general x6, matrix products, scores_block(): jnp.einsum('qhd,khd->hqk', query_block, keys_all, preferred_element_type=...  101 us
    convert_element_type x3, other arithmetic, backward_block(): grad_scores = (prob_full * (grad_probs - row_dot)).astype(jnp.bfloat16)  95.3 us
    ppermute x32, starting transfers between devices, passed_along(): return lax.ppermute(value, axis, pairs)  92.2 us
    dot_general x3, matrix products, backward_block(): jnp.einsum('qhd,khd->hqk', grad_block, values_all, preferred_element_type...  89.7 us
    ppermute x32, waiting for transfers between devices, passed_along(): return lax.ppermute(value, axis, pairs)  86.7 us
    all_gather x4, waiting for transfers between devices, all_channels(): return lax.all_gather(values, 'ch', axis=1, tiled=True)  79.7 us
    dot_general x2, local copies, waits for them, and re-layouts, conv_backward(): jnp.einsum('tk,tc->kc', columns, grad_out, preferred_element_type=jnp.flo...  73.4 us
  transfers between devices with their start and end apart: 54, of which 23 were waited for; matrix products, arithmetic and copies ran while one was open for 25% of the time, Pallas kernels for 0%

commit v1 on v0

v1 whole, which is shorter than its diff:
```python
import functools

import jax
import jax.numpy as jnp
from jax import lax
from jax.experimental import pallas as pl
from jax.experimental.pallas import tpu as pltpu
from jax.sharding import PartitionSpec as P

HEAD_DIM = 64
W = 32
CROP_ROWS = 32
CTX = 4
GSIZE = 32
HALO = (CROP_ROWS - 1) * W
QB = 256
KB = 256

HIGHEST = lax.Precision.HIGHEST
EPSILON = 1e-05
NEGATIVE = -1e30
BF = jnp.bfloat16
F32 = jnp.float32
VMEM_LIMIT = 58 * 1024 * 1024


def dot(left, right, dims):
    return lax.dot_general(left, right, (dims, ((), ())), preferred_element_type=F32)


NN = ((1,), (0,))
NT = ((1,), (1,))
TN = ((0,), (0,))


def params(**more):
    return pltpu.CompilerParams(vmem_limit_bytes=VMEM_LIMIT, **more)


def cost(flops, moved, exps=0):
    return pl.CostEstimate(flops=flops, bytes_accessed=moved, transcendentals=exps)


WITH_PREV, WITH_NEXT, INVERSE = 3, 4, 5
EDGE = 40


def exact(left, right):
    return lax.dot_general(
        left, right, (NN, ((), ())), precision=HIGHEST, preferred_element_type=F32
    )


def write_totals(first, second, same_ref, totals_ref, next_ref, prev_ref):
    lines, width = first.shape
    row = lax.broadcasted_iota(jnp.int32, (width, width), 0) // GSIZE
    column = lax.broadcasted_iota(jnp.int32, (width, width), 1) // GSIZE
    group = (row == column).astype(F32)
    for place, value in ((0, first), (1, second)):
        total = exact(same_ref[...], exact(value, group))
        totals_ref[place] = total
        next_ref[W + place : W + place + 1, :] = total[lines - 1 : lines, :]
        prev_ref[W + place : W + place + 1, :] = total[0:1, :]
    for target in (next_ref, prev_ref):
        target[W + 2 : EDGE, :] = jnp.zeros((EDGE - W - 2, width), F32)


def crop_means(totals_ref, before_ref, after_ref, rows_ref):
    found = []
    for place in range(2):
        line = slice(W + place, W + place + 1)
        total = totals_ref[place] + rows_ref[WITH_PREV] * before_ref[line, :]
        total = total + rows_ref[WITH_NEXT] * after_ref[line, :]
        found.append(total * rows_ref[INVERSE])
    return found


def square_sums(value_ref, sums_ref):
    lines = sums_ref.shape[1]

    def one(line, carry):
        cells = value_ref[pl.ds(pl.multiple_of(line * W, W), W), :]
        sums_ref[0, pl.ds(line, 1), :] = jnp.sum(cells, axis=0, keepdims=True)
        sums_ref[1, pl.ds(line, 1), :] = jnp.sum(cells * cells, axis=0, keepdims=True)
        return carry

    lax.fori_loop(0, lines, one, 0, unroll=4)


def stats_shapes(lines, width):
    return (
        jax.ShapeDtypeStruct((2, lines, width), F32),
        jax.ShapeDtypeStruct((EDGE, width), F32),
        jax.ShapeDtypeStruct((EDGE, width), F32),
    )


def stats_body(value_ref, same_ref, totals_ref, next_ref, prev_ref, sums_ref):
    tokens = value_ref.shape[0]
    square_sums(value_ref, sums_ref)
    write_totals(sums_ref[0], sums_ref[1], same_ref, totals_ref, next_ref, prev_ref)
    next_ref[0:W, :] = value_ref[tokens - W :, :]
    prev_ref[0:W, :] = value_ref[0:W, :]


def stats(value, same):
    tokens, width = value.shape
    return pl.pallas_call(
        stats_body,
        out_shape=stats_shapes(tokens // W, width),
        scratch_shapes=[pltpu.VMEM((2, tokens // W, width), F32)],
        compiler_params=params(),
        cost_estimate=cost(tokens * width * 4, tokens * width * 4),
        name="stats",
    )(value, same)


def norm_body(active, wide, *refs):
    value_ref, totals_ref, before_ref, after_ref, rows_ref, gain_ref, shift_ref = refs[:7]
    refs = refs[7:]
    if active == "mixed":
        growth_ref, add_ref = refs[:2]
        refs = refs[2:]
    out_ref, stats_ref, scale_ref, bias_ref = refs
    lines = totals_ref.shape[1]
    mean, square = crop_means(totals_ref, before_ref, after_ref, rows_ref)
    scale = lax.rsqrt(square - mean * mean + EPSILON)
    stats_ref[0] = mean
    stats_ref[1] = scale
    if active == "mixed":
        scale_ref[...] = scale * gain_ref[...] * growth_ref[...]
        bias_ref[...] = shift_ref[...] * growth_ref[...] + add_ref[...]
    else:
        scale_ref[...] = scale * gain_ref[...]
        bias_ref[...] = jnp.broadcast_to(shift_ref[...], bias_ref.shape)

    def cells_of(cells, line):
        here = pl.ds(line, 1)
        value = (cells - stats_ref[0, here, :]) * scale_ref[here, :] + bias_ref[here, :]
        if active is not None:
            value = value / (1.0 + jnp.exp(-value))
        return value.astype(BF)

    base = W if wide else 0

    def one(line, carry):
        start = pl.multiple_of(line * W, W)
        out_ref[pl.ds(start + base, W), :] = cells_of(value_ref[pl.ds(start, W), :], line)
        return carry

    lax.fori_loop(0, lines, one, 0, unroll=4)
    if wide:
        out_ref[0:W, :] = cells_of(before_ref[0:W, :], 0)
        out_ref[(lines + 1) * W :, :] = cells_of(after_ref[0:W, :], lines - 1)


def norm(value, totals, before, after, rows, gain, shift, mixed=None, active="plain", wide=True):
    tokens, width = value.shape
    lines = tokens // W
    operands = [value, totals, before, after, rows, gain, shift]
    if mixed is not None:
        operands += list(mixed)
        active = "mixed"
    return pl.pallas_call(
        functools.partial(norm_body, active, wide),
        out_shape=(
            jax.ShapeDtypeStruct((tokens + (2 * W if wide else 0), width), BF),
            jax.ShapeDtypeStruct((2, lines, width), F32),
        ),
        scratch_shapes=[pltpu.VMEM((lines, width), F32), pltpu.VMEM((lines, width), F32)],
        compiler_params=params(),
        cost_estimate=cost(tokens * width * 12, tokens * width * 6, tokens * width),
        name="norm",
    )(*operands)


def sums_body(count, active, *refs):
    parts = refs[:count]
    value_ref, stats_ref, gain_ref, shift_ref, same_ref = refs[count : count + 5]
    refs = refs[count + 5 :]
    if active == "mixed":
        growth_ref, add_ref = refs[:2]
        refs = refs[2:]
    grad_ref, raw_ref, totals_ref, next_ref, prev_ref = refs
    tokens, width = value_ref.shape
    lines = tokens // W

    def one(line, carry):
        here = pl.ds(line, 1)
        cells = pl.ds(pl.multiple_of(line * W, W), W)
        grad = parts[0][cells, :].astype(F32)
        for part in parts[1:]:
            grad = grad + part[cells, :].astype(F32)
        normal = (value_ref[cells, :] - stats_ref[0, here, :]) * stats_ref[1, here, :]
        if active is not None:
            inner = normal * gain_ref[...] + shift_ref[...]
            if active == "mixed":
                inner = inner * growth_ref[here, :] + add_ref[here, :]
            sigmoid = 1.0 / (1.0 + jnp.exp(-inner))
            grad = grad * sigmoid * (1.0 + inner * (1.0 - sigmoid))
        raw_ref[0, here, :] = jnp.sum(grad, axis=0, keepdims=True)
        raw_ref[1, here, :] = jnp.sum(grad * normal, axis=0, keepdims=True)
        if active == "mixed":
            grad = grad * growth_ref[here, :]
        grad_ref[cells, :] = grad
        return carry

    lax.fori_loop(0, lines, one, 0, unroll=4)
    first, second = raw_ref[0] * gain_ref[...], raw_ref[1] * gain_ref[...]
    if active == "mixed":
        first, second = first * growth_ref[...], second * growth_ref[...]
    write_totals(first, second, same_ref, totals_ref, next_ref, prev_ref)
    next_ref[0:W, :] = grad_ref[tokens - W :, :]
    prev_ref[0:W, :] = grad_ref[0:W, :]


def gradient_sums(parts, value, stats_found, gain, shift, same, mixed=None, active=None):
    tokens, width = value.shape
    operands = [*parts, value, stats_found, gain, shift, same]
    if mixed is not None:
        operands += list(mixed)
        active = "mixed"
    return pl.pallas_call(
        functools.partial(sums_body, len(parts), active),
        out_shape=(
            jax.ShapeDtypeStruct((tokens, width), F32),
            jax.ShapeDtypeStruct((2, tokens // W, width), F32),
        )
        + stats_shapes(tokens // W, width),
        compiler_params=params(),
        cost_estimate=cost(tokens * width * 20, tokens * width * 14, tokens * width),
        name="gradient_sums",
    )(*operands)


def norm_gradient(grad, value, line, stats_ref, mean_ref, gain_ref):
    here = pl.ds(line, 1)
    scale = stats_ref[1, here, :]
    normal = (value - stats_ref[0, here, :]) * scale
    return scale * (grad * gain_ref[...] - mean_ref[0, here, :] - normal * mean_ref[1, here, :])


def taps_body(based, ids, *refs):
    grad_ref, value_ref, value_before, value_after, stats_ref, totals_ref = refs[:6]
    before_ref, after_ref, rows_ref, gain_ref = refs[6:10]
    refs = refs[10:]
    if based:
        base_ref, base_before, base_after = refs[:3]
        refs = refs[3:]
    map_ref = refs[0]
    refs = refs[1:]
    if based:
        full_ref = refs[0]
        refs = refs[1:]
    taps_ref = refs[0]
    refs = refs[1:]
    same_core, other_core, wide_ref, mean_ref = refs
    tokens, width = grad_ref.shape
    lines = tokens // W
    padded = tokens + 2 * W

    @pl.when(pl.program_id(0) == 0)
    def _():
        mean_ref[0], mean_ref[1] = crop_means(totals_ref, before_ref, after_ref, rows_ref)

        def one(line, carry):
            start = pl.multiple_of(line * W, W)
            cells = pl.ds(start, W)
            found = norm_gradient(
                grad_ref[cells, :], value_ref[cells, :], line, stats_ref, mean_ref, gain_ref
            )
            if based:
                found = found + base_ref[cells, :].astype(F32)
                full_ref[cells, :] = found
            wide_ref[pl.ds(start + W, W), :] = found
            return carry

        lax.fori_loop(0, lines, one, 0, unroll=4)
        for edge_ref, edge_value, line, start in (
            (before_ref, value_before, 0, 0),
            (after_ref, value_after, lines - 1, padded - W),
        ):
            found = norm_gradient(
                edge_ref[0:W, :], edge_value[0:W, :], line, stats_ref, mean_ref, gain_ref
            )
            if based:
                found = found + (base_before if line == 0 else base_after)[0:W, :].astype(F32)
            wide_ref[start : start + W, :] = found

        column = lax.broadcasted_iota(jnp.int32, (W, width), 0)

        def spread_row(line, carry):
            start = pl.multiple_of(line * W, W)
            target = pl.ds(start, W)
            for up in range(3):
                mask = rows_ref[up, pl.ds(line, 1), :]
                values = wide_ref[pl.ds(start + up * W, W), :] * mask
                left = jnp.where(column > 0, pltpu.roll(values, 1, 0), 0.0)
                right = jnp.where(column < W - 1, pltpu.roll(values, W - 1, 0), 0.0)
                for side, moved in enumerate((left, values, right)):
                    tap = 8 - (3 * up + side)
                    taps_ref[target, tap * width : (tap + 1) * width] = moved.astype(BF)
            return carry

        lax.fori_loop(0, lines, spread_row, 0, unroll=2)

    core = ids[ids.shape[0] - 1]
    write_products(taps_ref, map_ref, core, same_core, other_core)


def write_products(grad_ref, map_ref, core, same_core, other_core):
    tokens, width = same_core.shape[1:]
    for place, target in ((core, same_core), (1 - core, other_core)):
        rows = pl.ds(pl.multiple_of(place * width, width), width)
        for start in range(0, tokens, 512):
            here = slice(start, start + 512)
            target[0, here, :] = dot(grad_ref[here, :], map_ref[rows, :], NT).astype(BF)


def gradient_taps(
    grad, value, beside, stats_found, totals, before, after, rows, gain, base, ids, maps
):
    tokens, width = grad.shape
    lines = tokens // W
    count = ids.shape[0] - 1
    wide = 9 * width
    operands = [grad, value, *beside, stats_found, totals, before, after, rows, gain]
    if base is not None:
        operands += list(base)
    whole = lambda array: pl.BlockSpec(array.shape, lambda step, ids: (0,) * len(array.shape))
    in_specs = [whole(operand) for operand in operands]
    operands.append(maps)
    in_specs.append(pl.BlockSpec((2 * width, wide), lambda step, ids: (ids[step], 0)))
    taps_shape = jax.ShapeDtypeStruct((tokens, wide), BF)
    shapes, out_specs = [taps_shape], [whole(taps_shape)]
    if base is not None:
        full_shape = jax.ShapeDtypeStruct((tokens, width), F32)
        shapes, out_specs = [full_shape] + shapes, [whole(full_shape)] + out_specs
    shapes += [jax.ShapeDtypeStruct((count, tokens, width), BF)] * 2
    out_specs += [pl.BlockSpec((1, tokens, width), lambda step, ids: (step, 0, 0))] * 2
    return pl.pallas_call(
        functools.partial(taps_body, base is not None),
        out_shape=shapes,
        grid_spec=pltpu.PrefetchScalarGridSpec(
            num_scalar_prefetch=1,
            grid=(count,),
            in_specs=in_specs,
            out_specs=out_specs,
            scratch_shapes=[
                pltpu.VMEM((tokens + 2 * W, width), F32),
                pltpu.VMEM((2, lines, width), F32),
            ],
        ),
        compiler_params=params(),
        cost_estimate=cost(2 * tokens * count * width * wide, tokens * wide * 4),
        name="gradient_taps",
    )(ids, *operands)


def last_body(grad_ref, value_ref, stats_ref, totals_ref, before_ref, after_ref, rows_ref, gain_ref,
              base_ref, out_ref, mean_ref):
    mean_ref[0], mean_ref[1] = crop_means(totals_ref, before_ref, after_ref, rows_ref)

    def one(line, carry):
        cells = pl.ds(pl.multiple_of(line * W, W), W)
        out_ref[cells, :] = base_ref[cells, :] + norm_gradient(
            grad_ref[cells, :], value_ref[cells, :], line, stats_ref, mean_ref, gain_ref
        )
        return carry

    lax.fori_loop(0, grad_ref.shape[0] // W, one, 0, unroll=4)


def last_gradient(grad, value, stats_found, totals, before, after, rows, gain, base):
    tokens, width = grad.shape
    return pl.pallas_call(
        last_body,
        out_shape=jax.ShapeDtypeStruct((tokens, width), F32),
        scratch_shapes=[pltpu.VMEM((2, tokens // W, width), F32)],
        compiler_params=params(),
        cost_estimate=cost(tokens * width * 10, tokens * width * 16),
        name="last_gradient",
    )(grad, value, stats_found, totals, before, after, rows, gain, base)


def conv_body(prior, resid, ids, *refs):
    own_ref, mate_ref, kernel_ref, rows_ref = refs[:4]
    refs = refs[4:]
    prior_ref = refs[0] if prior else None
    refs = refs[1:] if prior else refs
    if resid:
        input_ref, bias_ref = refs[:2]
        refs = refs[2:]
    if resid is not None:
        same_ref, out_ref, totals_ref, next_ref, prev_ref, both_ref, sums_ref = refs
    else:
        out_ref, both_ref = refs
    tokens, width = out_ref.shape
    first = ids[1]
    for place, block in ((first, own_ref), (1 - first, mate_ref)):
        both_ref[:, pl.ds(pl.multiple_of(place * width, width), width)] = block[...]
    chunk = 256
    lines = chunk // W
    for start in range(0, tokens, chunk):
        here = slice(start, start + chunk)
        sides = [None] * 3
        for up in range(3):
            taps = kernel_ref[:, up * 3 * width : (up + 1) * 3 * width]
            part = dot(both_ref[up * W + start : up * W + start + chunk, :], taps, NN)
            part = part.reshape(lines, W, 3 * width)
            mask = rows_ref[up, start // W : start // W + lines, :][:, None, :]
            for side in range(3):
                piece = part[:, :, side * width : (side + 1) * width]
                piece = piece if up == 1 else piece * mask
                sides[side] = piece if sides[side] is None else sides[side] + piece
        sides = [piece.reshape(chunk, width) for piece in sides]
        column = lax.broadcasted_iota(jnp.int32, (chunk, width), 0) % W
        left = jnp.where(column > 0, pltpu.roll(sides[0], 1, 0), 0.0)
        right = jnp.where(column < W - 1, pltpu.roll(sides[2], chunk - 1, 0), 0.0)
        total = sides[1] + left + right
        if prior:
            total += prior_ref[here, :]
        if resid:
            total += input_ref[here, :] + bias_ref[...]
        out_ref[here, :] = total
    if resid is not None:
        square_sums(out_ref, sums_ref)
        write_totals(sums_ref[0], sums_ref[1], same_ref, totals_ref, next_ref, prev_ref)
        next_ref[0:W, :] = out_ref[tokens - W :, :]
        prev_ref[0:W, :] = out_ref[0:W, :]


def conv_pair(own, mate, ids, kernel, rows, prior=None, resid=None, same=None):
    padded, width = own.shape
    tokens = padded - 2 * W
    lines = tokens // W
    wide = 9 * width

    def whole(array):
        return pl.BlockSpec(array.shape, lambda step, ids: (0,) * len(array.shape))

    operands = [own, mate, kernel, rows]
    in_specs = [whole(own), whole(mate)]
    in_specs += [pl.BlockSpec((2 * width, wide), lambda step, ids: (ids[0], 0)), whole(rows)]
    for extra in ([prior] if prior is not None else []) + list(resid or ()):
        operands.append(extra)
        in_specs.append(whole(extra))
    shapes = [jax.ShapeDtypeStruct((tokens, width), F32)]
    scratch = [pltpu.VMEM((padded, 2 * width), BF)]
    if resid is not None:
        operands.append(same)
        in_specs.append(whole(same))
        shapes += list(stats_shapes(lines, width))
        scratch.append(pltpu.VMEM((2, lines, width), F32))
    found = pl.pallas_call(
        functools.partial(conv_body, prior is not None, None if resid is None else len(resid)),
        out_shape=shapes,
        grid_spec=pltpu.PrefetchScalarGridSpec(
            num_scalar_prefetch=1,
            grid=(1,),
            in_specs=in_specs,
            out_specs=[whole(shape) for shape in shapes],
            scratch_shapes=scratch,
        ),
        compiler_params=params(),
        cost_estimate=cost(4 * tokens * width * wide, 4 * width * wide + tokens * width * 12),
        name="conv_pair",
    )(ids, *operands)
    return found if resid is not None else found[0]


def convolve(blocks, far, ids, kernel, rows, same, resid):
    pairs = lax.axis_size("ch") // 2
    found = None
    for pair in range(pairs):
        place = jnp.stack([ids[2 * pair] // 2, ids[2 * pair] % 2])
        final = pair == pairs - 1
        found = conv_pair(
            blocks[2 * pair], blocks[2 * pair + 1], place, kernel, rows, found,
            resid if final else None, same,
        )
        if pair == 0 and far:
            found, *far = tie(found, *far)
            blocks = blocks + with_mates(far)
    return blocks, found


def project_body(count, width, ids, *refs):
    blocks = refs[:count]
    map_ref, out_ref, all_ref = refs[count:]

    @pl.when(pl.program_id(0) == 0)
    def _():
        for place in range(count):
            first = pl.multiple_of(ids[place] * width, width)
            all_ref[:, pl.ds(first, width)] = blocks[place][...]

    for start in range(0, out_ref.shape[0], 512):
        here = slice(start, start + 512)
        out_ref[here, :] = dot(all_ref[here, :], map_ref[...], NN).astype(out_ref.dtype)


def project(blocks, ids, maps, first, wide):
    count = len(blocks)
    tokens, width = blocks[0].shape
    depth = maps.shape[0]
    start = first // width
    return pl.pallas_call(
        functools.partial(project_body, count, width),
        out_shape=jax.ShapeDtypeStruct((tokens, wide), BF),
        grid_spec=pltpu.PrefetchScalarGridSpec(
            num_scalar_prefetch=1,
            grid=(wide // width,),
            in_specs=[pl.BlockSpec((tokens, width), lambda step, ids: (0, 0))] * count
            + [pl.BlockSpec((depth, width), lambda step, ids: (0, start + step))],
            out_specs=pl.BlockSpec((tokens, width), lambda step, ids: (0, step)),
            scratch_shapes=[pltpu.VMEM((tokens, depth), BF)],
        ),
        compiler_params=params(),
        cost_estimate=cost(2 * tokens * depth * wide, (tokens + depth) * wide * 2),
        name="project",
    )(ids, *blocks, maps)


def spread_body(ids, grad_ref, *refs):
    core = ids[ids.shape[0] - 1]
    write_products(grad_ref, refs[0], core, *refs[1:])


def spread(grad, ids, maps, first=0):
    tokens, wide = grad.shape
    count = ids.shape[0] - 1
    width = maps.shape[0] // lax.axis_size("ch")
    start = first // wide
    return pl.pallas_call(
        spread_body,
        out_shape=[jax.ShapeDtypeStruct((count, tokens, width), BF)] * 2,
        grid_spec=pltpu.PrefetchScalarGridSpec(
            num_scalar_prefetch=1,
            grid=(count,),
            in_specs=[
                pl.BlockSpec((tokens, wide), lambda step, ids: (0, 0)),
                pl.BlockSpec((2 * width, wide), lambda step, ids: (ids[step], start)),
            ],
            out_specs=[pl.BlockSpec((1, tokens, width), lambda step, ids: (step, 0, 0))] * 2,
        ),
        compiler_params=params(),
        cost_estimate=cost(4 * tokens * count * width * wide, (tokens + count * width) * wide * 2),
        name="spread",
    )(ids, grad, maps)


def outer_body(count, shift, ids, *refs):
    blocks = refs[:count]
    grad_ref, out_ref, turned_ref = refs[count:]
    tokens = grad_ref.shape[0]
    width = blocks[0].shape[1]

    @pl.when(pl.program_id(0) == 0)
    def _():
        for place in range(count):
            first = pl.multiple_of(ids[place] * width, width)
            turned_ref[pl.ds(first, width), :] = blocks[place][shift : shift + tokens, :].T

    depth = turned_ref.shape[0]
    for start in range(0, depth, 512):
        here = slice(start, start + 512)
        out_ref[here, :] = dot(turned_ref[here, :], grad_ref[...], NN).astype(BF)


def outer(blocks, ids, grad, shift=0, columns=None):
    count = len(blocks)
    tokens = grad.shape[0]
    first, wide = columns or (0, grad.shape[1])
    padded, width = blocks[0].shape
    depth = count * width
    tile = min(wide, 3 * width)
    before = first // tile
    return pl.pallas_call(
        functools.partial(outer_body, count, shift),
        out_shape=jax.ShapeDtypeStruct((depth, wide), BF),
        grid_spec=pltpu.PrefetchScalarGridSpec(
            num_scalar_prefetch=1,
            grid=(wide // tile,),
            in_specs=[pl.BlockSpec((padded, width), lambda step, ids: (0, 0))] * count
            + [pl.BlockSpec((tokens, tile), lambda step, ids: (0, before + step))],
            out_specs=pl.BlockSpec((depth, tile), lambda step, ids: (0, step)),
            scratch_shapes=[pltpu.VMEM((depth, tokens), BF)],
        ),
        compiler_params=params(),
        cost_estimate=cost(2 * tokens * depth * wide, (tokens + depth) * wide * 2),
        name="outer",
    )(ids, *blocks, grad)


def attention_body(
    heads, starts, counts, crops, query_ref, grad_ref, low_ref, own_ref, high_ref, ckey_ref,
    cval_ref, qcrop_ref, ccrop_ref, att_ref, dquery_ref, dlow_ref, down_ref, dhigh_ref, dckey_ref,
    dcval_ref, keys, values, keys_t, values_t, dkeys, dvalues, kcrop_ref, score_ref, prob_ref,
    cscore_ref, cprob_ref, qt_ref, qn_ref, gt_ref, gn_ref, att_t, dq_t,
):
    step = pl.program_id(0)
    window, width = keys.shape
    tokens = own_ref.shape[0]

    @pl.when(step == 0)
    def _():
        def label(line, carry):
            here = pl.ds(pl.multiple_of(line * W, W), W)
            kcrop_ref[here, :] = jnp.full((W, 128), crops[line], jnp.int32)
            return carry

        lax.fori_loop(0, window // W, label, 0, unroll=2)
        for place, target, turned in ((0, keys, keys_t), (1, values, values_t)):
            part = slice(place * width, (place + 1) * width)
            target[0:HALO, :] = low_ref[:, part]
            shifted = slice((place + 1) * width, (place + 2) * width)
            target[HALO : HALO + tokens, :] = own_ref[:, shifted]
            target[HALO + tokens : 2 * HALO + tokens, :] = high_ref[:, part]
            rest = window - 2 * HALO - tokens
            target[2 * HALO + tokens :, :] = jnp.zeros((rest, width), BF)
            for place in range(0, window, KB):
                turned[:, place : place + KB] = target[place : place + KB, :].T
        dkeys[...] = jnp.zeros_like(dkeys)
        dvalues[...] = jnp.zeros_like(dvalues)
        dckey_ref[...] = jnp.zeros_like(dckey_ref)
        dcval_ref[...] = jnp.zeros_like(dcval_ref)

    first = starts[step]
    blocks = counts[step]
    query = (query_ref[...].astype(F32) * (HEAD_DIM**-0.5)).astype(BF)
    query_t = query.T
    grad_t = grad_ref[...].T
    lane = lax.broadcasted_iota(jnp.int32, (QB, width), 1)
    for head in range(heads):
        mine = slice(head * HEAD_DIM, (head + 1) * HEAD_DIM)
        qt_ref[head] = jnp.zeros((width, QB), BF)
        qt_ref[head, mine, :] = query_t[mine, :]
        gt_ref[head] = jnp.zeros((width, QB), BF)
        in_head = (lane >= head * HEAD_DIM) & (lane < (head + 1) * HEAD_DIM)
        qn_ref[head] = jnp.where(in_head, query, jnp.zeros_like(query))
    crop_row = qcrop_ref[...].reshape(1, QB)
    ccrop = ccrop_ref[...]
    same_context = jnp.concatenate([ccrop] * (QB // 128), axis=1) == crop_row

    def span(block):
        return pl.ds(pl.multiple_of(first + block * KB, 128), KB)

    largest = []
    for head in range(heads):
        scores = jnp.where(same_context, dot(ckey_ref[...], qt_ref[head], NN), NEGATIVE)
        cscore_ref[head] = scores
        largest.append(jnp.max(scores.reshape(-1, 8, QB), axis=0))

    def pass_one(block, carry):
        here = span(block)
        crops = kcrop_ref[here, :]
        same = jnp.concatenate([crops] * (QB // 128), axis=1) == crop_row
        rows = keys[here, :]
        out = []
        for head in range(heads):
            scores = jnp.where(same, dot(rows, qt_ref[head], NN), NEGATIVE)
            score_ref[head, block] = scores
            out.append(jnp.maximum(carry[head], jnp.max(scores.reshape(-1, 8, QB), axis=0)))
        return tuple(out)

    largest = lax.fori_loop(0, blocks, pass_one, tuple(largest))
    largest = [jnp.max(value, axis=0, keepdims=True) for value in largest]

    sums = []
    for head in range(heads):
        mine = slice(head * HEAD_DIM, (head + 1) * HEAD_DIM)
        prob = jnp.exp(cscore_ref[head] - largest[head])
        sums.append(jnp.sum(prob.reshape(-1, 8, QB), axis=0))
        low = prob.astype(BF)
        cprob_ref[head] = low
        att_t[mine, :] = dot(cval_ref[...], low, TN)[mine, :]

    def pass_two(block, carry):
        here = span(block)
        out = []
        for head in range(heads):
            mine = slice(head * HEAD_DIM, (head + 1) * HEAD_DIM)
            prob = jnp.exp(score_ref[head, block] - largest[head])
            out.append(carry[head] + jnp.sum(prob.reshape(-1, 8, QB), axis=0))
            low = prob.astype(BF)
            prob_ref[head, block] = low
            att_t[mine, :] += dot(values_t[mine, here], low, NN)
        return tuple(out)

    sums = lax.fori_loop(0, blocks, pass_two, tuple(sums))
    offsets = []
    for head in range(heads):
        mine = slice(head * HEAD_DIM, (head + 1) * HEAD_DIM)
        inverse = 1.0 / jnp.sum(sums[head], axis=0, keepdims=True)
        attended = att_t[mine, :] * inverse
        att_t[mine, :] = attended
        scaled = grad_t[mine, :].astype(F32) * inverse
        gt_ref[head, mine, :] = scaled.astype(BF)
        offsets.append(jnp.sum(scaled * attended, axis=0, keepdims=True))
        gn_ref[head] = gt_ref[head].T
    att_ref[...] = att_t[...].T.astype(BF)

    for head in range(heads):
        mine = slice(head * HEAD_DIM, (head + 1) * HEAD_DIM)
        prob = cprob_ref[head]
        slope = dot(cval_ref[...], gt_ref[head], NN)
        dscore = (prob.astype(F32) * (slope - offsets[head])).astype(BF)
        dcval_ref[...] += dot(prob, gn_ref[head], NN)
        dckey_ref[...] += dot(dscore, qn_ref[head], NN)
        dq_t[mine, :] = dot(ckey_ref[...], dscore, TN)[mine, :]

    def pass_three(block, carry):
        here = span(block)
        rows = values[here, :]
        value_sum = None
        key_sum = None
        for head in range(heads):
            mine = slice(head * HEAD_DIM, (head + 1) * HEAD_DIM)
            prob = prob_ref[head, block]
            slope = dot(rows, gt_ref[head], NN)
            dscore = (prob.astype(F32) * (slope - offsets[head])).astype(BF)
            value_part = dot(prob, gn_ref[head], NN)
            key_part = dot(dscore, qn_ref[head], NN)
            value_sum = value_part if value_sum is None else value_sum + value_part
            key_sum = key_part if key_sum is None else key_sum + key_part
            dq_t[mine, :] += dot(keys_t[mine, here], dscore, NN)
        dvalues[here, :] += value_sum
        dkeys[here, :] += key_sum
        return carry

    lax.fori_loop(0, blocks, pass_three, 0)
    dquery_ref[...] = (dq_t[...] * (HEAD_DIM**-0.5)).T.astype(BF)

    @pl.when(step == pl.num_programs(0) - 1)
    def _():
        for place, source in ((0, dkeys), (1, dvalues)):
            part = slice(place * width, (place + 1) * width)
            dlow_ref[:, part] = source[0:HALO, :].astype(BF)
            down_ref[:, part] = source[HALO : HALO + tokens, :]
            dhigh_ref[:, part] = source[HALO + tokens : 2 * HALO + tokens, :].astype(BF)


def attend(qkv, grad, low, high, ckey, cval, tables):
    starts, counts, crops, qcrop, ccrop = tables
    tokens, width = grad.shape
    heads = width // HEAD_DIM
    window = crops.shape[0] * W
    context = ckey.shape[0]
    most = ((QB // W + 2 * (CROP_ROWS - 1)) * W + 127 + KB - 1) // KB
    q_block = pl.BlockSpec((QB, width), lambda step, *_: (step, 0))

    def whole(array):
        return pl.BlockSpec(array.shape, lambda step, *_: (0,) * len(array.shape))

    full = [low, qkv, high, ckey, cval]
    shapes = (
        jax.ShapeDtypeStruct((tokens, width), BF),
        jax.ShapeDtypeStruct((tokens, width), BF),
        jax.ShapeDtypeStruct((HALO, 2 * width), BF),
        jax.ShapeDtypeStruct((tokens, 2 * width), F32),
        jax.ShapeDtypeStruct((HALO, 2 * width), BF),
        jax.ShapeDtypeStruct((context, width), F32),
        jax.ShapeDtypeStruct((context, width), F32),
    )
    flops = 12 * tokens * 1280 * width
    return pl.pallas_call(
        functools.partial(attention_body, heads),
        out_shape=shapes,
        grid_spec=pltpu.PrefetchScalarGridSpec(
            num_scalar_prefetch=3,
            grid=(tokens // QB,),
            in_specs=[q_block, q_block]
            + [whole(array) for array in full]
            + [pl.BlockSpec((1, 1, QB), lambda step, *_: (step, 0, 0)), whole(ccrop)],
            out_specs=[q_block, q_block] + [whole(shape) for shape in shapes[2:]],
            scratch_shapes=[
                pltpu.VMEM((window, width), BF),
                pltpu.VMEM((window, width), BF),
                pltpu.VMEM((width, window), BF),
                pltpu.VMEM((width, window), BF),
                pltpu.VMEM((window, width), F32),
                pltpu.VMEM((window, width), F32),
                pltpu.VMEM((window, 128), jnp.int32),
                pltpu.VMEM((heads, most, KB, QB), F32),
                pltpu.VMEM((heads, most, KB, QB), BF),
                pltpu.VMEM((heads, context, QB), F32),
                pltpu.VMEM((heads, context, QB), BF),
                pltpu.VMEM((heads, width, QB), BF),
                pltpu.VMEM((heads, QB, width), BF),
                pltpu.VMEM((heads, width, QB), BF),
                pltpu.VMEM((heads, QB, width), BF),
                pltpu.VMEM((width, QB), F32),
                pltpu.VMEM((width, QB), F32),
            ],
        ),
        compiler_params=params(),
        cost_estimate=cost(flops // 3, 20 * tokens * width, tokens * 1280 * heads),
        name="attend",
    )(starts, counts, crops, qkv, grad, *full, qcrop, ccrop)


def along_pix(value, by):
    size = lax.axis_size("pix")
    return lax.ppermute(value, "pix", [(i, i + by) for i in range(size) if 0 <= i + by < size])


def across_pix(value, bit):
    return lax.ppermute(value, "pix", [(i, i ^ bit) for i in range(lax.axis_size("pix"))])


def pix_sum(value):
    bit = 1
    while bit < lax.axis_size("pix"):
        value = value + across_pix(value, bit)
        bit *= 2
    return value


def to_mate(value):
    return lax.ppermute(value, "ch", [(i, i ^ 1) for i in range(lax.axis_size("ch"))])


def to_chip(value, by):
    size = lax.axis_size("ch")
    return lax.ppermute(value, "ch", [(i, (i + 2 * by) % size) for i in range(size)])


def gather_rows(value):
    return lax.all_gather(value, "pix", axis=0, tiled=True)


def scatter_rows(value):
    return lax.psum_scatter(value, "pix", scatter_dimension=0, tiled=True)


def block_ids():
    size = lax.axis_size("ch")
    here = lax.axis_index("ch")
    ids = [here, here ^ 1]
    for by in range(1, size // 2):
        other = lax.rem(here + size - 2 * by, size)
        ids += [other, other ^ 1]
    return jnp.stack(ids).astype(jnp.int32)


def chip_ids():
    size = lax.axis_size("ch")
    here = lax.axis_index("ch")
    chips = [lax.rem(here // 2 + by, size // 2) for by in range(1, size // 2)]
    home = jnp.stack([here // 2, here % 2]).astype(jnp.int32)
    return home, jnp.stack(chips + [here % 2]).astype(jnp.int32)


def tie(*values):
    return lax.optimization_barrier(values)


def far_blocks(value):
    return [to_chip(value, by) for by in range(1, lax.axis_size("ch") // 2)]


def with_mates(blocks):
    found = []
    for block in blocks:
        found += [block, to_mate(block)]
    return found


def gather_blocks(value):
    far = far_blocks(value)
    return [value, to_mate(value)] + with_mates(far)


def chip_sums(parts):
    own, mate = parts
    return [
        (own[i].astype(F32) + to_mate(mate[i]).astype(F32)).astype(BF) for i in range(own.shape[0])
    ]


def sent_sums(sums):
    return [to_chip(piece, by + 1) for by, piece in enumerate(sums)]


def home_parts(parts):
    return [parts[0][0], to_mate(parts[1][0])]


def unpack_rows(packed):
    lines = packed.shape[0]
    width = packed.shape[1] // W
    return packed.reshape(lines, width, W).transpose(0, 2, 1).reshape(lines * W, width)


def pack_rows(cells):
    width = cells.shape[1]
    lines = cells.shape[0] // W
    return cells.reshape(lines, W, width).transpose(0, 2, 1).reshape(lines, width * W)


def small(left, right):
    return jnp.dot(left, right, precision=HIGHEST)


def turned(left, right):
    return lax.dot_general(left, right, (TN, ((), ())), precision=HIGHEST)


def beside_rows(messages):
    to_next, to_prev = messages
    return along_pix(to_next, 1), along_pix(to_prev, -1)


def local(
    pixels,
    cotangent,
    crop_rows,
    condition,
    context,
    kernels,
    attention,
    embedding,
    gains,
    shifts,
    offsets,
):
    lines = pixels.shape[0]
    width = pixels.shape[1] // W
    tokens = lines * W
    depth_here = kernels.shape[0]
    crop_count = crop_rows.shape[0]
    place = lax.axis_index("pix")
    kernel_local = (
        kernels.reshape(depth_here, width, 18).transpose(0, 2, 1).reshape(depth_here, 18 * width)
    )
    maps_local = (
        attention.reshape(depth_here, width, 6).transpose(0, 2, 1).reshape(depth_here, 6 * width)
    )
    kernel_one = gather_rows(kernel_local[:, : 9 * width])
    two_local = kernel_local[:, 9 * width :]
    four = jnp.concatenate([maps_local[:, : 3 * width], maps_local[:, 5 * width :]], axis=1)
    embedding_local = (
        embedding.reshape(depth_here, width, 2).transpose(0, 2, 1).reshape(depth_here, 2 * width)
    )
    context_flat = context.reshape(-1, context.shape[2])
    own_rows = place * depth_here
    context_own = lax.dynamic_slice_in_dim(context_flat, own_rows, depth_here, axis=1)
    condition_own = lax.dynamic_slice_in_dim(condition, own_rows, depth_here, axis=1)
    summed = pix_sum(
        jnp.concatenate(
            [
                dot(condition_own, embedding_local, NN),
                dot(context_own, maps_local[:, 3 * width : 5 * width], NN),
            ],
            axis=0,
        )
    )
    embed_terms = summed[:crop_count]
    ckey = summed[crop_count:, :width].astype(BF)
    cval = summed[crop_count:, width:].astype(BF)
    bounds = jnp.cumsum(crop_rows)
    line = place * lines + jnp.arange(-(CROP_ROWS - 1), lines + CROP_ROWS - 1, dtype=jnp.int32)
    found = jnp.sum((line[:, None] >= bounds[None, :]).astype(jnp.int32), axis=1)
    crop_wide = jnp.where((line >= 0) & (line < bounds[-1]), found, -1)
    near = crop_wide[CROP_ROWS - 2 : CROP_ROWS + lines]
    crop_row = near[1:-1]
    same = (crop_row[:, None] == crop_row[None, :]).astype(F32)
    member = (crop_row[:, None] == jnp.arange(crop_count)[None, :]).astype(F32)
    sizes = jnp.sum(jnp.where(member > 0, crop_rows[None, :], 0), axis=1)
    rows = jnp.stack(
        [
            (near[:-2] == crop_row).astype(F32),
            jnp.ones((lines,), F32),
            (near[2:] == crop_row).astype(F32),
            (crop_row == near[0]).astype(F32),
            (crop_row == near[-1]).astype(F32),
            1.0 / (sizes * (W * GSIZE)).astype(F32),
        ]
    )
    rows = jnp.broadcast_to(rows[:, :, None], (6, lines, width))
    crop_end = jnp.sum(jnp.where(member > 0, bounds[None, :], 0), axis=1)
    crop_start = crop_end - sizes
    base = place * lines - (CROP_ROWS - 1)
    step = QB // W
    window_low = (crop_start[::step] - base) * W
    window_high = (crop_end[step - 1 :: step] - base) * W
    starts = window_low // 128 * 128
    counts = (window_high - starts + KB - 1) // KB
    window = -(-(2 * HALO + tokens + KB) // KB) * KB
    key_crop = jnp.pad(
        crop_wide, (0, window // W - crop_wide.shape[0]), constant_values=-2
    ).astype(jnp.int32)
    context_crop = jnp.broadcast_to(
        jnp.repeat(jnp.arange(crop_count, dtype=jnp.int32), CTX)[:, None], (crop_count * CTX, 128)
    )
    query_crop = jnp.repeat(crop_row, W).reshape(-1, 1, QB)
    tables = (starts.astype(jnp.int32), counts.astype(jnp.int32), key_crop, query_crop, context_crop)

    ids = block_ids()
    home, away = chip_ids()
    gain = [gains[i : i + 1] for i in range(3)]
    shift = [shifts[i : i + 1] for i in range(3)]
    inputs = unpack_rows(pixels).astype(F32)
    dy_low = unpack_rows(cotangent)
    dy_beside = along_pix(dy_low[-W:], 1), along_pix(dy_low[:W], -1)
    totals, *messages = stats(inputs, same)
    input_beside = beside_rows(messages)
    a_one, stats_one = norm(inputs, totals, *input_beside, rows, gain[0], shift[0])
    far = far_blocks(a_one)
    blocks = [a_one, to_mate(a_one)]
    blocks, kernel_one, two_local = tie(blocks, kernel_one, two_local)
    kernel_two = gather_rows(two_local)
    one_blocks, (c_one, totals, *messages) = convolve(blocks, far, ids, kernel_one, rows, same, ())
    growth = 1.0 + small(member, embed_terms[:, :width] + offsets[2])
    shift_add = small(member, embed_terms[:, width:] + offsets[3])
    mixed = (growth, shift_add)
    c_beside = beside_rows(messages)
    a_two, stats_two = norm(c_one, totals, *c_beside, rows, gain[1], shift[1], mixed)
    far = far_blocks(a_two)
    blocks = [a_two, to_mate(a_two)]
    blocks, kernel_two, four = tie(blocks, kernel_two, four)
    four = gather_rows(four)
    two_blocks, (resid, totals, *messages) = convolve(
        blocks, far, ids, kernel_two, rows, same, (inputs, offsets[0:1])
    )
    resid_beside = beside_rows(messages)
    n_three, stats_three = norm(
        resid, totals, *resid_beside, rows, gain[2], shift[2], active=None, wide=False
    )
    dy_low, n_three = tie(dy_low, n_three)
    three_blocks = gather_blocks(n_three)
    dy_blocks = gather_blocks(dy_low)
    qkv = project(three_blocks, ids, four, 0, 3 * width)
    first_dy, qkv = lax.optimization_barrier((dy_blocks[0], qkv))
    datt = project([first_dy] + dy_blocks[1:], ids, four, 3 * width, width)
    low = along_pix(qkv[tokens - HALO :, width:], 1)
    high = along_pix(qkv[:HALO, width:], -1)
    att, dquery, dlow, down, dhigh, dckey, dcval = attend(qkv, datt, low, high, ckey, cval, tables)
    from_prev, from_next = along_pix(dhigh, 1), along_pix(dlow, -1)
    arrived = sent_sums(chip_sums(spread(att, away, four, 3 * width)))
    result = resid + offsets[1:2]
    for piece in home_parts(spread(att, home, four, 3 * width)) + arrived:
        result = result + piece.astype(F32)
    result = pack_rows(result)
    dmap_out = outer(dy_blocks, ids, att)
    from_prev, from_next, result, dmap_out = tie(from_prev, from_next, result, dmap_out)
    gap = ((0, tokens - HALO), (0, 0)), ((tokens - HALO, 0), (0, 0))
    down = down + jnp.pad(from_prev.astype(F32), gap[0]) + jnp.pad(from_next.astype(F32), gap[1])
    dqkv = jnp.concatenate([dquery, down.astype(BF)], axis=1)
    sums_three = chip_sums(spread(dqkv, away, four))
    dqkv, sums_three = tie(dqkv, sums_three)
    arrived = sent_sums(sums_three)
    parts = spread(dqkv, home, four)
    dqkv, parts = tie(dqkv, parts)
    dmaps = jnp.concatenate([outer(three_blocks, ids, dqkv), dmap_out], axis=1)
    parts, arrived, dmaps = tie(home_parts(parts), arrived, dmaps)
    parts = parts + arrived
    dmaps = scatter_rows(dmaps)
    e_three, raw_three, totals, *messages = gradient_sums(
        parts, resid, stats_three, gain[2], shift[2], same
    )
    e_beside = beside_rows(messages)
    dresid, taps_two, *parts = gradient_taps(
        e_three, resid, resid_beside, stats_three, totals, *e_beside, rows, gain[2],
        (dy_low, *dy_beside), away, kernel_two,
    )
    sums_two = chip_sums(parts)
    taps_two, sums_two = tie(taps_two, sums_two)
    arrived = sent_sums(sums_two)
    parts = spread(taps_two, home, kernel_two)
    taps_two, parts = tie(taps_two, parts)
    dkernel_two = outer(two_blocks, ids, taps_two, W)
    parts, arrived, dkernel_two, dmaps = tie(home_parts(parts), arrived, dkernel_two, dmaps)
    parts = parts + arrived
    dkernel_two = scatter_rows(dkernel_two)
    e_two, raw_two, totals, *messages = gradient_sums(
        parts, c_one, stats_two, gain[1], shift[1], same, mixed
    )
    e_beside = beside_rows(messages)
    taps_one, *parts = gradient_taps(
        e_two, c_one, c_beside, stats_two, totals, *e_beside, rows, gain[1], None, away, kernel_one
    )
    sums_one = chip_sums(parts)
    taps_one, sums_one = tie(taps_one, sums_one)
    arrived = sent_sums(sums_one)
    parts = spread(taps_one, home, kernel_one)
    taps_one, parts = tie(taps_one, parts)
    dkernel_one = outer(one_blocks, ids, taps_one, W)
    parts, arrived, dkernel_one, dkernel_two = tie(
        home_parts(parts), arrived, dkernel_one, dkernel_two
    )
    parts = parts + arrived
    dkernel_one = scatter_rows(dkernel_one)
    demb = jnp.concatenate(
        [turned(member, raw_two[1] * gain[1] + raw_two[0] * shift[1]), turned(member, raw_two[0])]
    )
    e_one, raw_one, totals, *messages = gradient_sums(
        parts, inputs, stats_one, gain[0], shift[0], same, active="plain"
    )
    grad_pixels = last_gradient(
        e_one, inputs, stats_one, totals, *beside_rows(messages), rows, gain[0], dresid
    )
    sums = jnp.concatenate(
        [
            (raw_two[1] * growth).sum(0)[None],
            raw_three[1].sum(0)[None],
            (raw_two[0] * growth).sum(0)[None],
            raw_three[0].sum(0)[None],
            dresid.sum(0)[None],
            dy_low.astype(F32).sum(0)[None],
            jnp.zeros((2, width), F32),
            demb,
            dckey,
            dcval,
        ],
        axis=0,
    )
    sums = pix_sum(sums)
    last = pix_sum(raw_one.sum(1))
    grad_gains = jnp.concatenate([last[1:2], sums[0:2]])
    grad_shifts = jnp.concatenate([last[0:1], sums[2:4]])
    demb = sums[8 : 8 + 2 * crop_count].reshape(2, crop_count, width)
    grad_offsets = jnp.concatenate([sums[4:6], demb.sum(1)])
    dcontext = sums[8 + 2 * crop_count :].reshape(2, crop_count * CTX, width)
    own_condition = condition_own.astype(F32)
    grad_embedding = jnp.stack([turned(own_condition, demb[i]) for i in range(2)], axis=2)
    own_context = context_own.astype(F32)
    dcontext_maps = [turned(own_context, dcontext[i]) for i in range(2)]
    dmaps = dmaps.astype(F32).reshape(depth_here, 4, width)
    grad_attention = jnp.stack(
        [dmaps[:, 0], dmaps[:, 1], dmaps[:, 2], *dcontext_maps, dmaps[:, 3]], axis=2
    )
    dkernels = jnp.concatenate([dkernel_one, dkernel_two], axis=1)
    grad_kernels = dkernels.reshape(depth_here, 18, width).transpose(0, 2, 1)
    return (
        result,
        pack_rows(grad_pixels),
        grad_kernels.reshape(depth_here, 18 * width).astype(F32),
        grad_attention.reshape(depth_here, 6 * width),
        grad_embedding.reshape(depth_here, 2 * width),
        grad_gains,
        grad_shifts,
        grad_offsets,
    )


def solution(mesh):
    split = P("pix", "ch")
    tall = P(None, "ch")
    return jax.shard_map(
        local,
        mesh=mesh,
        in_specs=(split, split, P(), P(), P(), split, split, split, tall, tall, tall),
        out_specs=(split, split, split, split, split, tall, tall, tall),
        check_vma=False,
    )
```

time: 1780 us -> 781 us (0.44)
  matrix products: 495 us -> 3.34 us
  local copies, waits for them, and re-layouts: 368 us -> 77.4 us
  other arithmetic: 311 us -> 23.8 us
  Pallas kernels: 0 us -> 238 us
  waiting for transfers between devices: 418 us -> 333 us
  blocking collectives: 40.3 us -> 0 us
  starting transfers between devices: 118 us -> 86.9 us
    dot_general x65 -> x10, matrix products: 495 us -> 3.34 us  [the longest x2 1.68 us: small(): return jnp.dot(left, right, precision=HIGHEST)]
    pallas_call x0 -> x27, Pallas kernels: none -> 238 us  [the longest x1 61.6 us: attend(): pl.pallas_call(functools.partial(attention_body, heads), out_shape=shapes...]
    all_gather x7 -> x3, waiting for transfers between devices: 211 us -> 73.3 us  [gather_rows(): return lax.all_gather(value, 'pix', axis=0, tiled=True)]
    convert_element_type x12 -> x7, other arithmetic: 112 us -> 8.31 us  [the longest x4 4.19 us: chip_sums(): (own[i].astype(F32) + to_mate(mate[i]).astype(F32)).astype(BF)]
    ppermute x40 -> x51, waiting for transfers between devices: 99.7 us -> 199 us  [the longest x18 75.2 us: along_pix(): lax.ppermute(value, 'pix', [(i, i + by) for i in range(size) if 0 <= i +...]
    reduce_sum x21 -> x8, other arithmetic: 77.9 us -> 2.16 us  [the longest x1 0.92 us: local(): last = pix_sum(raw_one.sum(1))]
    dot_general x3 -> x0, local copies, waits for them, and re-layouts: 75.3 us -> none  [the longest x2 73.4 us: conv_backward(): jnp.einsum('tk,tc->kc', columns, grad_out, preferred_element_type=jnp.flo...]
    unnamed x17 -> x6, waiting for transfers between devices: 60 us -> 0.1 us
  transfers between devices with their start and end apart: 54 -> 57, of which waited for: 23 -> 35; matrix products, arithmetic and copies ran while one was open for 25% -> 9% of each run, Pallas kernels for 0% -> 21%
where the time goes in v1:
time: 781 us; the launch traced here: 778 us
  waiting for transfers between devices  333 us (43%)
  Pallas kernels  238 us (30%)
  starting transfers between devices  86.9 us (11%)
  local copies, waits for them, and re-layouts  77.4 us (10%)
  other arithmetic  23.8 us (3%)
  between operations  15.6 us (2%)
    ppermute x18, waiting for transfers between devices, along_pix(): lax.ppermute(value, 'pix', [(i, i + by) for i in range(size) if 0 <= i +...  75.2 us
    all_gather x3, waiting for transfers between devices, gather_rows(): return lax.all_gather(value, 'pix', axis=0, tiled=True)  73.3 us
    ppermute x18, starting transfers between devices, along_pix(): lax.ppermute(value, 'pix', [(i, i + by) for i in range(size) if 0 <= i +...  67.4 us
    pallas_call x1, Pallas kernels, attend(): pl.pallas_call(functools.partial(attention_body, heads), out_shape=shapes...  61.6 us
    ppermute x9, waiting for transfers between devices, across_pix(): lax.ppermute(value, 'pix', [(i, i ^ bit) for i in range(lax.axis_size('pi...  61.4 us
    reduce_scatter x3, waiting for transfers between devices, scatter_rows(): return lax.psum_scatter(value, 'pix', scatter_dimension=0, tiled=True)  60.2 us
    ppermute x8, waiting for transfers between devices, to_chip(): lax.ppermute(value, 'ch', [(i, (i + 2 * by) % size) for i in range(size)])  49.7 us
    pallas_call x4, Pallas kernels, outer(): pl.pallas_call(functools.partial(outer_body, count, shift), out_shape=jax...  39.7 us
  transfers between devices with their start and end apart: 57, of which 35 were waited for; matrix products, arithmetic and copies ran while one was open for 9% of the time, Pallas kernels for 21%

profile of v1, /device:TPU:0, one launch (start us, length us, event | category | flops | bytes accessed | tf_op | source)
XLA Modules:
  0.0 778.1 jit_solution(3777307030985488703)
XLA Ops:
  12.4 4.0 reshape.178
  16.4 5.5 copy.58
  22.6 3.4 stats.1
  26.1 5.0 collective-permute-start
  38.0 3.3 norm.3
  43.8 50.5 %all-gather.4.cloned.1.call-done.refs_2_.refs_10_.refs_0_ = bf16[1024,2304]{1,0:T(8,128)(2,1)} async-done(((bf16[128,2304]{1,0:T(8,128)(2,1)}), bf16[1024,2304]{1,0:T(8,128)(2,1)}) %all-gather.4.cloned.1.call-update) | async-done | bytes 4718608 | tf_op jit(solution)/shard_map/all_gather | solution.py:830
  98.7 4.2 collective-permute-done.7
  103.5 8.1 %conv_pair.4.refs_4_ = f32[1536,256]{1,0:T(8,128)} custom-call(s32[2]{0:T(128)} %pad_add_fusion.1.ids, bf16[1600,256]{1,0:T(8,128)(2,1)} %get-tuple-element.119.refs_0_, bf16[1600,256]{1,0:T(8,128)(2,1)} %copy-done.56, bf16[1024,2304]{1,0:T(8,128)(2,1)} %all-gather.4.cloned.1.call-done.refs_2_.refs_10_.refs_0_, ...), custom_call_target="tpu_custom_call" | custom-call | flops 3623878656 | bytes 7077888 | tf_op jit(solution)/shard_map/conv_pair/pallas_call | solution.py:455
  111.6 3.5 collective-permute-done.3.refs_0_.refs_2_
  118.5 15.2 %collective-permute-done.9 = f32[80,512]{1,0:T(8,128)S(1)} collective-permute-done((f32[80,512]{1,0:T(8,128)S(1)}, f32[80,512]{1,0:T(8,128)S(1)}, u32[]{:S(2)}, u32[]{:S(2)}) %collective-permute-start.9) | collective-permute-done | bytes 163872 | tf_op jit(solution)/shard_map/ppermute | solution.py:809
  135.4 9.8 %conv_pair.5 = (f32[1536,256]{1,0:T(8,128)}, f32[2,48,256]{2,1,0:T(8,128)}, f32[40,256]{1,0:T(8,128)}, f32[40,256]{1,0:T(8,128)}) custom-call(s32[2]{0:T(128)} %pad_add_fusion.ids, bf16[1600,256]{1,0:T(8,128)(2,1)} %collective-permute-done.3.refs_0_.refs_2_, bf16[1600,256]{1,0:T(8,128)(2,1)} %copy-done.57, ...), custom_call_target="tpu_custom_call" | custom-call | flops 3623878656 | bytes 7077888 | tf_op jit(solution)/shard_map/conv_pair/pallas_call | solution.py:455
  150.6 4.2 collective-permute-done.6.refs_3_
  155.4 3.3 norm.4
  161.2 22.8 %all-gather.6.cloned.1.call-done.refs_2_.refs_13_.refs_0_ = bf16[1024,2304]{1,0:T(8,128)(2,1)} async-done(((bf16[128,2304]{1,0:T(8,128)(2,1)}), bf16[1024,2304]{1,0:T(8,128)(2,1)}) %all-gather.6.cloned.1.call-update) | async-done | bytes 4718608 | tf_op jit(solution)/shard_map/all_gather | solution.py:830
  185.9 8.1 %conv_pair.6.refs_4_ = f32[1536,256]{1,0:T(8,128)} custom-call(s32[2]{0:T(128)} %pad_add_fusion.1.ids, bf16[1600,256]{1,0:T(8,128)(2,1)} %get-tuple-element.130.refs_0_, bf16[1600,256]{1,0:T(8,128)(2,1)} %copy-done.59, bf16[1024,2304]{1,0:T(8,128)(2,1)} %all-gather.6.cloned.1.call-done.refs_2_.refs_13_.refs_0_, ...), custom_call_target="tpu_custom_call" | custom-call | flops 3623878656 | bytes 7077888 | tf_op jit(solution)/shard_map/conv_pair/pallas_call | solution.py:455
  194.0 9.4 %collective-permute-done.11.refs_0_.refs_2_ = bf16[1600,256]{1,0:T(8,128)(2,1)S(1)} collective-permute-done((bf16[1600,256]{1,0:T(8,128)(2,1)S(1)}, bf16[1600,256]{1,0:T(8,128)(2,1)S(1)}, u32[]{:S(2)}, u32[]{:S(2)}) %collective-permute-start.11) | collective-permute-done | bytes 819232 | tf_op jit(solution)/shard_map/ppermute | solution.py:826
  206.7 10.1 %conv_pair.7 = (f32[1536,256]{1,0:T(8,128)}, f32[2,48,256]{2,1,0:T(8,128)}, f32[40,256]{1,0:T(8,128)}, f32[40,256]{1,0:T(8,128)}) custom-call(s32[2]{0:T(128)} %pad_add_fusion.ids, bf16[1600,256]{1,0:T(8,128)(2,1)} %copy-done.60, bf16[1600,256]{1,0:T(8,128)(2,1)} %copy-done.61, bf16[1024,2304]{1,0:T(8,128)(2,1)} %all-gather.6.cloned.1.call-done.refs_2_.refs_13_.refs_0_, ...), custom_call_target="tpu_custom_call" | custom-call | flops 3623878656 | bytes 7077888 | tf_op jit(solution)/shard_map/conv_pair/pallas_call | solution.py:455
  216.8 3.7 collective-permute-start.13
  221.8 3.6 reshape.147
  225.3 3.1 copy.57
  233.5 18.0 %collective-permute-done.16.refs_2_ = bf16[1536,256]{1,0:T(8,128)(2,1)S(1)} collective-permute-done((bf16[1536,256]{1,0:T(8,128)(2,1)}, bf16[1536,256]{1,0:T(8,128)(2,1)S(1)}, u32[]{:S(2)}, u32[]{:S(2)}) %collective-permute-start.16) | collective-permute-done | bytes 786464 | tf_op jit(solution)/shard_map/ppermute | solution.py:826
  254.5 7.3 project.2.query_ref.own_ref
  264.7 5.2 collective-permute-start.21
  277.6 4.9 project.3.grad_ref
  282.5 30.6 %collective-permute-done.21.low_ref = bf16[992,512]{1,0:T(8,128)(2,1)} collective-permute-done((bf16[992,512]{1,0:T(8,128)(2,1)}, bf16[992,512]{1,0:T(8,128)(2,1)}, u32[]{:S(2)}, u32[]{:S(2)}) %collective-permute-start.21) | collective-permute-done | bytes 1015840 | tf_op jit(solution)/shard_map/ppermute | solution.py:805
  313.8 61.6 %attend.1 = (bf16[1536,256]{1,0:T(8,128)(2,1)}, bf16[1536,256]{1,0:T(8,128)(2,1)}, bf16[992,512]{1,0:T(8,128)(2,1)}, f32[1536,512]{1,0:T(8,128)}, bf16[992,512]{...) custom-call(s32[6]{0:T(128)} %get-tuple-element.247.starts, s32[6]{0:T(128)} %get-tuple-element.246.counts, ...), custom_call_target="tpu_custom_call" | custom-call | flops 2013265920 | bytes 7864320 | tf_op jit(solution)/shard_map/attend/pallas_call | solution.py:767
  375.4 3.5 spread.7
  378.9 3.6 spread.6
  384.0 15.2 %collective-permute-start.23 = (bf16[992,512]{1,0:T(8,128)(2,1)}, bf16[992,512]{1,0:T(8,128)(2,1)}, u32[]{:S(2)}, u32[]{:S(2)}) collective-permute-start(bf16[992,512]{1,0:T(8,128)(2,1)} %get-tuple-element.145), channel_id=1, source_target_pairs={{0,4},{4,8},{8,12},{12,16},{16,20},{20,24},{24,28},{1,5},{5,9},{9,... | collective-permute-start | bytes 3047432 | tf_op jit(solution)/shard_map/ppermute | solution.py:805
  400.8 5.3 outer.4
  408.5 4.0 copy.69
  412.5 6.2 reshape.157
  418.7 23.3 %collective-permute-done.23 = bf16[992,512]{1,0:T(8,128)(2,1)} collective-permute-done((bf16[992,512]{1,0:T(8,128)(2,1)}, bf16[992,512]{1,0:T(8,128)(2,1)}, u32[]{:S(2)}, u32[]{:S(2)}) %collective-permute-start.23) | collective-permute-done | bytes 1015840 | tf_op jit(solution)/shard_map/ppermute | solution.py:805
  445.8 4.8 spread.8
  454.4 4.8 spread.9
  460.6 7.9 %outer.5 = bf16[1024,768]{1,0:T(8,128)(2,1)} custom-call(s32[4]{0:T(128)} %pad_add_fusion.2.ids, bf16[1536,256]{1,0:T(8,128)(2,1)} %get-tuple-element.141.refs_0_, bf16[1536,256]{1,0:T(8,128)(2,1)} %copy-done.63, bf16[1536,256]{1,0:T(8,128)(2,1)} %copy-done.62, bf16[1536,256]{1,0:T(8,128)(2,1)} %collective-permute-done.17.refs_3_, ...), custom_call_target="tpu_custom_call" | custom-call | flops 2415919104 | bytes 3932160 | tf_op jit(solution)/shard_map/outer/pallas_call | solution.py:579
  471.5 7.7 collective-permute-done.30.refs_2_
  480.1 4.5 gradient_sums.3
  484.6 4.4 collective-permute-start.31
  491.0 10.8 %collective-permute-start.33 = (bf16[32,256]{1,0:T(8,128)(2,1)S(1)}, bf16[32,256]{1,0:T(8,128)(2,1)S(1)}, u32[]{:S(2)}, u32[]{:S(2)}) collective-permute-start(bf16[32,256]{1,0:T(8,128)(2,1)S(1)} %get-tuple-element.253), channel_id=1, source_target_pairs={{0,4},{4,8},{8,12},{12,16},{16,20},{20,24},{24,28},{1,5},{5,9},{9,... | collective-permute-start | bytes 49160 | tf_op jit(solution)/shard_map/ppermute | solution.py:805
  503.4 5.1 collective-permute-done.34.refs_12_
  509.2 10.6 %gradient_taps.2 = (f32[1536,256]{1,0:T(8,128)}, bf16[1536,2304]{1,0:T(8,128)(2,1)}, bf16[1,1536,256]{2,1,0:T(8,128)(2,1)}, bf16[1,1536,256]{2,1,0:T(8,128)(2,1)}) custom-call(s32[2]{0:T(128)} %pad_add_fusion.3.ids, f32[1536,256]{1,0:T(8,128)} %get-tuple-element.171.refs_0_, f32[1536,256]{1,0:T(8,128)} %get-tuple-element.135.refs_0_.refs_3_.refs_1_, ...), custom_call_target="tpu_custom_call" | custom-call | flops 1811939328 | bytes 14155776 | tf_op jit(solution)/shard_map/gradient_taps/pallas_call | solution.py:341
  523.6 9.2 %spread.10 = (bf16[1,1536,256]{2,1,0:T(8,128)(2,1)}, bf16[1,1536,256]{2,1,0:T(8,128)(2,1)}) custom-call(s32[2]{0:T(128)} %pad_add_fusion.1.ids, bf16[1536,2304]{1,0:T(8,128)(2,1)} %get-tuple-element.184.grad_ref.refs_4_, bf16[1024,2304]{1,0:T(8,128)(2,1)} %all-gather.6.cloned.1.call-done.refs_2_.refs_13_.refs_0_), custom_call_target="tpu_custom_call" | custom-call | flops 3623878656 | bytes 8257536 | tf_op jit(solution)/shard_map/spread/pallas_call | solution.py:535
  534.0 13.2 %outer.6 = bf16[1024,2304]{1,0:T(8,128)(2,1)} custom-call(s32[4]{0:T(128)} %pad_add_fusion.2.ids, bf16[1600,256]{1,0:T(8,128)(2,1)} %get-tuple-element.130.refs_0_, bf16[1600,256]{1,0:T(8,128)(2,1)} %copy-done.59, bf16[1600,256]{1,0:T(8,128)(2,1)} %copy-done.60, bf16[1600,256]{1,0:T(8,128)(2,1)} %copy-done.61, ...), custom_call_target="tpu_custom_call" | custom-call | flops 7247757312 | bytes 11796480 | tf_op jit(solution)/shard_map/outer/pallas_call | solution.py:579
  547.2 5.6 collective-permute-done.37.refs_2_
  554.8 5.3 gradient_sums.4
  560.1 3.9 collective-permute-start.38
  566.4 4.5 collective-permute-done.39.refs_7_
  571.6 10.2 %gradient_taps.3 = (bf16[1536,2304]{1,0:T(8,128)(2,1)}, bf16[1,1536,256]{2,1,0:T(8,128)(2,1)}, bf16[1,1536,256]{2,1,0:T(8,128)(2,1)}) custom-call(s32[2]{0:T(128)} %pad_add_fusion.3.ids, f32[1536,256]{1,0:T(8,128)} %get-tuple-element.190.refs_0_, f32[1536,256]{1,0:T(8,128)} %get-tuple-element.124.refs_0_.refs_3_.refs_1_, f32[40,256]{1,0:T(8,128)} %copy-done.27, ...), custom_call_target="tpu_custom_call" | custom-call | flops 1811939328 | bytes 14155776 | tf_op jit(solution)/shard_map/gradient_taps/pallas_call | solution.py:341
  585.6 9.4 %spread.11 = (bf16[1,1536,256]{2,1,0:T(8,128)(2,1)}, bf16[1,1536,256]{2,1,0:T(8,128)(2,1)}) custom-call(s32[2]{0:T(128)} %pad_add_fusion.1.ids, bf16[1536,2304]{1,0:T(8,128)(2,1)} %get-tuple-element.203.grad_ref.refs_4_, bf16[1024,2304]{1,0:T(8,128)(2,1)} %all-gather.4.cloned.1.call-done.refs_2_.refs_10_.refs_0_), custom_call_target="tpu_custom_call" | custom-call | flops 3623878656 | bytes 8257536 | tf_op jit(solution)/shard_map/spread/pallas_call | solution.py:535
  596.3 13.3 %outer.7 = bf16[1024,2304]{1,0:T(8,128)(2,1)} custom-call(s32[4]{0:T(128)} %pad_add_fusion.2.ids, bf16[1600,256]{1,0:T(8,128)(2,1)} %get-tuple-element.119.refs_0_, bf16[1600,256]{1,0:T(8,128)(2,1)} %copy-done.56, bf16[1600,256]{1,0:T(8,128)(2,1)} %collective-permute-done.3.refs_0_.refs_2_, bf16[1600,256]{1,0:T(8,128)(2,1)} %copy-done.57, ...), custom_call_target="tpu_custom_call" | custom-call | flops 7247757312 | bytes 11796480 | tf_op jit(solution)/shard_map/outer/pallas_call | solution.py:579
  609.6 5.3 collective-permute-done.42.refs_2_
  615.0 37.3 %reduce-scatter.6.cloned.1.call-done = bf16[128,2304]{1,0:T(8,128)(2,1)} async-done(((bf16[1024,2304]{1,0:T(8,128)(2,1)}), bf16[128,2304]{1,0:T(8,128)(2,1)}) %reduce-scatter.6.cloned.1.call-update) | async-done | bytes 589840 | tf_op jit(solution)/shard_map/reduce_scatter | solution.py:834
  657.4 4.0 collective-permute-done.45
  662.9 13.4 %collective-permute-done.46 = f32[168,256]{1,0:T(8,128)S(1)} collective-permute-done((f32[168,256]{1,0:T(8,128)S(1)}, f32[168,256]{1,0:T(8,128)S(1)}, u32[]{:S(2)}, u32[]{:S(2)}) %collective-permute-start.46) | collective-permute-done | bytes 172064 | tf_op jit(solution)/shard_map/ppermute | solution.py:809
  676.4 17.3 %collective-permute-done.47 = f32[168,256]{1,0:T(8,128)S(1)} collective-permute-done((f32[168,256]{1,0:T(8,128)S(1)}, f32[168,256]{1,0:T(8,128)S(1)}, u32[]{:S(2)}, u32[]{:S(2)}) %collective-permute-start.47) | collective-permute-done | bytes 172064 | tf_op jit(solution)/shard_map/ppermute | solution.py:809
  694.9 5.2 gradient_sums.5
  704.6 3.6 collective-permute-done.49
  712.4 3.7 collective-permute-start.43
  718.4 4.3 collective-permute-done.44.after_ref
  723.3 4.3 last_gradient.1
  727.6 5.0 copy.70
  732.6 6.1 reshape.159
  738.8 21.0 %reduce-scatter.8.cloned.1.call-done = bf16[128,2304]{1,0:T(8,128)(2,1)} async-done(((bf16[1024,2304]{1,0:T(8,128)(2,1)}), bf16[128,2304]{1,0:T(8,128)(2,1)}) %reduce-scatter.8.cloned.1.call-update) | async-done | bytes 589840 | tf_op jit(solution)/shard_map/reduce_scatter | solution.py:834
  (334 shorter events, 126.8 us)
Async XLA Ops:
  7.2 88.3 %copy-start = (bf16[16,1024]{1,0:T(8,128)(2,1)S(1)}, bf16[16,1024]{1,0:T(8,128)(2,1)}, u32[]{:S(2)}) copy-start(bf16[16,1024]{1,0:T(8,128)(2,1)} %param.14) | copy-start | bytes 98308
  7.2 87.2 %all-gather.4.cloned.1.call-start = ((), (), s32[]{:S(2)}) async-start(), calls=%async_computation.3 | async-start | bytes 5308416 | tf_op jit(solution)/shard_map/all_gather | solution.py:830
  10.8 173.3 %all-gather.6.cloned.1.call-start = ((), (), s32[]{:S(2)}) async-start(), calls=%async_computation.4 | async-start | bytes 5308416 | tf_op jit(solution)/shard_map/all_gather | solution.py:830
  12.4 260.0 %copy-start.44 = (s32[48]{0:T(128)}, s32[48]{0:T(128)S(1)}, u32[]{:S(2)}) copy-start(s32[48]{0:T(128)S(1)} %slice.178) | copy-start | bytes 580
  26.1 9.5 %collective-permute-start = (f32[40,256]{1,0:T(8,128)}, f32[40,256]{1,0:T(8,128)S(1)}, u32[]{:S(2)}, u32[]{:S(2)}) collective-permute-start(f32[40,256]{1,0:T(8,128)} %get-tuple-element.116), channel_id=1, source_target_pairs={{0,4},{4,8},{8,12},{12,16},{16,20},{20,24},{24,28},{1,5},{5,9},{9,... | collective-permute-start | bytes 122888 | tf_op jit(solution)/shard_map/ppermute | solution.py:805
  31.0 6.1 collective-permute-start.1
  38.0 56.7 %copy-start.24 = (bf16[128,1536]{1,0:T(8,128)(2,1)S(1)}, bf16[128,1536]{1,0:T(8,128)(2,1)}, u32[]{:S(2)}) copy-start(bf16[128,1536]{1,0:T(8,128)(2,1)} %param.17) | copy-start | bytes 1179652
  41.3 2.5 collective-permute-start.2
  42.3 52.7 %copy-start.31 = (bf16[16,4,1024]{2,1,0:T(4,128)(2,1)S(1)}, bf16[16,4,1024]{2,1,0:T(4,128)(2,1)}, u32[]{:S(2)}) copy-start(bf16[16,4,1024]{2,1,0:T(4,128)(2,1)} %param.15) | copy-start | bytes 393220
  43.8 51.3 %copy-start.56 = (bf16[1600,256]{1,0:T(8,128)(2,1)}, bf16[1600,256]{1,0:T(8,128)(2,1)S(1)}, u32[]{:S(2)}) copy-start(bf16[1600,256]{1,0:T(8,128)(2,1)S(1)} %collective-permute-done.2.refs_1_) | copy-start | bytes 2457604
  94.4 159.5 %all-gather.8.cloned.1.call-start = ((), (), s32[]{:S(2)}) async-start(), calls=%async_computation.5 | async-start | bytes 2359296 | tf_op jit(solution)/shard_map/all_gather | solution.py:830
  96.0 19.1 %collective-permute-start.3 = (bf16[1600,256]{1,0:T(8,128)(2,1)S(1)}, bf16[1600,256]{1,0:T(8,128)(2,1)}, u32[]{:S(2)}, u32[]{:S(2)}) collective-permute-start(bf16[1600,256]{1,0:T(8,128)(2,1)S(1)} %copy-done.55), channel_id=1, source_target_pairs={{0,2},{1,3},{2,0},{3,1},{4,6},{5,7},{6,4},{7,5},{8,10},{9,11},{10,... | collective-permute-start | bytes 2457608 | tf_op jit(solution)/shard_map/ppermute | solution.py:826
  97.5 5.4 collective-permute-start.7
  102.9 13.9 %collective-permute-start.8 = (f32[80,512]{1,0:T(8,128)S(1)}, f32[80,512]{1,0:T(8,128)S(1)}, u32[]{:S(2)}, u32[]{:S(2)}) collective-permute-start(f32[80,512]{1,0:T(8,128)S(1)} %fusion.55), channel_id=1, source_target_pairs={{0,8},{4,12},{8,0},{12,4},{16,24},{20,28},{24,16},{28,20},{1,9},{5... | collective-permute-start | bytes 491528 | tf_op jit(solution)/shard_map/ppermute | solution.py:809
  115.1 19.4 %collective-permute-start.4 = (bf16[1600,256]{1,0:T(8,128)(2,1)}, bf16[1600,256]{1,0:T(8,128)(2,1)S(1)}, u32[]{:S(2)}, u32[]{:S(2)}) collective-permute-start(bf16[1600,256]{1,0:T(8,128)(2,1)} %collective-permute-done.3.refs_0_.refs_2_), channel_id=1, source_target_pairs={{0,1},{1,0},{2,3},{3,2},{4,5},{5,4},{6,7},{7,6},{8,9},{9,8},{10,11... | collective-permute-start | bytes 2457608 | tf_op jit(solution)/shard_map/ppermute | solution.py:821
  116.9 16.7 %collective-permute-start.9 = (f32[80,512]{1,0:T(8,128)S(1)}, f32[80,512]{1,0:T(8,128)S(1)}, u32[]{:S(2)}, u32[]{:S(2)}) collective-permute-start(f32[80,512]{1,0:T(8,128)S(1)} %add.164), channel_id=1, source_target_pairs={{0,16},{4,20},{8,24},{12,28},{16,0},{20,4},{24,8},{28,12},{1,17},{... | collective-permute-start | bytes 491528 | tf_op jit(solution)/shard_map/ppermute | solution.py:809
  145.3 5.3 collective-permute-start.5
  147.7 7.0 collective-permute-start.6
  158.7 2.5 collective-permute-start.10
  184.0 370.6 %reduce-scatter.4.cloned.1.call-start = ((), (), s32[]{:S(2)}) async-start(), calls=%async_computation.6 | async-start | bytes 2359296 | tf_op jit(solution)/shard_map/reduce_scatter | solution.py:834
  184.3 19.1 %collective-permute-start.11 = (bf16[1600,256]{1,0:T(8,128)(2,1)S(1)}, bf16[1600,256]{1,0:T(8,128)(2,1)S(1)}, u32[]{:S(2)}, u32[]{:S(2)}) collective-permute-start(bf16[1600,256]{1,0:T(8,128)(2,1)S(1)} %copy-done.58), channel_id=1, source_target_pairs={{0,2},{1,3},{2,0},{3,1},{4,6},{5,7},{6,4},{7,5},{8,10},{9,11},{10,... | collective-permute-start | bytes 2457608 | tf_op jit(solution)/shard_map/ppermute | solution.py:826
  203.4 2.3 collective-permute-start.12
  216.8 11.7 %collective-permute-start.13 = (f32[40,256]{1,0:T(8,128)}, f32[40,256]{1,0:T(8,128)S(1)}, u32[]{:S(2)}, u32[]{:S(2)}) collective-permute-start(f32[40,256]{1,0:T(8,128)} %get-tuple-element.137), channel_id=1, source_target_pairs={{0,4},{4,8},{8,12},{12,16},{16,20},{20,24},{24,28},{1,5},{5,9},{9,... | collective-permute-start | bytes 122888 | tf_op jit(solution)/shard_map/ppermute | solution.py:805
  220.4 8.1 %collective-permute-start.14 = (f32[40,256]{1,0:T(8,128)}, f32[40,256]{1,0:T(8,128)S(1)}, u32[]{:S(2)}, u32[]{:S(2)}) collective-permute-start(f32[40,256]{1,0:T(8,128)} %get-tuple-element.138), channel_id=1, source_target_pairs={{4,0},{8,4},{12,8},{16,12},{20,16},{24,20},{28,24},{5,1},{9,5},{13... | collective-permute-start | bytes 122888 | tf_op jit(solution)/shard_map/ppermute | solution.py:805
  228.5 43.2 %copy-start.2 = (bf16[48,256,32]{1,2,0:T(8,128)(2,1)}, bf16[48,256,32]{1,2,0:T(8,128)(2,1)S(1)}, u32[]{:S(2)}) copy-start(bf16[48,256,32]{1,2,0:T(8,128)(2,1)S(1)} %copy.57) | copy-start | bytes 2359300
  232.0 19.5 %collective-permute-start.16 = (bf16[1536,256]{1,0:T(8,128)(2,1)}, bf16[1536,256]{1,0:T(8,128)(2,1)S(1)}, u32[]{:S(2)}, u32[]{:S(2)}) collective-permute-start(bf16[1536,256]{1,0:T(8,128)(2,1)} %get-tuple-element.141.refs_0_), channel_id=1, source_target_pairs={{0,2},{1,3},{2,0},{3,1},{4,6},{5,7},{6,4},{7,5},{8,10},{9,11},{10,... | collective-permute-start | bytes 2359304 | tf_op jit(solution)/shard_map/ppermute | solution.py:826
  233.5 20.1 %collective-permute-start.15 = (bf16[1536,256]{1,0:T(8,128)(2,1)}, bf16[1536,256]{1,0:T(8,128)(2,1)S(1)}, u32[]{:S(2)}, u32[]{:S(2)}) collective-permute-start(bf16[1536,256]{1,0:T(8,128)(2,1)} %get-tuple-element.141.refs_0_), channel_id=1, source_target_pairs={{0,1},{1,0},{2,3},{3,2},{4,5},{5,4},{6,7},{7,6},{8,9},{9,8},{10,11... | collective-permute-start | bytes 2359304 | tf_op jit(solution)/shard_map/ppermute | solution.py:821
  251.5 2.4 collective-permute-start.17
  251.5 20.3 %collective-permute-start.19 = (bf16[1536,256]{1,0:T(8,128)(2,1)S(1)}, bf16[1536,256]{1,0:T(8,128)(2,1)S(1)}, u32[]{:S(2)}, u32[]{:S(2)}) collective-permute-start(bf16[1536,256]{1,0:T(8,128)(2,1)S(1)} %bitcast.150), channel_id=1, source_target_pairs={{0,2},{1,3},{2,0},{3,1},{4,6},{5,7},{6,4},{7,5},{8,10},{9,11},{10,... | collective-permute-start | bytes 2359304 | tf_op jit(solution)/shard_map/ppermute | solution.py:826
  264.7 48.4 %collective-permute-start.21 = (bf16[992,512]{1,0:T(8,128)(2,1)}, bf16[992,512]{1,0:T(8,128)(2,1)}, u32[]{:S(2)}, u32[]{:S(2)}) collective-permute-start(bf16[992,512]{1,0:T(8,128)(2,1)} %get-tuple-element.249), channel_id=1, source_target_pairs={{0,4},{4,8},{8,12},{12,16},{16,20},{20,24},{24,28},{1,5},{5,9},{9,... | collective-permute-start | bytes 3047432 | tf_op jit(solution)/shard_map/ppermute | solution.py:805
  269.9 43.2 %collective-permute-start.22 = (bf16[992,512]{1,0:T(8,128)(2,1)}, bf16[992,512]{1,0:T(8,128)(2,1)}, u32[]{:S(2)}, u32[]{:S(2)}) collective-permute-start(bf16[992,512]{1,0:T(8,128)(2,1)} %get-tuple-element.248), channel_id=1, source_target_pairs={{4,0},{8,4},{12,8},{16,12},{20,16},{24,20},{28,24},{5,1},{9,5},{13... | collective-permute-start | bytes 3047432 | tf_op jit(solution)/shard_map/ppermute | solution.py:805
  271.7 4.1 collective-permute-start.18
  271.8 4.0 collective-permute-start.20
  378.9 4.0 collective-permute-start.26
  382.5 23.6 %collective-permute-start.25 = (bf16[1536,256]{1,0:T(8,128)(2,1)}, bf16[1536,256]{1,0:T(8,128)(2,1)S(1)}, u32[]{:S(2)}, u32[]{:S(2)}) collective-permute-start(bf16[1536,256]{1,0:T(8,128)(2,1)} %bitcast.184), channel_id=1, source_target_pairs={{0,1},{1,0},{2,3},{3,2},{4,5},{5,4},{6,7},{7,6},{8,9},{9,8},{10,11... | collective-permute-start | bytes 2359304 | tf_op jit(solution)/shard_map/ppermute | solution.py:821
  383.1 23.1 %collective-permute-start.27 = (bf16[1536,256]{1,0:T(8,128)(2,1)S(1)}, bf16[1536,256]{1,0:T(8,128)(2,1)S(1)}, u32[]{:S(2)}, u32[]{:S(2)}) collective-permute-start(bf16[1536,256]{1,0:T(8,128)(2,1)S(1)} %fusion.3), channel_id=1, source_target_pairs={{0,2},{1,3},{2,0},{3,1},{4,6},{5,7},{6,4},{7,5},{8,10},{9,11},{10,... | collective-permute-start | bytes 2359304 | tf_op jit(solution)/shard_map/ppermute | solution.py:826
  384.0 58.0 %collective-permute-start.23 = (bf16[992,512]{1,0:T(8,128)(2,1)}, bf16[992,512]{1,0:T(8,128)(2,1)}, u32[]{:S(2)}, u32[]{:S(2)}) collective-permute-start(bf16[992,512]{1,0:T(8,128)(2,1)} %get-tuple-element.145), channel_id=1, source_target_pairs={{0,4},{4,8},{8,12},{12,16},{16,20},{20,24},{24,28},{1,5},{5,9},{9,... | collective-permute-start | bytes 3047432 | tf_op jit(solution)/shard_map/ppermute | solution.py:805
  399.2 42.8 %collective-permute-start.24 = (bf16[992,512]{1,0:T(8,128)(2,1)}, bf16[992,512]{1,0:T(8,128)(2,1)}, u32[]{:S(2)}, u32[]{:S(2)}) collective-permute-start(bf16[992,512]{1,0:T(8,128)(2,1)} %get-tuple-element.146), channel_id=1, source_target_pairs={{4,0},{8,4},{12,8},{16,12},{20,16},{24,20},{28,24},{5,1},{9,5},{13... | collective-permute-start | bytes 3047432 | tf_op jit(solution)/shard_map/ppermute | solution.py:805
  450.6 2.5 collective-permute-start.28
  459.3 12.2 %collective-permute-start.29 = (bf16[1536,256]{1,0:T(8,128)(2,1)}, bf16[1536,256]{1,0:T(8,128)(2,1)S(1)}, u32[]{:S(2)}, u32[]{:S(2)}) collective-permute-start(bf16[1536,256]{1,0:T(8,128)(2,1)} %bitcast.185), channel_id=1, source_target_pairs={{0,1},{1,0},{2,3},{3,2},{4,5},{5,4},{6,7},{7,6},{8,9},{9,8},{10,11... | collective-permute-start | bytes 2359304 | tf_op jit(solution)/shard_map/ppermute | solution.py:821
  459.4 19.8 %collective-permute-start.30 = (bf16[1536,256]{1,0:T(8,128)(2,1)S(1)}, bf16[1536,256]{1,0:T(8,128)(2,1)S(1)}, u32[]{:S(2)}, u32[]{:S(2)}) collective-permute-start(bf16[1536,256]{1,0:T(8,128)(2,1)S(1)} %fusion.2), channel_id=1, source_target_pairs={{0,2},{1,3},{2,0},{3,1},{4,6},{5,7},{6,4},{7,5},{8,10},{9,11},{10,... | collective-permute-start | bytes 2359304 | tf_op jit(solution)/shard_map/ppermute | solution.py:826
  479.3 173.0 %reduce-scatter.6.cloned.1.call-start = ((), (), s32[]{:S(2)}) async-start(), calls=%async_computation.7 | async-start | bytes 5308416 | tf_op jit(solution)/shard_map/reduce_scatter | solution.py:834
  484.6 23.9 %collective-permute-start.31 = (f32[40,256]{1,0:T(8,128)}, f32[40,256]{1,0:T(8,128)S(1)}, u32[]{:S(2)}, u32[]{:S(2)}) collective-permute-start(f32[40,256]{1,0:T(8,128)} %get-tuple-element.173), channel_id=1, source_target_pairs={{0,4},{4,8},{8,12},{12,16},{16,20},{20,24},{24,28},{1,5},{5,9},{9,... | collective-permute-start | bytes 122888 | tf_op jit(solution)/shard_map/ppermute | solution.py:805
  489.0 19.6 %collective-permute-start.32 = (f32[40,256]{1,0:T(8,128)}, f32[40,256]{1,0:T(8,128)S(1)}, u32[]{:S(2)}, u32[]{:S(2)}) collective-permute-start(f32[40,256]{1,0:T(8,128)} %get-tuple-element.174), channel_id=1, source_target_pairs={{4,0},{8,4},{12,8},{16,12},{20,16},{24,20},{28,24},{5,1},{9,5},{13... | collective-permute-start | bytes 122888 | tf_op jit(solution)/shard_map/ppermute | solution.py:805
  491.0 12.3 %collective-permute-start.33 = (bf16[32,256]{1,0:T(8,128)(2,1)S(1)}, bf16[32,256]{1,0:T(8,128)(2,1)S(1)}, u32[]{:S(2)}, u32[]{:S(2)}) collective-permute-start(bf16[32,256]{1,0:T(8,128)(2,1)S(1)} %get-tuple-element.253), channel_id=1, source_target_pairs={{0,4},{4,8},{8,12},{12,16},{16,20},{20,24},{24,28},{1,5},{5,9},{9,... | collective-permute-start | bytes 49160 | tf_op jit(solution)/shard_map/ppermute | solution.py:805
  501.8 6.7 collective-permute-start.34
  519.8 2.5 collective-permute-start.35
  532.8 14.4 %collective-permute-start.36 = (bf16[1536,256]{1,0:T(8,128)(2,1)}, bf16[1536,256]{1,0:T(8,128)(2,1)S(1)}, u32[]{:S(2)}, u32[]{:S(2)}) collective-permute-start(bf16[1536,256]{1,0:T(8,128)(2,1)} %bitcast.188), channel_id=1, source_target_pairs={{0,1},{1,0},{2,3},{3,2},{4,5},{5,4},{6,7},{7,6},{8,9},{9,8},{10,11... | collective-permute-start | bytes 2359304 | tf_op jit(solution)/shard_map/ppermute | solution.py:821
  532.9 19.9 %collective-permute-start.37 = (bf16[1536,256]{1,0:T(8,128)(2,1)S(1)}, bf16[1536,256]{1,0:T(8,128)(2,1)S(1)}, u32[]{:S(2)}, u32[]{:S(2)}) collective-permute-start(bf16[1536,256]{1,0:T(8,128)(2,1)S(1)} %fusion.1), channel_id=1, source_target_pairs={{0,2},{1,3},{2,0},{3,1},{4,6},{5,7},{6,4},{7,5},{8,10},{9,11},{10,... | collective-permute-start | bytes 2359304 | tf_op jit(solution)/shard_map/ppermute | solution.py:826
  554.7 205.1 %reduce-scatter.8.cloned.1.call-start = ((), (), s32[]{:S(2)}) async-start(), calls=%async_computation.8 | async-start | bytes 5308416 | tf_op jit(solution)/shard_map/reduce_scatter | solution.py:834
  560.1 6.3 collective-permute-start.38
  564.0 7.0 collective-permute-start.39
  581.8 2.5 collective-permute-start.40
  595.0 14.6 %collective-permute-start.41 = (bf16[1536,256]{1,0:T(8,128)(2,1)}, bf16[1536,256]{1,0:T(8,128)(2,1)S(1)}, u32[]{:S(2)}, u32[]{:S(2)}) collective-permute-start(bf16[1536,256]{1,0:T(8,128)(2,1)} %bitcast.186), channel_id=1, source_target_pairs={{0,1},{1,0},{2,3},{3,2},{4,5},{5,4},{6,7},{7,6},{8,9},{9,8},{10,11... | collective-permute-start | bytes 2359304 | tf_op jit(solution)/shard_map/ppermute | solution.py:821
  595.1 19.9 %collective-permute-start.42 = (bf16[1536,256]{1,0:T(8,128)(2,1)S(1)}, bf16[1536,256]{1,0:T(8,128)(2,1)S(1)}, u32[]{:S(2)}, u32[]{:S(2)}) collective-permute-start(bf16[1536,256]{1,0:T(8,128)(2,1)S(1)} %fusion), channel_id=1, source_target_pairs={{0,2},{1,3},{2,0},{3,1},{4,6},{5,7},{6,4},{7,5},{8,10},{9,11},{10,... | collective-permute-start | bytes 2359304 | tf_op jit(solution)/shard_map/ppermute | solution.py:826
  609.6 42.7 %copy-start.12 = (bf16[1536,256]{1,0:T(8,128)(2,1)}, bf16[1536,256]{1,0:T(8,128)(2,1)S(1)}, u32[]{:S(2)}) copy-start(bf16[1536,256]{1,0:T(8,128)(2,1)S(1)} %collective-permute-done.41.refs_1_) | copy-start | bytes 2359300
  655.2 6.1 collective-permute-start.45
  661.4 14.9 %collective-permute-start.46 = (f32[168,256]{1,0:T(8,128)S(1)}, f32[168,256]{1,0:T(8,128)S(1)}, u32[]{:S(2)}, u32[]{:S(2)}) collective-permute-start(f32[168,256]{1,0:T(8,128)S(1)} %add.188), channel_id=1, source_target_pairs={{0,8},{4,12},{8,0},{12,4},{16,24},{20,28},{24,16},{28,20},{1,9},{5... | collective-permute-start | bytes 516104 | tf_op jit(solution)/shard_map/ppermute | solution.py:809
  676.3 17.4 %collective-permute-start.47 = (f32[168,256]{1,0:T(8,128)S(1)}, f32[168,256]{1,0:T(8,128)S(1)}, u32[]{:S(2)}, u32[]{:S(2)}) collective-permute-start(f32[168,256]{1,0:T(8,128)S(1)} %add.189), channel_id=1, source_target_pairs={{0,16},{4,20},{8,24},{12,28},{16,0},{20,4},{24,8},{28,12},{1,17},{... | collective-permute-start | bytes 516104 | tf_op jit(solution)/shard_map/ppermute | solution.py:809
  701.0 3.6 collective-permute-start.48
  704.6 3.6 collective-permute-start.49
  708.2 9.5 %collective-permute-start.50 = (f32[2,256]{1,0:T(2,128)S(1)}, f32[2,256]{1,0:T(2,128)S(1)}, u32[]{:S(2)}, u32[]{:S(2)}) collective-permute-start(f32[2,256]{1,0:T(2,128)S(1)} %add.192), channel_id=1, source_target_pairs={{0,16},{4,20},{8,24},{12,28},{16,0},{20,4},{24,8},{28,12},{1,17},{... | collective-permute-start | bytes 6152 | tf_op jit(solution)/shard_map/ppermute | solution.py:809
  712.4 6.0 collective-permute-start.43
  716.1 6.6 collective-permute-start.44
  (59 other events, 316.3 us)
Sparse Core Ops, SparseCore 0:
  10.9 83.4 all-gather.3
  97.1 86.8 all-gather.5
  186.7 49.1 all-gather.7
  479.4 75.2 reduce-scatter.3
  558.2 94.0 reduce-scatter.5
  655.8 103.9 reduce-scatter.7

commit v2 on v1

--- a/solution.py
+++ b/solution.py
@@ -240,6 +240,27 @@
     return scale * (grad * gain_ref[...] - mean_ref[0, here, :] - normal * mean_ref[1, here, :])
 
 
+def write_taps(wide_ref, rows_ref, taps_ref):
+    tokens = taps_ref.shape[0]
+    width = wide_ref.shape[1]
+    column = lax.broadcasted_iota(jnp.int32, (W, width), 0)
+
+    def spread_row(line, carry):
+        start = pl.multiple_of(line * W, W)
+        target = pl.ds(start, W)
+        for up in range(3):
+            mask = rows_ref[up, pl.ds(line, 1), :]
+            values = wide_ref[pl.ds(start + up * W, W), :].astype(F32) * mask
+            left = jnp.where(column > 0, pltpu.roll(values, 1, 0), 0.0)
+            right = jnp.where(column < W - 1, pltpu.roll(values, W - 1, 0), 0.0)
+            for side, moved in enumerate((left, values, right)):
+                tap = 8 - (3 * up + side)
+                taps_ref[target, tap * width : (tap + 1) * width] = moved.astype(BF)
+        return carry
+
+    lax.fori_loop(0, tokens // W, spread_row, 0, unroll=2)
+
+
 def taps_body(based, ids, *refs):
     grad_ref, value_ref, value_before, value_after, stats_ref, totals_ref = refs[:6]
     before_ref, after_ref, rows_ref, gain_ref = refs[6:10]
@@ -254,7 +275,7 @@
         refs = refs[1:]
     taps_ref = refs[0]
     refs = refs[1:]
-    same_core, other_core, wide_ref, mean_ref = refs
+    low_ref, same_core, other_core, wide_ref, mean_ref = refs
     tokens, width = grad_ref.shape
     lines = tokens // W
     padded = tokens + 2 * W
@@ -287,22 +308,8 @@
                 found = found + (base_before if line == 0 else base_after)[0:W, :].astype(F32)
             wide_ref[start : start + W, :] = found
 
-        column = lax.broadcasted_iota(jnp.int32, (W, width), 0)
-
-        def spread_row(line, carry):
-            start = pl.multiple_of(line * W, W)
-            target = pl.ds(start, W)
-            for up in range(3):
-                mask = rows_ref[up, pl.ds(line, 1), :]
-                values = wide_ref[pl.ds(start + up * W, W), :] * mask
-                left = jnp.where(column > 0, pltpu.roll(values, 1, 0), 0.0)
-                right = jnp.where(column < W - 1, pltpu.roll(values, W - 1, 0), 0.0)
-                for side, moved in enumerate((left, values, right)):
-                    tap = 8 - (3 * up + side)
-                    taps_ref[target, tap * width : (tap + 1) * width] = moved.astype(BF)
-            return carry
-
-        lax.fori_loop(0, lines, spread_row, 0, unroll=2)
+        write_taps(wide_ref, rows_ref, taps_ref)
+        low_ref[...] = wide_ref[...].astype(BF)
 
     core = ids[ids.shape[0] - 1]
     write_products(taps_ref, map_ref, core, same_core, other_core)
@@ -336,6 +343,9 @@
     if base is not None:
         full_shape = jax.ShapeDtypeStruct((tokens, width), F32)
         shapes, out_specs = [full_shape] + shapes, [whole(full_shape)] + out_specs
+    low_shape = jax.ShapeDtypeStruct((tokens + 2 * W, width), BF)
+    shapes.append(low_shape)
+    out_specs.append(whole(low_shape))
     shapes += [jax.ShapeDtypeStruct((count, tokens, width), BF)] * 2
     out_specs += [pl.BlockSpec((1, tokens, width), lambda step, ids: (step, 0, 0))] * 2
     return pl.pallas_call(
@@ -469,20 +479,16 @@
     return found if resid is not None else found[0]
 
 
-def convolve(blocks, far, ids, kernel, rows, same, resid):
-    pairs = lax.axis_size("ch") // 2
+def convolve(blocks, ids, kernel, rows, same, resid):
     found = None
-    for pair in range(pairs):
+    for pair in range(len(blocks) // 2):
         place = jnp.stack([ids[2 * pair] // 2, ids[2 * pair] % 2])
-        final = pair == pairs - 1
+        final = 2 * pair + 2 == len(blocks)
         found = conv_pair(
             blocks[2 * pair], blocks[2 * pair + 1], place, kernel, rows, found,
             resid if final else None, same,
         )
-        if pair == 0 and far:
-            found, *far = tie(found, *far)
-            blocks = blocks + with_mates(far)
-    return blocks, found
+    return found
 
 
 def project_body(count, width, ids, *refs):
@@ -548,6 +554,93 @@
         cost_estimate=cost(4 * tokens * count * width * wide, (tokens + count * width) * wide * 2),
         name="spread",
     )(ids, grad, maps)
+
+
+def half_own_body(count, ids, *refs):
+    blocks = refs[:count]
+    grad_ref, out_ref, turned_ref = refs[count:]
+    tokens = grad_ref.shape[0]
+    half = blocks[0].shape[1] // 2
+
+    @pl.when(pl.program_id(0) == 0)
+    def _():
+        lanes = pl.ds(pl.multiple_of(ids[count] * half, half), half)
+        for place in range(count):
+            rows = pl.ds(pl.multiple_of(ids[place] * half, half), half)
+            turned_ref[rows, :] = blocks[place][W : W + tokens, lanes].T
+
+    out_ref[...] = dot(turned_ref[...], grad_ref[...], NN)
+
+
+def half_own(blocks, ids, grad):
+    count = len(blocks)
+    tokens, wide = grad.shape
+    padded, width = blocks[0].shape
+    depth, tile = count * width // 2, 3 * width
+    return pl.pallas_call(
+        functools.partial(half_own_body, count),
+        out_shape=jax.ShapeDtypeStruct((depth, wide), F32),
+        grid_spec=pltpu.PrefetchScalarGridSpec(
+            num_scalar_prefetch=1,
+            grid=(wide // tile,),
+            in_specs=[pl.BlockSpec((padded, width), lambda step, ids: (0, 0))] * count
+            + [pl.BlockSpec((tokens, tile), lambda step, ids: (0, step))],
+            out_specs=pl.BlockSpec((depth, tile), lambda step, ids: (0, step)),
+            scratch_shapes=[pltpu.VMEM((depth, tokens), BF)],
+        ),
+        compiler_params=params(),
+        cost_estimate=cost(2 * tokens * depth * wide, (tokens + 2 * depth) * wide * 2),
+        name="half_own",
+    )(ids, *blocks, grad)
+
+
+def half_beside_body(count, ids, *refs):
+    pairs = refs[:2]
+    wide_ref, rows_ref, own_ref, out_ref, turned_ref, taps_ref = refs[2:]
+    tokens = taps_ref.shape[0]
+    half = pairs[0].shape[1] // (count // 2)
+    tile = out_ref.shape[1]
+    step = pl.program_id(0)
+
+    @pl.when(step == 0)
+    def _():
+        write_taps(wide_ref, rows_ref, taps_ref)
+        for place in range(count):
+            rows = pl.ds(pl.multiple_of(ids[place] * half, half), half)
+            lanes = slice(place // 2 * half, (place // 2 + 1) * half)
+            turned_ref[rows, :] = pairs[place % 2][:, lanes].T
+
+    columns = pl.ds(pl.multiple_of(step * tile, tile), tile)
+    out_ref[...] = (own_ref[...] + dot(turned_ref[...], taps_ref[:, columns], NN)).astype(BF)
+
+
+def half_beside(pairs, ids, wide_grad, row_masks, own):
+    count = ids.shape[0] - 1
+    tokens, both = pairs[0].shape
+    depth, wide = own.shape
+    padded, width = wide_grad.shape
+    tile = 3 * width
+    once = lambda step, ids: (0, 0)
+    return pl.pallas_call(
+        functools.partial(half_beside_body, count),
+        out_shape=jax.ShapeDtypeStruct((depth, wide), BF),
+        grid_spec=pltpu.PrefetchScalarGridSpec(
+            num_scalar_prefetch=1,
+            grid=(wide // tile,),
+            in_specs=[
+                pl.BlockSpec((tokens, both), once),
+                pl.BlockSpec((tokens, both), once),
+                pl.BlockSpec((padded, width), once),
+                pl.BlockSpec(row_masks.shape, lambda step, ids: (0, 0, 0)),
+                pl.BlockSpec((depth, tile), lambda step, ids: (0, step)),
+            ],
+            out_specs=pl.BlockSpec((depth, tile), lambda step, ids: (0, step)),
+            scratch_shapes=[pltpu.VMEM((depth, tokens), BF), pltpu.VMEM((tokens, wide), BF)],
+        ),
+        compiler_params=params(),
+        cost_estimate=cost(2 * tokens * depth * wide, (tokens + 3 * depth) * wide * 2),
+        name="half_beside",
+    )(ids, *pairs, wide_grad, row_masks, own)
 
 
 def outer_body(count, shift, ids, *refs):
@@ -597,7 +690,7 @@
     heads, starts, counts, crops, query_ref, grad_ref, low_ref, own_ref, high_ref, ckey_ref,
     cval_ref, qcrop_ref, ccrop_ref, att_ref, dquery_ref, dlow_ref, down_ref, dhigh_ref, dckey_ref,
     dcval_ref, keys, values, keys_t, values_t, dkeys, dvalues, kcrop_ref, score_ref, prob_ref,
-    cscore_ref, cprob_ref, qt_ref, qn_ref, gt_ref, gn_ref, att_t, dq_t,
+    cscore_ref, cprob_ref, slope_ref, cslope_ref, qt_ref, qn_ref, gt_ref, gn_ref, att_t, dq_t,
 ):
     step = pl.program_id(0)
     window, width = keys.shape
@@ -632,36 +725,40 @@
     query_t = query.T
     grad_t = grad_ref[...].T
     lane = lax.broadcasted_iota(jnp.int32, (QB, width), 1)
+    zero = jnp.zeros((width, QB), BF)
+    mine = [slice(head * HEAD_DIM, (head + 1) * HEAD_DIM) for head in range(heads)]
+    part = [slice(head * QB, (head + 1) * QB) for head in range(heads)]
     for head in range(heads):
-        mine = slice(head * HEAD_DIM, (head + 1) * HEAD_DIM)
-        qt_ref[head] = jnp.zeros((width, QB), BF)
-        qt_ref[head, mine, :] = query_t[mine, :]
-        gt_ref[head] = jnp.zeros((width, QB), BF)
+        qt_ref[:, part[head]] = zero
+        qt_ref[mine[head], part[head]] = query_t[mine[head], :]
+        gt_ref[:, part[head]] = zero
         in_head = (lane >= head * HEAD_DIM) & (lane < (head + 1) * HEAD_DIM)
-        qn_ref[head] = jnp.where(in_head, query, jnp.zeros_like(query))
+        qn_ref[part[head], :] = jnp.where(in_head, query, jnp.zeros_like(query))
     crop_row = qcrop_ref[...].reshape(1, QB)
-    ccrop = ccrop_ref[...]
-    same_context = jnp.concatenate([ccrop] * (QB // 128), axis=1) == crop_row
+    same_context = jnp.concatenate([ccrop_ref[...]] * (QB // 128), axis=1) == crop_row
 
     def span(block):
         return pl.ds(pl.multiple_of(first + block * KB, 128), KB)
 
+    def folded(values, combine):
+        return combine(values.reshape(-1, 8, QB), axis=0)
+
     largest = []
+    products = dot(ckey_ref[...], qt_ref[...], NN)
     for head in range(heads):
-        scores = jnp.where(same_context, dot(ckey_ref[...], qt_ref[head], NN), NEGATIVE)
-        cscore_ref[head] = scores
-        largest.append(jnp.max(scores.reshape(-1, 8, QB), axis=0))
+        scores = jnp.where(same_context, products[:, part[head]], NEGATIVE)
+        cscore_ref[:, part[head]] = scores
+        largest.append(folded(scores, jnp.max))
 
     def pass_one(block, carry):
         here = span(block)
-        crops = kcrop_ref[here, :]
-        same = jnp.concatenate([crops] * (QB // 128), axis=1) == crop_row
-        rows = keys[here, :]
+        same = jnp.concatenate([kcrop_ref[here, :]] * (QB // 128), axis=1) == crop_row
+        products = dot(keys[here, :], qt_ref[...], NN)
         out = []
         for head in range(heads):
-            scores = jnp.where(same, dot(rows, qt_ref[head], NN), NEGATIVE)
-            score_ref[head, block] = scores
-            out.append(jnp.maximum(carry[head], jnp.max(scores.reshape(-1, 8, QB), axis=0)))
+            scores = jnp.where(same, products[:, part[head]], NEGATIVE)
+            score_ref[block, :, part[head]] = scores
+            out.append(jnp.maximum(carry[head], folded(scores, jnp.max)))
         return tuple(out)
 
     largest = lax.fori_loop(0, blocks, pass_one, tuple(largest))
@@ -669,64 +766,54 @@
 
     sums = []
     for head in range(heads):
-        mine = slice(head * HEAD_DIM, (head + 1) * HEAD_DIM)
-        prob = jnp.exp(cscore_ref[head] - largest[head])
-        sums.append(jnp.sum(prob.reshape(-1, 8, QB), axis=0))
+        prob = jnp.exp(cscore_ref[:, part[head]] - largest[head])
+        sums.append(folded(prob, jnp.sum))
         low = prob.astype(BF)
-        cprob_ref[head] = low
-        att_t[mine, :] = dot(cval_ref[...], low, TN)[mine, :]
+        cprob_ref[:, part[head]] = low
+        att_t[mine[head], :] = dot(cval_ref[...], low, TN)[mine[head], :]
 
     def pass_two(block, carry):
         here = span(block)
         out = []
         for head in range(heads):
-            mine = slice(head * HEAD_DIM, (head + 1) * HEAD_DIM)
-            prob = jnp.exp(score_ref[head, block] - largest[head])
-            out.append(carry[head] + jnp.sum(prob.reshape(-1, 8, QB), axis=0))
+            prob = jnp.exp(score_ref[block, :, part[head]] - largest[head])
+            out.append(carry[head] + folded(prob, jnp.sum))
             low = prob.astype(BF)
-            prob_ref[head, block] = low
-            att_t[mine, :] += dot(values_t[mine, here], low, NN)
+            prob_ref[block, :, part[head]] = low
+            att_t[mine[head], :] += dot(values_t[mine[head], here], low, NN)
         return tuple(out)
 
     sums = lax.fori_loop(0, blocks, pass_two, tuple(sums))
     offsets = []
     for head in range(heads):
-        mine = slice(head * HEAD_DIM, (head + 1) * HEAD_DIM)
         inverse = 1.0 / jnp.sum(sums[head], axis=0, keepdims=True)
-        attended = att_t[mine, :] * inverse
-        att_t[mine, :] = attended
-        scaled = grad_t[mine, :].astype(F32) * inverse
-        gt_ref[head, mine, :] = scaled.astype(BF)
+        attended = att_t[mine[head], :] * inverse
+        att_t[mine[head], :] = attended
+        scaled = grad_t[mine[head], :].astype(F32) * inverse
+        gt_ref[mine[head], part[head]] = scaled.astype(BF)
         offsets.append(jnp.sum(scaled * attended, axis=0, keepdims=True))
-        gn_ref[head] = gt_ref[head].T
+        gn_ref[part[head], :] = gt_ref[:, part[head]].T
     att_ref[...] = att_t[...].T.astype(BF)
 
+    slope = dot(cval_ref[...], gt_ref[...], NN)
     for head in range(heads):
-        mine = slice(head * HEAD_DIM, (head + 1) * HEAD_DIM)
-        prob = cprob_ref[head]
-        slope = dot(cval_ref[...], gt_ref[head], NN)
-        dscore = (prob.astype(F32) * (slope - offsets[head])).astype(BF)
-        dcval_ref[...] += dot(prob, gn_ref[head], NN)
-        dckey_ref[...] += dot(dscore, qn_ref[head], NN)
-        dq_t[mine, :] = dot(ckey_ref[...], dscore, TN)[mine, :]
+        prob = cprob_ref[:, part[head]].astype(F32)
+        dscore = (prob * (slope[:, part[head]] - offsets[head])).astype(BF)
+        cslope_ref[:, part[head]] = dscore
+        dq_t[mine[head], :] = dot(ckey_ref[...], dscore, TN)[mine[head], :]
+    dcval_ref[...] += dot(cprob_ref[...], gn_ref[...], NN)
+    dckey_ref[...] += dot(cslope_ref[...], qn_ref[...], NN)
 
     def pass_three(block, carry):
         here = span(block)
-        rows = values[here, :]
-        value_sum = None
-        key_sum = None
+        slope = dot(values[here, :], gt_ref[...], NN)
         for head in range(heads):
-            mine = slice(head * HEAD_DIM, (head + 1) * HEAD_DIM)
-            prob = prob_ref[head, block]
-            slope = dot(rows, gt_ref[head], NN)
-            dscore = (prob.astype(F32) * (slope - offsets[head])).astype(BF)
-            value_part = dot(prob, gn_ref[head], NN)
-            key_part = dot(dscore, qn_ref[head], NN)
-            value_sum = value_part if value_sum is None else value_sum + value_part
-            key_sum = key_part if key_sum is None else key_sum + key_part
-            dq_t[mine, :] += dot(keys_t[mine, here], dscore, NN)
-        dvalues[here, :] += value_sum
-        dkeys[here, :] += key_sum
+            prob = prob_ref[block, :, part[head]].astype(F32)
+            dscore = (prob * (slope[:, part[head]] - offsets[head])).astype(BF)
+            slope_ref[:, part[head]] = dscore
+            dq_t[mine[head], :] += dot(keys_t[mine[head], here], dscore, NN)
+        dvalues[here, :] += dot(prob_ref[block], gn_ref[...], NN)
+        dkeys[here, :] += dot(slope_ref[...], qn_ref[...], NN)
         return carry
 
     lax.fori_loop(0, blocks, pass_three, 0)
@@ -782,14 +869,16 @@
                 pltpu.VMEM((window, width), F32),
                 pltpu.VMEM((window, width), F32),
                 pltpu.VMEM((window, 128), jnp.int32),
-                pltpu.VMEM((heads, most, KB, QB), F32),
-                pltpu.VMEM((heads, most, KB, QB), BF),
-                pltpu.VMEM((heads, context, QB), F32),
-                pltpu.VMEM((heads, context, QB), BF),
-                pltpu.VMEM((heads, width, QB), BF),
-                pltpu.VMEM((heads, QB, width), BF),
-                pltpu.VMEM((heads, width, QB), BF),
-                pltpu.VMEM((heads, QB, width), BF),
+                pltpu.VMEM((most, KB, heads * QB), F32),
+                pltpu.VMEM((most, KB, heads * QB), BF),
+                pltpu.VMEM((context, heads * QB), F32),
+                pltpu.VMEM((context, heads * QB), BF),
+                pltpu.VMEM((KB, heads * QB), BF),
+                pltpu.VMEM((context, heads * QB), BF),
+                pltpu.VMEM((width, heads * QB), BF),
+                pltpu.VMEM((heads * QB, width), BF),
+                pltpu.VMEM((width, heads * QB), BF),
+                pltpu.VMEM((heads * QB, width), BF),
                 pltpu.VMEM((width, QB), F32),
                 pltpu.VMEM((width, QB), F32),
             ],
@@ -828,6 +917,27 @@
 
 def gather_rows(value):
     return lax.all_gather(value, "pix", axis=0, tiled=True)
+
+
+def paired():
+    return lax.axis_size("ch") == 4 and lax.axis_size("pix") == 8
+
+
+def scatter_lines(value):
+    size = lax.axis_size("pix")
+    lines = [[2 * i + side for i in range(size // 2)] for side in range(2)]
+    return lax.psum_scatter(
+        value, "pix", scatter_dimension=0, tiled=True, axis_index_groups=lines
+    )
+
+
+def halves_to_send(blocks, side):
+    half = blocks[0].shape[1] // 2
+    sent = [
+        lax.dynamic_slice_in_dim(block[W:-W], (1 - side) * half, half, axis=1)
+        for block in blocks[::2]
+    ]
+    return jnp.concatenate(sent, axis=1)
 
 
 def scatter_rows(value):
@@ -956,9 +1066,6 @@
             axis=0,
         )
     )
-    embed_terms = summed[:crop_count]
-    ckey = summed[crop_count:, :width].astype(BF)
-    cval = summed[crop_count:, width:].astype(BF)
     bounds = jnp.cumsum(crop_rows)
     line = place * lines + jnp.arange(-(CROP_ROWS - 1), lines + CROP_ROWS - 1, dtype=jnp.int32)
     found = jnp.sum((line[:, None] >= bounds[None, :]).astype(jnp.int32), axis=1)
@@ -979,6 +1086,19 @@
         ]
     )
     rows = jnp.broadcast_to(rows[:, :, None], (6, lines, width))
+    if paired():
+        other = (place ^ 1) * lines + jnp.arange(-1, lines + 1, dtype=jnp.int32)
+        found = jnp.sum((other[:, None] >= bounds[None, :]).astype(jnp.int32), axis=1)
+        found = jnp.where((other >= 0) & (other < bounds[-1]), found, -1)
+        other_rows = jnp.stack(
+            [
+                (found[:-2] == found[1:-1]).astype(F32),
+                jnp.ones((lines,), F32),
+                (found[2:] == found[1:-1]).astype(F32),
+            ]
+        )
+        other_rows = jnp.broadcast_to(other_rows[:, :, None], (3, lines, width))
+        side = place % 2
     crop_end = jnp.sum(jnp.where(member > 0, bounds[None, :], 0), axis=1)
     crop_start = crop_end - sizes
     base = place * lines - (CROP_ROWS - 1)
@@ -999,6 +1119,8 @@
 
     ids = block_ids()
     home, away = chip_ids()
+    if paired():
+        half_ids = jnp.concatenate([ids, side.astype(jnp.int32)[None]])
     gain = [gains[i : i + 1] for i in range(3)]
     shift = [shifts[i : i + 1] for i in range(3)]
     inputs = unpack_rows(pixels).astype(F32)
@@ -1007,22 +1129,23 @@
     totals, *messages = stats(inputs, same)
     input_beside = beside_rows(messages)
     a_one, stats_one = norm(inputs, totals, *input_beside, rows, gain[0], shift[0])
-    far = far_blocks(a_one)
-    blocks = [a_one, to_mate(a_one)]
-    blocks, kernel_one, two_local = tie(blocks, kernel_one, two_local)
+    one_blocks, kernel_one, two_local, summed = tie(
+        gather_blocks(a_one), kernel_one, two_local, summed
+    )
+    embed_terms = summed[:crop_count]
+    ckey = summed[crop_count:, :width].astype(BF)
+    cval = summed[crop_count:, width:].astype(BF)
     kernel_two = gather_rows(two_local)
-    one_blocks, (c_one, totals, *messages) = convolve(blocks, far, ids, kernel_one, rows, same, ())
+    c_one, totals, *messages = convolve(one_blocks, ids, kernel_one, rows, same, ())
     growth = 1.0 + small(member, embed_terms[:, :width] + offsets[2])
     shift_add = small(member, embed_terms[:, width:] + offsets[3])
     mixed = (growth, shift_add)
     c_beside = beside_rows(messages)
     a_two, stats_two = norm(c_one, totals, *c_beside, rows, gain[1], shift[1], mixed)
-    far = far_blocks(a_two)
-    blocks = [a_two, to_mate(a_two)]
-    blocks, kernel_two, four = tie(blocks, kernel_two, four)
+    two_blocks, kernel_two, four = tie(gather_blocks(a_two), kernel_two, four)
     four = gather_rows(four)
-    two_blocks, (resid, totals, *messages) = convolve(
-        blocks, far, ids, kernel_two, rows, same, (inputs, offsets[0:1])
+    resid, totals, *messages = convolve(
+        two_blocks, ids, kernel_two, rows, same, (inputs, offsets[0:1])
     )
     resid_beside = beside_rows(messages)
     n_three, stats_three = norm(
@@ -1036,7 +1159,16 @@
     datt = project([first_dy] + dy_blocks[1:], ids, four, 3 * width, width)
     low = along_pix(qkv[tokens - HALO :, width:], 1)
     high = along_pix(qkv[:HALO, width:], -1)
-    att, dquery, dlow, down, dhigh, dckey, dcval = attend(qkv, datt, low, high, ckey, cval, tables)
+    low, high, one_blocks, two_blocks = tie(low, high, one_blocks, two_blocks)
+    if paired():
+        sent = [halves_to_send(blocks, side) for blocks in (one_blocks, two_blocks)]
+        sent, qkv, datt = tie(sent, qkv, datt)
+        sent = [across_pix(part, 1) for part in sent]
+    found = attend(qkv, datt, low, high, ckey, cval, tables)
+    if paired():
+        found, sent = tie(found, sent)
+        one_pairs, two_pairs = [(part, to_mate(part)) for part in sent]
+    att, dquery, dlow, down, dhigh, dckey, dcval = found
     from_prev, from_next = along_pix(dhigh, 1), along_pix(dlow, -1)
     arrived = sent_sums(chip_sums(spread(att, away, four, 3 * width)))
     result = resid + offsets[1:2]
@@ -1061,7 +1193,7 @@
         parts, resid, stats_three, gain[2], shift[2], same
     )
     e_beside = beside_rows(messages)
-    dresid, taps_two, *parts = gradient_taps(
+    dresid, taps_two, wide_two, *parts = gradient_taps(
         e_three, resid, resid_beside, stats_three, totals, *e_beside, rows, gain[2],
         (dy_low, *dy_beside), away, kernel_two,
     )
@@ -1070,15 +1202,21 @@
     arrived = sent_sums(sums_two)
     parts = spread(taps_two, home, kernel_two)
     taps_two, parts = tie(taps_two, parts)
-    dkernel_two = outer(two_blocks, ids, taps_two, W)
-    parts, arrived, dkernel_two, dmaps = tie(home_parts(parts), arrived, dkernel_two, dmaps)
+    if paired():
+        beside_two = across_pix(wide_two, 1)
+        dkernel_two = half_own(two_blocks, half_ids, taps_two)
+        dkernel_two = half_beside(two_pairs, half_ids, beside_two, other_rows, dkernel_two)
+    else:
+        dkernel_two = outer(two_blocks, ids, taps_two, W)
+    parts, arrived, dkernel_two = tie(home_parts(parts), arrived, dkernel_two)
     parts = parts + arrived
-    dkernel_two = scatter_rows(dkernel_two)
+    dkernel_two, dmaps = tie(dkernel_two, dmaps)
+    dkernel_two = scatter_lines(dkernel_two) if paired() else scatter_rows(dkernel_two)
     e_two, raw_two, totals, *messages = gradient_sums(
         parts, c_one, stats_two, gain[1], shift[1], same, mixed
     )
     e_beside = beside_rows(messages)
-    taps_one, *parts = gradient_taps(
+    taps_one, wide_one, *parts = gradient_taps(
         e_two, c_one, c_beside, stats_two, totals, *e_beside, rows, gain[1], None, away, kernel_one
     )
     sums_one = chip_sums(parts)
@@ -1086,12 +1224,17 @@
     arrived = sent_sums(sums_one)
     parts = spread(taps_one, home, kernel_one)
     taps_one, parts = tie(taps_one, parts)
-    dkernel_one = outer(one_blocks, ids, taps_one, W)
+    if paired():
+        beside_one = across_pix(wide_one, 1)
+        dkernel_one = half_own(one_blocks, half_ids, taps_one)
+        dkernel_one = half_beside(one_pairs, half_ids, beside_one, other_rows, dkernel_one)
+    else:
+        dkernel_one = outer(one_blocks, ids, taps_one, W)
     parts, arrived, dkernel_one, dkernel_two = tie(
         home_parts(parts), arrived, dkernel_one, dkernel_two
     )
     parts = parts + arrived
-    dkernel_one = scatter_rows(dkernel_one)
+    dkernel_one = scatter_lines(dkernel_one) if paired() else scatter_rows(dkernel_one)
     demb = jnp.concatenate(
         [turned(member, raw_two[1] * gain[1] + raw_two[0] * shift[1]), turned(member, raw_two[0])]
     )
@@ -1101,15 +1244,17 @@
     grad_pixels = last_gradient(
         e_one, inputs, stats_one, totals, *beside_rows(messages), rows, gain[0], dresid
     )
+    grad_pixels, raw_one = tie(grad_pixels, raw_one)
     sums = jnp.concatenate(
         [
+            raw_one[1].sum(0)[None],
             (raw_two[1] * growth).sum(0)[None],
             raw_three[1].sum(0)[None],
+            raw_one[0].sum(0)[None],
             (raw_two[0] * growth).sum(0)[None],
             raw_three[0].sum(0)[None],
             dresid.sum(0)[None],
             dy_low.astype(F32).sum(0)[None],
-            jnp.zeros((2, width), F32),
             demb,
             dckey,
             dcval,
@@ -1117,11 +1262,9 @@
         axis=0,
     )
     sums = pix_sum(sums)
-    last = pix_sum(raw_one.sum(1))
-    grad_gains = jnp.concatenate([last[1:2], sums[0:2]])
-    grad_shifts = jnp.concatenate([last[0:1], sums[2:4]])
+    grad_gains, grad_shifts = sums[0:3], sums[3:6]
     demb = sums[8 : 8 + 2 * crop_count].reshape(2, crop_count, width)
-    grad_offsets = jnp.concatenate([sums[4:6], demb.sum(1)])
+    grad_offsets = jnp.concatenate([sums[6:8], demb.sum(1)])
     dcontext = sums[8 + 2 * crop_count :].reshape(2, crop_count * CTX, width)
     own_condition = condition_own.astype(F32)
     grad_embedding = jnp.stack([turned(own_condition, demb[i]) for i in range(2)], axis=2)

time: 781 us -> 697 us (0.89)
  waiting for transfers between devices: 333 us -> 226 us
  starting transfers between devices: 86.9 us -> 102 us
    reduce_scatter x3 -> x1, waiting for transfers between devices: 60.2 us -> 0.46 us  [scatter_rows(): return lax.psum_scatter(value, 'pix', scatter_dimension=0, tiled=True)]
    all_gather x3, waiting for transfers between devices: 73.3 us -> 30.9 us  [gather_rows(): return lax.all_gather(value, 'pix', axis=0, tiled=True)]
    pallas_call x0 -> x4, Pallas kernels: none -> 40.2 us  [the longest x2 20.3 us: half_beside(): pl.pallas_call(functools.partial(half_beside_body, count), out_shape=jax....]
    pallas_call x4 -> x2, Pallas kernels: 39.7 us -> 13.2 us  [outer(): pl.pallas_call(functools.partial(outer_body, count, shift), out_shape=jax...]
    ppermute x9 -> x10, starting transfers between devices: 7.16 us -> 26.7 us  [across_pix(): lax.ppermute(value, 'pix', [(i, i ^ bit) for i in range(lax.axis_size('pi...]
    ppermute x8, waiting for transfers between devices: 49.7 us -> 66 us  [to_chip(): lax.ppermute(value, 'ch', [(i, (i + 2 * by) % size) for i in range(size)])]
    pallas_call x1, Pallas kernels: 61.6 us -> 52 us  [attend(): pl.pallas_call(functools.partial(attention_body, heads), out_shape=shapes...]
    ppermute x18, waiting for transfers between devices: 75.2 us -> 67.2 us  [along_pix(): lax.ppermute(value, 'pix', [(i, i + by) for i in range(size) if 0 <= i +...]
  transfers between devices with their start and end apart: 57 -> 60, of which waited for: 35 -> 27; matrix products, arithmetic and copies ran while one was open for 9% -> 11% of each run, Pallas kernels for 21% -> 33%
where the time goes in v2:
time: 697 us; the launch traced here: 694 us
  Pallas kernels  243 us (35%)
  waiting for transfers between devices  226 us (32%)
  starting transfers between devices  102 us (15%)
  local copies, waits for them, and re-layouts  80.1 us (11%)
  other arithmetic  24.2 us (3%)
  between operations  15.8 us (2%)
    ppermute x18, waiting for transfers between devices, along_pix(): lax.ppermute(value, 'pix', [(i, i + by) for i in range(size) if 0 <= i +...  67.2 us
    ppermute x8, waiting for transfers between devices, to_chip(): lax.ppermute(value, 'ch', [(i, (i + 2 * by) % size) for i in range(size)])  66 us
    ppermute x18, starting transfers between devices, along_pix(): lax.ppermute(value, 'pix', [(i, i + by) for i in range(size) if 0 <= i +...  62.8 us
    ppermute x10, waiting for transfers between devices, across_pix(): lax.ppermute(value, 'pix', [(i, i ^ bit) for i in range(lax.axis_size('pi...  53.8 us
    pallas_call x1, Pallas kernels, attend(): pl.pallas_call(functools.partial(attention_body, heads), out_shape=shapes...  52 us
    pallas_call x4, Pallas kernels, conv_pair(): pl.pallas_call(functools.partial(conv_body, prior is not None, None if re...  35.7 us
    pallas_call x6, Pallas kernels, spread(): pl.pallas_call(spread_body, out_shape=[jax.ShapeDtypeStruct((count, token...  35.2 us
    all_gather x3, waiting for transfers between devices, gather_rows(): return lax.all_gather(value, 'pix', axis=0, tiled=True)  30.9 us
  transfers between devices with their start and end apart: 60, of which 27 were waited for; matrix products, arithmetic and copies ran while one was open for 11% of the time, Pallas kernels for 33%

profile of v2, /device:TPU:0, one launch (start us, length us, event | category | flops | bytes accessed | tf_op | source)
XLA Modules:
  0.0 693.6 jit_solution(3692721163012608387)
XLA Ops:
  12.3 4.0 reshape.186
  16.3 5.5 copy.58
  22.5 3.4 stats.1
  26.0 5.1 collective-permute-start
  38.0 3.3 norm.3
  44.7 15.6 %collective-permute-done.3.refs_0_.refs_2_ = bf16[1600,256]{1,0:T(8,128)(2,1)S(1)} collective-permute-done((bf16[1600,256]{1,0:T(8,128)(2,1)}, bf16[1600,256]{1,0:T(8,128)(2,1)S(1)}, u32[]{:S(2)}, u32[]{:S(2)}) %collective-permute-start.3) | collective-permute-done | bytes 819232 | tf_op jit(solution)/shard_map/ppermute | solution.py:915
  60.4 4.3 collective-permute-start.5
  64.7 8.5 %collective-permute-done.5 = f32[80,512]{1,0:T(8,128)S(1)} collective-permute-done((f32[80,512]{1,0:T(8,128)S(1)}, f32[80,512]{1,0:T(8,128)S(1)}, u32[]{:S(2)}, u32[]{:S(2)}) %collective-permute-start.5) | collective-permute-done | bytes 163872 | tf_op jit(solution)/shard_map/ppermute | solution.py:898
  75.0 7.6 %collective-permute-done.6 = f32[80,512]{1,0:T(8,128)S(1)} collective-permute-done((f32[80,512]{1,0:T(8,128)S(1)}, f32[80,512]{1,0:T(8,128)S(1)}, u32[]{:S(2)}, u32[]{:S(2)}) %collective-permute-start.6) | collective-permute-done | bytes 163872 | tf_op jit(solution)/shard_map/ppermute | solution.py:898
  84.4 17.7 %collective-permute-done.7 = f32[80,512]{1,0:T(8,128)S(1)} collective-permute-done((f32[80,512]{1,0:T(8,128)S(1)}, f32[80,512]{1,0:T(8,128)S(1)}, u32[]{:S(2)}, u32[]{:S(2)}) %collective-permute-start.7) | collective-permute-done | bytes 163872 | tf_op jit(solution)/shard_map/ppermute | solution.py:898
  107.0 8.1 %conv_pair.4.refs_4_ = f32[1536,256]{1,0:T(8,128)} custom-call(s32[2]{0:T(128)} %pad_add_fusion.1.ids, bf16[1600,256]{1,0:T(8,128)(2,1)} %get-tuple-element.174.refs_0_, bf16[1600,256]{1,0:T(8,128)(2,1)} %collective-permute-done.2.refs_1_, bf16[1024,2304]{1,0:T(8,128)(2,1)} %all-gather.4.cloned.1.call-done.refs_2_.refs_10_.refs_0_, ...), custom_call_target="tpu_custom_call" | custom-call | flops 3623878656 | bytes 7077888 | tf_op jit(solution)/shard_map/conv_pair/pallas_call | solution.py:465
  115.0 9.4 %conv_pair.5 = (f32[1536,256]{1,0:T(8,128)}, f32[2,48,256]{2,1,0:T(8,128)}, f32[40,256]{1,0:T(8,128)}, f32[40,256]{1,0:T(8,128)}) custom-call(s32[2]{0:T(128)} %pad_add_fusion.ids, bf16[1600,256]{1,0:T(8,128)(2,1)} %copy-done.8, bf16[1600,256]{1,0:T(8,128)(2,1)} %collective-permute-done.4.refs_1_.refs_3_, ...), custom_call_target="tpu_custom_call" | custom-call | flops 3623878656 | bytes 7077888 | tf_op jit(solution)/shard_map/conv_pair/pallas_call | solution.py:465
  130.0 3.1 collective-permute-done.9.refs_3_
  133.8 3.3 norm.4
  138.5 17.4 %collective-permute-done.11.refs_0_.refs_2_ = bf16[1600,256]{1,0:T(8,128)(2,1)S(1)} collective-permute-done((bf16[1600,256]{1,0:T(8,128)(2,1)}, bf16[1600,256]{1,0:T(8,128)(2,1)S(1)}, u32[]{:S(2)}, u32[]{:S(2)}) %collective-permute-start.11) | collective-permute-done | bytes 819232 | tf_op jit(solution)/shard_map/ppermute | solution.py:915
  158.3 28.2 %all-gather.6.cloned.1.call-done.refs_2_.refs_13_.refs_0_ = bf16[1024,2304]{1,0:T(8,128)(2,1)} async-done(((bf16[128,2304]{1,0:T(8,128)(2,1)}), bf16[1024,2304]{1,0:T(8,128)(2,1)}) %all-gather.6.cloned.1.call-update) | async-done | bytes 4718608 | tf_op jit(solution)/shard_map/all_gather | solution.py:919
  186.8 8.1 %conv_pair.6.refs_4_ = f32[1536,256]{1,0:T(8,128)} custom-call(s32[2]{0:T(128)} %pad_add_fusion.1.ids, bf16[1600,256]{1,0:T(8,128)(2,1)} %get-tuple-element.176.refs_0_, bf16[1600,256]{1,0:T(8,128)(2,1)} %copy-done.18, bf16[1024,2304]{1,0:T(8,128)(2,1)} %all-gather.6.cloned.1.call-done.refs_2_.refs_13_.refs_0_, ...), custom_call_target="tpu_custom_call" | custom-call | flops 3623878656 | bytes 7077888 | tf_op jit(solution)/shard_map/conv_pair/pallas_call | solution.py:465
  194.9 10.1 %conv_pair.7 = (f32[1536,256]{1,0:T(8,128)}, f32[2,48,256]{2,1,0:T(8,128)}, f32[40,256]{1,0:T(8,128)}, f32[40,256]{1,0:T(8,128)}) custom-call(s32[2]{0:T(128)} %pad_add_fusion.ids, bf16[1600,256]{1,0:T(8,128)(2,1)} %copy-done.11, bf16[1600,256]{1,0:T(8,128)(2,1)} %copy-done.19, bf16[1024,2304]{1,0:T(8,128)(2,1)} %all-gather.6.cloned.1.call-done.refs_2_.refs_13_.refs_0_, ...), custom_call_target="tpu_custom_call" | custom-call | flops 3623878656 | bytes 7077888 | tf_op jit(solution)/shard_map/conv_pair/pallas_call | solution.py:465
  208.9 3.6 reshape.153
  212.5 3.1 copy.57
  220.8 16.6 %collective-permute-done.16.refs_2_ = bf16[1536,256]{1,0:T(8,128)(2,1)S(1)} collective-permute-done((bf16[1536,256]{1,0:T(8,128)(2,1)}, bf16[1536,256]{1,0:T(8,128)(2,1)S(1)}, u32[]{:S(2)}, u32[]{:S(2)}) %collective-permute-start.16) | collective-permute-done | bytes 786464 | tf_op jit(solution)/shard_map/ppermute | solution.py:915
  240.4 7.3 %project.2.query_ref.own_ref = bf16[1536,768]{1,0:T(8,128)(2,1)} custom-call(s32[4]{0:T(128)} %pad_add_fusion.2.ids, bf16[1536,256]{1,0:T(8,128)(2,1)} %get-tuple-element.171.refs_0_, bf16[1536,256]{1,0:T(8,128)(2,1)} %copy-done.71, bf16[1536,256]{1,0:T(8,128)(2,1)} %copy-done.70, bf16[1536,256]{1,0:T(8,128)(2,1)} %collective-permute-done.17.refs_3_, ...), custom_call_target="tpu_custom_call" | custom-call | flops 2415919104 | bytes 3932160 | tf_op jit(solution)/shard_map/project/pallas_call | solution.py:514
  250.7 5.2 collective-permute-start.18
  262.1 5.1 project.3.grad_ref
  267.2 32.0 %collective-permute-done.18.low_ref = bf16[992,512]{1,0:T(8,128)(2,1)} collective-permute-done((bf16[992,512]{1,0:T(8,128)(2,1)}, bf16[992,512]{1,0:T(8,128)(2,1)}, u32[]{:S(2)}, u32[]{:S(2)}) %collective-permute-start.18) | collective-permute-done | bytes 1015840 | tf_op jit(solution)/shard_map/ppermute | solution.py:894
  307.7 52.0 %attend.1 = (bf16[1536,256]{1,0:T(8,128)(2,1)}, bf16[1536,256]{1,0:T(8,128)(2,1)}, bf16[992,512]{1,0:T(8,128)(2,1)}, f32[1536,512]{1,0:T(8,128)}, bf16[992,512]{...) custom-call(s32[6]{0:T(128)} %get-tuple-element.305.starts, s32[6]{0:T(128)} %get-tuple-element.304.counts, ...), custom_call_target="tpu_custom_call" | custom-call | flops 2013265920 | bytes 7864320 | tf_op jit(solution)/shard_map/attend/pallas_call | solution.py:854
  359.7 3.5 spread.7
  363.2 3.6 spread.6
  368.3 3.4 collective-permute-start.25
  373.2 5.3 outer.2
  378.5 8.6 %collective-permute-done.29 = bf16[1536,256]{1,0:T(8,128)(2,1)S(1)} collective-permute-done((bf16[1536,256]{1,0:T(8,128)(2,1)S(1)}, bf16[1536,256]{1,0:T(8,128)(2,1)S(1)}, u32[]{:S(2)}, u32[]{:S(2)}) %collective-permute-start.29) | collective-permute-done | bytes 786464 | tf_op jit(solution)/shard_map/ppermute | solution.py:915
  389.5 3.9 copy.69
  393.4 6.2 reshape.163
  399.7 15.0 %collective-permute-done.25 = bf16[992,512]{1,0:T(8,128)(2,1)} collective-permute-done((bf16[992,512]{1,0:T(8,128)(2,1)}, bf16[992,512]{1,0:T(8,128)(2,1)}, u32[]{:S(2)}, u32[]{:S(2)}) %collective-permute-start.25) | collective-permute-done | bytes 1015840 | tf_op jit(solution)/shard_map/ppermute | solution.py:894
  418.4 4.8 spread.8
  427.0 4.8 spread.9
  433.1 7.9 %outer.3 = bf16[1024,768]{1,0:T(8,128)(2,1)} custom-call(s32[4]{0:T(128)} %pad_add_fusion.2.ids, bf16[1536,256]{1,0:T(8,128)(2,1)} %get-tuple-element.171.refs_0_, bf16[1536,256]{1,0:T(8,128)(2,1)} %copy-done.71, bf16[1536,256]{1,0:T(8,128)(2,1)} %copy-done.70, bf16[1536,256]{1,0:T(8,128)(2,1)} %collective-permute-done.17.refs_3_, ...), custom_call_target="tpu_custom_call" | custom-call | flops 2415919104 | bytes 3932160 | tf_op jit(solution)/shard_map/outer/pallas_call | solution.py:672
  444.0 7.8 %collective-permute-done.32.refs_2_ = bf16[1536,256]{1,0:T(8,128)(2,1)S(1)} collective-permute-done((bf16[1536,256]{1,0:T(8,128)(2,1)S(1)}, bf16[1536,256]{1,0:T(8,128)(2,1)S(1)}, u32[]{:S(2)}, u32[]{:S(2)}) %collective-permute-start.32) | collective-permute-done | bytes 786464 | tf_op jit(solution)/shard_map/ppermute | solution.py:915
  452.7 4.5 gradient_sums.3
  457.2 4.4 collective-permute-start.33
  463.6 17.5 %collective-permute-start.35 = (bf16[32,256]{1,0:T(8,128)(2,1)S(1)}, bf16[32,256]{1,0:T(8,128)(2,1)S(1)}, u32[]{:S(2)}, u32[]{:S(2)}) collective-permute-start(bf16[32,256]{1,0:T(8,128)(2,1)S(1)} %get-tuple-element.311), channel_id=1, source_target_pairs={{0,4},{4,8},{8,12},{12,16},{16,20},{20,24},{24,28},{1,5},{5,9},{9,... | collective-permute-start | bytes 49160 | tf_op jit(solution)/shard_map/ppermute | solution.py:894
  482.6 5.0 collective-permute-done.36.refs_12_
  488.2 11.1 %gradient_taps.2 = (f32[1536,256]{1,0:T(8,128)}, bf16[1536,2304]{1,0:T(8,128)(2,1)}, bf16[1600,256]{1,0:T(8,128)(2,1)}, bf16[1,1536,256]{2,1,0:T(8,128)(2,1)}, bf16[1,1536,256]{2,1,0:T(8,128)(2,1)}) custom-call(s32[2]{0:T(128)} %pad_add_fusion.3.ids, f32[1536,256]{1,0:T(8,128)} %get-tuple-element.218.refs_0_, ...), custom_call_target="tpu_custom_call" | custom-call | flops 1811939328 | bytes 14155776 | tf_op jit(solution)/shard_map/gradient_taps/pallas_call | solution.py:351
  501.3 7.5 %collective-permute-start.41 = (bf16[1600,256]{1,0:T(8,128)(2,1)}, bf16[1600,256]{1,0:T(8,128)(2,1)S(1)}, u32[]{:S(2)}, u32[]{:S(2)}) collective-permute-start(bf16[1600,256]{1,0:T(8,128)(2,1)} %get-tuple-element.232), channel_id=1, source_target_pairs={{0,4},{4,0},{8,12},{12,8},{16,20},{20,16},{24,28},{28,24},{1,5},{5... | collective-permute-start | bytes 2457608 | tf_op jit(solution)/shard_map/ppermute | solution.py:898
  510.1 9.3 %spread.10 = (bf16[1,1536,256]{2,1,0:T(8,128)(2,1)}, bf16[1,1536,256]{2,1,0:T(8,128)(2,1)}) custom-call(s32[2]{0:T(128)} %pad_add_fusion.1.ids, bf16[1536,2304]{1,0:T(8,128)(2,1)} %get-tuple-element.235.grad_ref.refs_4_, bf16[1024,2304]{1,0:T(8,128)(2,1)} %all-gather.6.cloned.1.call-done.refs_2_.refs_13_.refs_0_), custom_call_target="tpu_custom_call" | custom-call | flops 3623878656 | bytes 8257536 | tf_op jit(solution)/shard_map/spread/pallas_call | solution.py:541
  520.0 10.0 %half_own.2.refs_4_ = f32[512,2304]{1,0:T(8,128)} custom-call(s32[5]{0:T(128)} %concatenate.37.ids, bf16[1600,256]{1,0:T(8,128)(2,1)} %get-tuple-element.176.refs_0_, bf16[1600,256]{1,0:T(8,128)(2,1)} %copy-done.18, bf16[1600,256]{1,0:T(8,128)(2,1)} %copy-done.11, bf16[1600,256]{1,0:T(8,128)(2,1)} %copy-done.19, ...), custom_call_target="tpu_custom_call" | custom-call | flops 3623878656 | bytes 11796480 | tf_op jit(solution)/shard_map/half_own/pallas_call | solution.py:580
  531.5 10.1 %half_beside.2 = bf16[512,2304]{1,0:T(8,128)(2,1)} custom-call(s32[5]{0:T(128)} %concatenate.37.ids, bf16[1536,256]{1,0:T(8,128)(2,1)} %collective-permute-done.24.refs_0_, bf16[1536,256]{1,0:T(8,128)(2,1)} %copy-done.72, bf16[1600,256]{1,0:T(8,128)(2,1)} %copy-done.66, f32[3,48,256]{2,1,0:T(8,128)} %broadcast_in_dim.102.refs_3_, f32[512,2304]{1,0:T(8,128)} %half_own.2.refs_4_), custom_call_target="tpu_custom_call" | custom-call | flops 3623878656 | bytes 14155776 | tf_op jit(solution)/shard_map/half_beside/pallas_call | solution.py:624
  542.8 5.3 gradient_sums.4
  548.2 4.3 collective-permute-start.42
  554.4 6.6 collective-permute-done.43.refs_7_
  561.6 10.8 %gradient_taps.3 = (bf16[1536,2304]{1,0:T(8,128)(2,1)}, bf16[1600,256]{1,0:T(8,128)(2,1)}, bf16[1,1536,256]{2,1,0:T(8,128)(2,1)}, bf16[1,1536,256]{2,1,0:T(8,128)(2,1)}) custom-call(s32[2]{0:T(128)} %pad_add_fusion.3.ids, f32[1536,256]{1,0:T(8,128)} %get-tuple-element.240.refs_0_, f32[1536,256]{1,0:T(8,128)} %get-tuple-element.153.refs_0_.refs_3_.refs_1_, ...), custom_call_target="tpu_custom_call" | custom-call | flops 1811939328 | bytes 14155776 | tf_op jit(solution)/shard_map/gradient_taps/pallas_call | solution.py:351
  572.9 5.1 collective-permute-start.48
  579.4 9.2 %spread.11 = (bf16[1,1536,256]{2,1,0:T(8,128)(2,1)}, bf16[1,1536,256]{2,1,0:T(8,128)(2,1)}) custom-call(s32[2]{0:T(128)} %pad_add_fusion.1.ids, bf16[1536,2304]{1,0:T(8,128)(2,1)} %get-tuple-element.257.grad_ref.refs_4_, bf16[1024,2304]{1,0:T(8,128)(2,1)} %all-gather.4.cloned.1.call-done.refs_2_.refs_10_.refs_0_), custom_call_target="tpu_custom_call" | custom-call | flops 3623878656 | bytes 8257536 | tf_op jit(solution)/shard_map/spread/pallas_call | solution.py:541
  589.3 10.0 %half_own.3.refs_4_ = f32[512,2304]{1,0:T(8,128)} custom-call(s32[5]{0:T(128)} %concatenate.37.ids, bf16[1600,256]{1,0:T(8,128)(2,1)} %get-tuple-element.174.refs_0_, bf16[1600,256]{1,0:T(8,128)(2,1)} %collective-permute-done.2.refs_1_, bf16[1600,256]{1,0:T(8,128)(2,1)} %copy-done.8, bf16[1600,256]{1,0:T(8,128)(2,1)} %collective-permute-done.4.refs_1_.refs_3_, ...), custom_call_target="tpu_custom_call" | custom-call | flops 3623878656 | bytes 11796480 | tf_op jit(solution)/shard_map/half_own/pallas_call | solution.py:580
  601.1 10.2 %half_beside.3 = bf16[512,2304]{1,0:T(8,128)(2,1)} custom-call(s32[5]{0:T(128)} %concatenate.37.ids, bf16[1536,256]{1,0:T(8,128)(2,1)} %copy-done.68, bf16[1536,256]{1,0:T(8,128)(2,1)} %copy-done.73, bf16[1600,256]{1,0:T(8,128)(2,1)} %copy-done.67, f32[3,48,256]{2,1,0:T(8,128)} %broadcast_in_dim.102.refs_3_, f32[512,2304]{1,0:T(8,128)} %half_own.3.refs_4_), custom_call_target="tpu_custom_call" | custom-call | flops 3623878656 | bytes 14155776 | tf_op jit(solution)/shard_map/half_beside/pallas_call | solution.py:624
  614.9 5.2 gradient_sums.5
  620.0 4.8 collective-permute-start.49
  626.8 4.1 collective-permute-done.50.after_ref
  631.6 4.3 last_gradient.1
  636.0 4.0 collective-permute-start.51
  640.0 4.6 collective-permute-done.51
  645.2 14.8 %collective-permute-done.52 = f32[168,256]{1,0:T(8,128)S(1)} collective-permute-done((f32[168,256]{1,0:T(8,128)S(1)}, f32[168,256]{1,0:T(8,128)S(1)}, u32[]{:S(2)}, u32[]{:S(2)}) %collective-permute-start.52) | collective-permute-done | bytes 172064 | tf_op jit(solution)/shard_map/ppermute | solution.py:898
  660.2 3.9 copy.70
  664.1 6.1 reshape.165
  (369 shorter events, 122.4 us)
Async XLA Ops:
  7.2 97.6 %all-gather.4.cloned.1.call-start = ((), (), s32[]{:S(2)}) async-start(), calls=%async_computation.3 | async-start | bytes 5308416 | tf_op jit(solution)/shard_map/all_gather | solution.py:919
  10.8 175.8 %all-gather.6.cloned.1.call-start = ((), (), s32[]{:S(2)}) async-start(), calls=%async_computation.4 | async-start | bytes 5308416 | tf_op jit(solution)/shard_map/all_gather | solution.py:919
  26.0 10.2 %collective-permute-start = (f32[40,256]{1,0:T(8,128)}, f32[40,256]{1,0:T(8,128)S(1)}, u32[]{:S(2)}, u32[]{:S(2)}) collective-permute-start(f32[40,256]{1,0:T(8,128)} %get-tuple-element.145), channel_id=1, source_target_pairs={{0,4},{4,8},{8,12},{12,16},{16,20},{20,24},{24,28},{1,5},{5,9},{9,... | collective-permute-start | bytes 122888 | tf_op jit(solution)/shard_map/ppermute | solution.py:894
  31.1 6.1 collective-permute-start.1
  41.2 19.1 %collective-permute-start.3 = (bf16[1600,256]{1,0:T(8,128)(2,1)}, bf16[1600,256]{1,0:T(8,128)(2,1)S(1)}, u32[]{:S(2)}, u32[]{:S(2)}) collective-permute-start(bf16[1600,256]{1,0:T(8,128)(2,1)} %get-tuple-element.174.refs_0_), channel_id=1, source_target_pairs={{0,2},{1,3},{2,0},{3,1},{4,6},{5,7},{6,4},{7,5},{8,10},{9,11},{10,... | collective-permute-start | bytes 2457608 | tf_op jit(solution)/shard_map/ppermute | solution.py:915
  44.6 57.5 %collective-permute-start.2 = (bf16[1600,256]{1,0:T(8,128)(2,1)S(1)}, bf16[1600,256]{1,0:T(8,128)(2,1)}, u32[]{:S(2)}, u32[]{:S(2)}) collective-permute-start(bf16[1600,256]{1,0:T(8,128)(2,1)S(1)} %copy-done.6), channel_id=1, source_target_pairs={{0,1},{1,0},{2,3},{3,2},{4,5},{5,4},{6,7},{7,6},{8,9},{9,8},{10,11... | collective-permute-start | bytes 2457608 | tf_op jit(solution)/shard_map/ppermute | solution.py:910
  60.4 44.5 %copy-start.8 = (bf16[1600,256]{1,0:T(8,128)(2,1)}, bf16[1600,256]{1,0:T(8,128)(2,1)S(1)}, u32[]{:S(2)}) copy-start(bf16[1600,256]{1,0:T(8,128)(2,1)S(1)} %collective-permute-done.3.refs_0_.refs_2_) | copy-start | bytes 2457604
  60.4 41.8 %collective-permute-start.4 = (bf16[1600,256]{1,0:T(8,128)(2,1)S(1)}, bf16[1600,256]{1,0:T(8,128)(2,1)}, u32[]{:S(2)}, u32[]{:S(2)}) collective-permute-start(bf16[1600,256]{1,0:T(8,128)(2,1)S(1)} %collective-permute-done.3.refs_0_.refs_2_), channel_id=1, source_target_pairs={{0,1},{1,0},{2,3},{3,2},{4,5},{5,4},{6,7},{7,6},{8,9},{9,8},{10,11... | collective-permute-start | bytes 2457608 | tf_op jit(solution)/shard_map/ppermute | solution.py:910
  60.4 46.0 %copy-start.57 = (f32[4,256]{1,0:T(4,128)S(1)}, f32[4,256]{1,0:T(4,128)}, u32[]{:S(2)}) copy-start(f32[4,256]{1,0:T(4,128)} %param.21) | copy-start | bytes 12292
  60.4 12.8 %collective-permute-start.5 = (f32[80,512]{1,0:T(8,128)S(1)}, f32[80,512]{1,0:T(8,128)S(1)}, u32[]{:S(2)}, u32[]{:S(2)}) collective-permute-start(f32[80,512]{1,0:T(8,128)S(1)} %pad_maximum_fusion.6), channel_id=1, source_target_pairs={{0,4},{4,0},{8,12},{12,8},{16,20},{20,16},{24,28},{28,24},{1,5},{5... | collective-permute-start | bytes 491528 | tf_op jit(solution)/shard_map/ppermute | solution.py:898
  73.2 9.4 %collective-permute-start.6 = (f32[80,512]{1,0:T(8,128)S(1)}, f32[80,512]{1,0:T(8,128)S(1)}, u32[]{:S(2)}, u32[]{:S(2)}) collective-permute-start(f32[80,512]{1,0:T(8,128)S(1)} %fusion.61), channel_id=1, source_target_pairs={{0,8},{4,12},{8,0},{12,4},{16,24},{20,28},{24,16},{28,20},{1,9},{5... | collective-permute-start | bytes 491528 | tf_op jit(solution)/shard_map/ppermute | solution.py:898
  82.6 19.5 %collective-permute-start.7 = (f32[80,512]{1,0:T(8,128)S(1)}, f32[80,512]{1,0:T(8,128)S(1)}, u32[]{:S(2)}, u32[]{:S(2)}) collective-permute-start(f32[80,512]{1,0:T(8,128)S(1)} %add.183), channel_id=1, source_target_pairs={{0,16},{4,20},{8,24},{12,28},{16,0},{20,4},{24,8},{28,12},{1,17},{... | collective-permute-start | bytes 491528 | tf_op jit(solution)/shard_map/ppermute | solution.py:898
  104.9 135.0 %all-gather.8.cloned.1.call-start = ((), (), s32[]{:S(2)}) async-start(), calls=%async_computation.5 | async-start | bytes 2359296 | tf_op jit(solution)/shard_map/all_gather | solution.py:919
  124.5 5.6 collective-permute-start.8
  127.1 6.1 collective-permute-start.9
  137.1 18.9 %collective-permute-start.11 = (bf16[1600,256]{1,0:T(8,128)(2,1)}, bf16[1600,256]{1,0:T(8,128)(2,1)S(1)}, u32[]{:S(2)}, u32[]{:S(2)}) collective-permute-start(bf16[1600,256]{1,0:T(8,128)(2,1)} %get-tuple-element.176.refs_0_), channel_id=1, source_target_pairs={{0,2},{1,3},{2,0},{3,1},{4,6},{5,7},{6,4},{7,5},{8,10},{9,11},{10,... | collective-permute-start | bytes 2457608 | tf_op jit(solution)/shard_map/ppermute | solution.py:915
  138.5 18.4 %collective-permute-start.10 = (bf16[1600,256]{1,0:T(8,128)(2,1)}, bf16[1600,256]{1,0:T(8,128)(2,1)S(1)}, u32[]{:S(2)}, u32[]{:S(2)}) collective-permute-start(bf16[1600,256]{1,0:T(8,128)(2,1)} %get-tuple-element.176.refs_0_), channel_id=1, source_target_pairs={{0,1},{1,0},{2,3},{3,2},{4,5},{5,4},{6,7},{7,6},{8,9},{9,8},{10,11... | collective-permute-start | bytes 2457608 | tf_op jit(solution)/shard_map/ppermute | solution.py:910
  155.9 2.3 collective-permute-start.12
  186.5 355.6 %reduce-scatter.4.cloned.1.call-start = ((), (), s32[]{:S(2)}) async-start(), calls=%async_computation.6 | async-start | bytes 2359296 | tf_op jit(solution)/shard_map/reduce_scatter | solution.py:944
  205.0 10.6 %collective-permute-start.13 = (f32[40,256]{1,0:T(8,128)}, f32[40,256]{1,0:T(8,128)S(1)}, u32[]{:S(2)}, u32[]{:S(2)}) collective-permute-start(f32[40,256]{1,0:T(8,128)} %get-tuple-element.167), channel_id=1, source_target_pairs={{0,4},{4,8},{8,12},{12,16},{16,20},{20,24},{24,28},{1,5},{5,9},{9,... | collective-permute-start | bytes 122888 | tf_op jit(solution)/shard_map/ppermute | solution.py:894
  207.6 8.1 %collective-permute-start.14 = (f32[40,256]{1,0:T(8,128)}, f32[40,256]{1,0:T(8,128)S(1)}, u32[]{:S(2)}, u32[]{:S(2)}) collective-permute-start(f32[40,256]{1,0:T(8,128)} %get-tuple-element.168), channel_id=1, source_target_pairs={{4,0},{8,4},{12,8},{16,12},{20,16},{24,20},{28,24},{5,1},{9,5},{13... | collective-permute-start | bytes 122888 | tf_op jit(solution)/shard_map/ppermute | solution.py:894
  215.7 42.1 %copy-start.2 = (bf16[48,256,32]{1,2,0:T(8,128)(2,1)}, bf16[48,256,32]{1,2,0:T(8,128)(2,1)S(1)}, u32[]{:S(2)}) copy-start(bf16[48,256,32]{1,2,0:T(8,128)(2,1)S(1)} %copy.57) | copy-start | bytes 2359300
  219.2 18.2 %collective-permute-start.16 = (bf16[1536,256]{1,0:T(8,128)(2,1)}, bf16[1536,256]{1,0:T(8,128)(2,1)S(1)}, u32[]{:S(2)}, u32[]{:S(2)}) collective-permute-start(bf16[1536,256]{1,0:T(8,128)(2,1)} %get-tuple-element.171.refs_0_), channel_id=1, source_target_pairs={{0,2},{1,3},{2,0},{3,1},{4,6},{5,7},{6,4},{7,5},{8,10},{9,11},{10,... | collective-permute-start | bytes 2359304 | tf_op jit(solution)/shard_map/ppermute | solution.py:915
  220.8 18.8 %collective-permute-start.15 = (bf16[1536,256]{1,0:T(8,128)(2,1)}, bf16[1536,256]{1,0:T(8,128)(2,1)S(1)}, u32[]{:S(2)}, u32[]{:S(2)}) collective-permute-start(bf16[1536,256]{1,0:T(8,128)(2,1)} %get-tuple-element.171.refs_0_), channel_id=1, source_target_pairs={{0,1},{1,0},{2,3},{3,2},{4,5},{5,4},{6,7},{7,6},{8,9},{9,8},{10,11... | collective-permute-start | bytes 2359304 | tf_op jit(solution)/shard_map/ppermute | solution.py:910
  237.4 2.4 collective-permute-start.17
  237.4 20.4 %collective-permute-start.21 = (bf16[1536,256]{1,0:T(8,128)(2,1)S(1)}, bf16[1536,256]{1,0:T(8,128)(2,1)S(1)}, u32[]{:S(2)}, u32[]{:S(2)}) collective-permute-start(bf16[1536,256]{1,0:T(8,128)(2,1)S(1)} %bitcast.157), channel_id=1, source_target_pairs={{0,2},{1,3},{2,0},{3,1},{4,6},{5,7},{6,4},{7,5},{8,10},{9,11},{10,... | collective-permute-start | bytes 2359304 | tf_op jit(solution)/shard_map/ppermute | solution.py:915
  250.7 48.4 %collective-permute-start.18 = (bf16[992,512]{1,0:T(8,128)(2,1)}, bf16[992,512]{1,0:T(8,128)(2,1)}, u32[]{:S(2)}, u32[]{:S(2)}) collective-permute-start(bf16[992,512]{1,0:T(8,128)(2,1)} %get-tuple-element.307), channel_id=1, source_target_pairs={{0,4},{4,8},{8,12},{12,16},{16,20},{20,24},{24,28},{1,5},{5,9},{9,... | collective-permute-start | bytes 3047432 | tf_op jit(solution)/shard_map/ppermute | solution.py:894
  256.0 43.2 %collective-permute-start.19 = (bf16[992,512]{1,0:T(8,128)(2,1)}, bf16[992,512]{1,0:T(8,128)(2,1)}, u32[]{:S(2)}, u32[]{:S(2)}) collective-permute-start(bf16[992,512]{1,0:T(8,128)(2,1)} %get-tuple-element.306), channel_id=1, source_target_pairs={{4,0},{8,4},{12,8},{16,12},{20,16},{24,20},{28,24},{5,1},{9,5},{13... | collective-permute-start | bytes 3047432 | tf_op jit(solution)/shard_map/ppermute | solution.py:894
  257.7 2.4 collective-permute-start.20
  257.8 3.4 collective-permute-start.22
  258.3 40.9 %copy-start.10 = (bf16[1600,256]{1,0:T(8,128)(2,1)S(1)}, bf16[1600,256]{1,0:T(8,128)(2,1)}, u32[]{:S(2)}) copy-start(bf16[1600,256]{1,0:T(8,128)(2,1)} %get-tuple-element.176.refs_0_) | copy-start | bytes 2457604
  300.8 58.9 %collective-permute-start.23 = (bf16[1536,256]{1,0:T(8,128)(2,1)S(1)}, bf16[1536,256]{1,0:T(8,128)(2,1)S(1)}, u32[]{:S(2)}, u32[]{:S(2)}) collective-permute-start(bf16[1536,256]{1,0:T(8,128)(2,1)S(1)} %pad_maximum_fusion.2), channel_id=1, source_target_pairs={{0,4},{4,0},{8,12},{12,8},{16,20},{20,16},{24,28},{28,24},{1,5},{5... | collective-permute-start | bytes 2359304 | tf_op jit(solution)/shard_map/ppermute | solution.py:898
  303.4 56.4 %collective-permute-start.24 = (bf16[1536,256]{1,0:T(8,128)(2,1)S(1)}, bf16[1536,256]{1,0:T(8,128)(2,1)}, u32[]{:S(2)}, u32[]{:S(2)}) collective-permute-start(bf16[1536,256]{1,0:T(8,128)(2,1)S(1)} %pad_maximum_fusion.3), channel_id=1, source_target_pairs={{0,4},{4,0},{8,12},{12,8},{16,20},{20,16},{24,28},{28,24},{1,5},{5... | collective-permute-start | bytes 2359304 | tf_op jit(solution)/shard_map/ppermute | solution.py:898
  363.2 4.0 collective-permute-start.28
  366.8 11.7 %collective-permute-start.27 = (bf16[1536,256]{1,0:T(8,128)(2,1)}, bf16[1536,256]{1,0:T(8,128)(2,1)S(1)}, u32[]{:S(2)}, u32[]{:S(2)}) collective-permute-start(bf16[1536,256]{1,0:T(8,128)(2,1)} %bitcast.196), channel_id=1, source_target_pairs={{0,1},{1,0},{2,3},{3,2},{4,5},{5,4},{6,7},{7,6},{8,9},{9,8},{10,11... | collective-permute-start | bytes 2359304 | tf_op jit(solution)/shard_map/ppermute | solution.py:910
  367.4 19.6 %collective-permute-start.29 = (bf16[1536,256]{1,0:T(8,128)(2,1)S(1)}, bf16[1536,256]{1,0:T(8,128)(2,1)S(1)}, u32[]{:S(2)}, u32[]{:S(2)}) collective-permute-start(bf16[1536,256]{1,0:T(8,128)(2,1)S(1)} %fusion.3), channel_id=1, source_target_pairs={{0,2},{1,3},{2,0},{3,1},{4,6},{5,7},{6,4},{7,5},{8,10},{9,11},{10,... | collective-permute-start | bytes 2359304 | tf_op jit(solution)/shard_map/ppermute | solution.py:915
  368.3 46.4 %collective-permute-start.25 = (bf16[992,512]{1,0:T(8,128)(2,1)}, bf16[992,512]{1,0:T(8,128)(2,1)}, u32[]{:S(2)}, u32[]{:S(2)}) collective-permute-start(bf16[992,512]{1,0:T(8,128)(2,1)} %get-tuple-element.192), channel_id=1, source_target_pairs={{0,4},{4,8},{8,12},{12,16},{16,20},{20,24},{24,28},{1,5},{5,9},{9,... | collective-permute-start | bytes 3047432 | tf_op jit(solution)/shard_map/ppermute | solution.py:894
  371.7 43.0 %collective-permute-start.26 = (bf16[992,512]{1,0:T(8,128)(2,1)}, bf16[992,512]{1,0:T(8,128)(2,1)}, u32[]{:S(2)}, u32[]{:S(2)}) collective-permute-start(bf16[992,512]{1,0:T(8,128)(2,1)} %get-tuple-element.193), channel_id=1, source_target_pairs={{4,0},{8,4},{12,8},{16,12},{20,16},{24,20},{28,24},{5,1},{9,5},{13... | collective-permute-start | bytes 3047432 | tf_op jit(solution)/shard_map/ppermute | solution.py:894
  423.2 2.5 collective-permute-start.30
  431.8 12.2 %collective-permute-start.31 = (bf16[1536,256]{1,0:T(8,128)(2,1)}, bf16[1536,256]{1,0:T(8,128)(2,1)S(1)}, u32[]{:S(2)}, u32[]{:S(2)}) collective-permute-start(bf16[1536,256]{1,0:T(8,128)(2,1)} %bitcast.198), channel_id=1, source_target_pairs={{0,1},{1,0},{2,3},{3,2},{4,5},{5,4},{6,7},{7,6},{8,9},{9,8},{10,11... | collective-permute-start | bytes 2359304 | tf_op jit(solution)/shard_map/ppermute | solution.py:910
  432.0 19.8 %collective-permute-start.32 = (bf16[1536,256]{1,0:T(8,128)(2,1)S(1)}, bf16[1536,256]{1,0:T(8,128)(2,1)S(1)}, u32[]{:S(2)}, u32[]{:S(2)}) collective-permute-start(bf16[1536,256]{1,0:T(8,128)(2,1)S(1)} %fusion.2), channel_id=1, source_target_pairs={{0,2},{1,3},{2,0},{3,1},{4,6},{5,7},{6,4},{7,5},{8,10},{9,11},{10,... | collective-permute-start | bytes 2359304 | tf_op jit(solution)/shard_map/ppermute | solution.py:915
  451.8 159.5 %reduce-scatter.6.cloned.1.call-start = ((), (), s32[]{:S(2)}) async-start(), calls=%async_computation.7 | async-start | bytes 2949120 | tf_op jit(solution)/shard_map/reduce_scatter | solution.py:929
  457.2 30.4 %collective-permute-start.33 = (f32[40,256]{1,0:T(8,128)}, f32[40,256]{1,0:T(8,128)S(1)}, u32[]{:S(2)}, u32[]{:S(2)}) collective-permute-start(f32[40,256]{1,0:T(8,128)} %get-tuple-element.220), channel_id=1, source_target_pairs={{0,4},{4,8},{8,12},{12,16},{16,20},{20,24},{24,28},{1,5},{5,9},{9,... | collective-permute-start | bytes 122888 | tf_op jit(solution)/shard_map/ppermute | solution.py:894
  461.5 26.1 %collective-permute-start.34 = (f32[40,256]{1,0:T(8,128)}, f32[40,256]{1,0:T(8,128)S(1)}, u32[]{:S(2)}, u32[]{:S(2)}) collective-permute-start(f32[40,256]{1,0:T(8,128)} %get-tuple-element.221), channel_id=1, source_target_pairs={{4,0},{8,4},{12,8},{16,12},{20,16},{24,20},{28,24},{5,1},{9,5},{13... | collective-permute-start | bytes 122888 | tf_op jit(solution)/shard_map/ppermute | solution.py:894
  463.6 19.0 %collective-permute-start.35 = (bf16[32,256]{1,0:T(8,128)(2,1)S(1)}, bf16[32,256]{1,0:T(8,128)(2,1)S(1)}, u32[]{:S(2)}, u32[]{:S(2)}) collective-permute-start(bf16[32,256]{1,0:T(8,128)(2,1)S(1)} %get-tuple-element.311), channel_id=1, source_target_pairs={{0,4},{4,8},{8,12},{12,16},{16,20},{20,24},{24,28},{1,5},{5,9},{9,... | collective-permute-start | bytes 49160 | tf_op jit(solution)/shard_map/ppermute | solution.py:894
  481.1 6.5 collective-permute-start.36
  499.4 9.4 %collective-permute-start.37 = (bf16[1536,256]{1,0:T(8,128)(2,1)}, bf16[1536,256]{1,0:T(8,128)(2,1)S(1)}, u32[]{:S(2)}, u32[]{:S(2)}) collective-permute-start(bf16[1536,256]{1,0:T(8,128)(2,1)} %bitcast.193), channel_id=1, source_target_pairs={{0,1},{1,0},{2,3},{3,2},{4,5},{5,4},{6,7},{7,6},{8,9},{9,8},{10,11... | collective-permute-start | bytes 2359304 | tf_op jit(solution)/shard_map/ppermute | solution.py:910
  500.8 29.2 %collective-permute-start.40 = (bf16[1536,256]{1,0:T(8,128)(2,1)}, bf16[1536,256]{1,0:T(8,128)(2,1)S(1)}, u32[]{:S(2)}, u32[]{:S(2)}) collective-permute-start(bf16[1536,256]{1,0:T(8,128)(2,1)} %collective-permute-done.24.refs_0_), channel_id=1, source_target_pairs={{0,1},{1,0},{2,3},{3,2},{4,5},{5,4},{6,7},{7,6},{8,9},{9,8},{10,11... | collective-permute-start | bytes 2359304 | tf_op jit(solution)/shard_map/ppermute | solution.py:910
  501.3 29.3 %collective-permute-start.41 = (bf16[1600,256]{1,0:T(8,128)(2,1)}, bf16[1600,256]{1,0:T(8,128)(2,1)S(1)}, u32[]{:S(2)}, u32[]{:S(2)}) collective-permute-start(bf16[1600,256]{1,0:T(8,128)(2,1)} %get-tuple-element.232), channel_id=1, source_target_pairs={{0,4},{4,0},{8,12},{12,8},{16,20},{20,16},{24,28},{28,24},{1,5},{5... | collective-permute-start | bytes 2457608 | tf_op jit(solution)/shard_map/ppermute | solution.py:898
  519.4 22.3 %collective-permute-start.38 = (bf16[1536,256]{1,0:T(8,128)(2,1)}, bf16[1536,256]{1,0:T(8,128)(2,1)S(1)}, u32[]{:S(2)}, u32[]{:S(2)}) collective-permute-start(bf16[1536,256]{1,0:T(8,128)(2,1)} %bitcast.194), channel_id=1, source_target_pairs={{0,1},{1,0},{2,3},{3,2},{4,5},{5,4},{6,7},{7,6},{8,9},{9,8},{10,11... | collective-permute-start | bytes 2359304 | tf_op jit(solution)/shard_map/ppermute | solution.py:910
  519.4 22.3 %collective-permute-start.39 = (bf16[1536,256]{1,0:T(8,128)(2,1)S(1)}, bf16[1536,256]{1,0:T(8,128)(2,1)S(1)}, u32[]{:S(2)}, u32[]{:S(2)}) collective-permute-start(bf16[1536,256]{1,0:T(8,128)(2,1)S(1)} %fusion.1), channel_id=1, source_target_pairs={{0,2},{1,3},{2,0},{3,1},{4,6},{5,7},{6,4},{7,5},{8,10},{9,11},{10,... | collective-permute-start | bytes 2359304 | tf_op jit(solution)/shard_map/ppermute | solution.py:915
  542.2 133.1 %reduce-scatter.8.cloned.1.call-start = ((), (), s32[]{:S(2)}) async-start(), calls=%async_computation.8 | async-start | bytes 2949120 | tf_op jit(solution)/shard_map/reduce_scatter | solution.py:929
  548.2 6.2 collective-permute-start.42
  552.4 8.5 %collective-permute-start.43 = (f32[40,256]{1,0:T(8,128)}, f32[40,256]{1,0:T(8,128)S(1)}, u32[]{:S(2)}, u32[]{:S(2)}) collective-permute-start(f32[40,256]{1,0:T(8,128)} %get-tuple-element.243), channel_id=1, source_target_pairs={{4,0},{8,4},{12,8},{16,12},{20,16},{24,20},{28,24},{5,1},{9,5},{13... | collective-permute-start | bytes 122888 | tf_op jit(solution)/shard_map/ppermute | solution.py:894
  572.4 5.6 collective-permute-start.44
  572.4 26.9 %collective-permute-start.47 = (bf16[1536,256]{1,0:T(8,128)(2,1)S(1)}, bf16[1536,256]{1,0:T(8,128)(2,1)S(1)}, u32[]{:S(2)}, u32[]{:S(2)}) collective-permute-start(bf16[1536,256]{1,0:T(8,128)(2,1)S(1)} %copy-done.69), channel_id=1, source_target_pairs={{0,1},{1,0},{2,3},{3,2},{4,5},{5,4},{6,7},{7,6},{8,9},{9,8},{10,11... | collective-permute-start | bytes 2359304 | tf_op jit(solution)/shard_map/ppermute | solution.py:910
  572.9 26.4 %collective-permute-start.48 = (bf16[1600,256]{1,0:T(8,128)(2,1)}, bf16[1600,256]{1,0:T(8,128)(2,1)S(1)}, u32[]{:S(2)}, u32[]{:S(2)}) collective-permute-start(bf16[1600,256]{1,0:T(8,128)(2,1)} %get-tuple-element.254), channel_id=1, source_target_pairs={{0,4},{4,0},{8,12},{12,8},{16,20},{20,16},{24,28},{28,24},{1,5},{5... | collective-permute-start | bytes 2457608 | tf_op jit(solution)/shard_map/ppermute | solution.py:898
  588.6 22.7 %collective-permute-start.45 = (bf16[1536,256]{1,0:T(8,128)(2,1)}, bf16[1536,256]{1,0:T(8,128)(2,1)S(1)}, u32[]{:S(2)}, u32[]{:S(2)}) collective-permute-start(bf16[1536,256]{1,0:T(8,128)(2,1)} %bitcast.195), channel_id=1, source_target_pairs={{0,1},{1,0},{2,3},{3,2},{4,5},{5,4},{6,7},{7,6},{8,9},{9,8},{10,11... | collective-permute-start | bytes 2359304 | tf_op jit(solution)/shard_map/ppermute | solution.py:910
  588.6 22.7 %collective-permute-start.46 = (bf16[1536,256]{1,0:T(8,128)(2,1)S(1)}, bf16[1536,256]{1,0:T(8,128)(2,1)S(1)}, u32[]{:S(2)}, u32[]{:S(2)}) collective-permute-start(bf16[1536,256]{1,0:T(8,128)(2,1)S(1)} %fusion), channel_id=1, source_target_pairs={{0,2},{1,3},{2,0},{3,1},{4,6},{5,7},{6,4},{7,5},{8,10},{9,11},{10,... | collective-permute-start | bytes 2359304 | tf_op jit(solution)/shard_map/ppermute | solution.py:915
  620.0 6.8 collective-permute-start.49
  624.8 6.1 collective-permute-start.50
  636.0 8.7 %collective-permute-start.51 = (f32[168,256]{1,0:T(8,128)S(1)}, f32[168,256]{1,0:T(8,128)S(1)}, u32[]{:S(2)}, u32[]{:S(2)}) collective-permute-start(f32[168,256]{1,0:T(8,128)S(1)} %concatenate.39), channel_id=1, source_target_pairs={{0,4},{4,0},{8,12},{12,8},{16,20},{20,16},{24,28},{28,24},{1,5},{5... | collective-permute-start | bytes 516104 | tf_op jit(solution)/shard_map/ppermute | solution.py:898
  644.7 15.4 %collective-permute-start.52 = (f32[168,256]{1,0:T(8,128)S(1)}, f32[168,256]{1,0:T(8,128)S(1)}, u32[]{:S(2)}, u32[]{:S(2)}) collective-permute-start(f32[168,256]{1,0:T(8,128)S(1)} %add.214), channel_id=1, source_target_pairs={{0,8},{4,12},{8,0},{12,4},{16,24},{20,28},{24,16},{28,20},{1,9},{5... | collective-permute-start | bytes 516104 | tf_op jit(solution)/shard_map/ppermute | solution.py:898
  660.1 10.2 %collective-permute-start.53 = (f32[168,256]{1,0:T(8,128)S(1)}, f32[168,256]{1,0:T(8,128)S(1)}, u32[]{:S(2)}, u32[]{:S(2)}) collective-permute-start(f32[168,256]{1,0:T(8,128)S(1)} %add.215), channel_id=1, source_target_pairs={{0,16},{4,20},{8,24},{12,28},{16,0},{20,4},{24,8},{28,12},{1,17},{... | collective-permute-start | bytes 516104 | tf_op jit(solution)/shard_map/ppermute | solution.py:898
  (70 other events, 541.9 us)
Sparse Core Ops, SparseCore 0:
  10.9 93.8 all-gather.3
  107.6 78.8 all-gather.5
  189.2 47.6 all-gather.7
  451.9 90.1 reduce-scatter.3
  544.9 48.6 reduce-scatter.5
  612.3 52.8 reduce-scatter.7
